TPU v7x, 128 devices: a whole 4x4x4 slice. The times are simulated.
128 devices in a mesh: ctx: 8 (over z, core), ep: 16 (over y, x).
Axes of the slice: x: 4, y: 4, z: 4, core: 2. Of those that a mesh axis runs over, the one named last changes fastest.
Arguments:
- query: bfloat16 [16, 1024, 4096], P('ep', 'ctx'), may hold values from -120 to 120
- keyval: bfloat16 [16, 1024, 512], P('ep', 'ctx'), may hold values from -4 to 4
- doc_lengths: int32 [16, 4], P('ep'), may hold values from 1 to 512, 1024 in all within a row
- norm_gain: float32 [4096], replicated, may hold values from 0.5 to 1.5
- router_logits: float32 [16, 1024, 3], P('ep', 'ctx'), may hold values from -10 to 310
- expert_ids: int32 [16, 1024, 3], P('ep', 'ctx'), may hold values from 0 to 127, all different within a row; in each aligned block of 128 rows (0 to 127, 128 to 255, ..., all dimensions but the last counted through in order) at most 4 rows name the same one
- grad_out: bfloat16 [16, 1024, 4096], P('ep', 'ctx'), may hold values from -6 to 6
- base_in: bfloat16 [128, 2, 4096, 768], P(('ctx', 'ep')), may hold values from -0.09375 to 0.09375
- low_in: bfloat16 [128, 2, 4096, 32], P(('ctx', 'ep')), may hold values from -0.09375 to 0.09375
- high_in: bfloat16 [128, 2, 32, 768], P(('ctx', 'ep')), may hold values from -1 to 1
- mag_in: float32 [128, 2, 768], P(('ctx', 'ep')), may hold values from 0.5 to 1.5
- base_out: bfloat16 [128, 768, 4096], P(('ctx', 'ep')), may hold values from -0.21875 to 0.21875
- low_out: bfloat16 [128, 768, 32], P(('ctx', 'ep')), may hold values from -0.21875 to 0.21875
- high_out: bfloat16 [128, 32, 4096], P(('ctx', 'ep')), may hold values from -1 to 1
- mag_out: float32 [128, 4096], P(('ctx', 'ep')), may hold values from 0.5 to 1.5
Outputs:
- grad_query: bfloat16 [16, 1024, 4096], P('ep', 'ctx')
- grad_keyval: bfloat16 [16, 1024, 512], P('ep', 'ctx')
- grad_logits: float32 [16, 1024, 3], P('ep', 'ctx')
- grad_low_in: float32 [128, 2, 4096, 32], P(('ctx', 'ep'))
- grad_high_in: float32 [128, 2, 32, 768], P(('ctx', 'ep'))
- grad_mag_in: float32 [128, 2, 768], P(('ctx', 'ep'))
- grad_low_out: float32 [128, 768, 32], P(('ctx', 'ep'))
- grad_high_out: float32 [128, 32, 4096], P(('ctx', 'ep'))
- grad_mag_out: float32 [128, 4096], P(('ctx', 'ep'))
Inputs may be any that keep to these rules, and one draw needn't show every extreme that they name: `expert_ids`: each row names 3 different experts; within the rows of one device no expert is named more than 4 times, and in some device's rows one expert is named exactly 4 times. `doc_lengths`: each group's lengths sum to 1024; the longest is 512.
All inputs are finite; a program needn't handle non-finite values.
Results may differ from a plain program's by a relative error of at most 0.04.
Values may be sent and summed in bfloat16 or wider, within the bound.
A program may use at most 192 MiB of HBM per device.

v0:
```python
import functools

import jax
import jax.numpy as jnp
from jax import lax
from jax.experimental import pallas as pl
from jax.experimental.pallas import tpu as pltpu
from jax.sharding import PartitionSpec as P

F32 = jnp.float32
BF16 = jnp.bfloat16
MESH = pl.DeviceIdType.MESH
HEAD = 128
NEGATIVE = -1e30
EPSILON = 1e-06
CAP = 4
BLOCK = 16
GROUP = 256
PER_GROUP = GROUP // BLOCK
REACH = 4
MB = 1 << 20


def params(megabytes):
    return pltpu.CompilerParams(vmem_limit_bytes=megabytes * MB)


def cost(flops, size, transcendentals=0):
    return pl.CostEstimate(flops=flops, bytes_accessed=size, transcendentals=transcendentals)


def iota(shape, dim):
    return lax.broadcasted_iota(jnp.int32, shape, dim)


def dot(left, right):
    return jnp.dot(left, right, preferred_element_type=F32)


def contract(left, right, left_dim, right_dim):
    return lax.dot_general(
        left, right, (((left_dim,), (right_dim,)), ((), ())), preferred_element_type=F32
    )


def is_row(row, col, slots, halves):
    pieces = BLOCK // (slots * halves)
    span = PER_GROUP * slots * halves
    return (
        (row // span == (col // (slots * halves)) % pieces)
        & ((row // (PER_GROUP * slots)) % halves == (col // slots) % halves)
        & ((row // slots) % PER_GROUP == col // BLOCK)
        & (row % slots == col % slots)
    )


def to_rows(slots, halves):
    same = is_row(iota((GROUP, GROUP), 0), iota((GROUP, GROUP), 1), slots, halves)
    return same.astype(F32).astype(BF16)


def to_blocks(slots, halves):
    same = is_row(iota((GROUP, GROUP), 1), iota((GROUP, GROUP), 0), slots, halves)
    return same.astype(F32).astype(BF16)


def dispatch_kernel(with_norm, slots_ref, rows_ref, gain_ref, *rest):
    outs, rinv_ref, stack = rest[:-2], rest[-2], rest[-1]
    tokens, width = rows_ref.shape
    slots = CAP // len(outs)
    pieces = BLOCK // slots
    piece = width // pieces

    @pl.when(pl.program_id(0) == 0)
    def _():
        if with_norm:
            square = jnp.zeros((tokens, 1), F32)
            for p in range(pieces):
                part = rows_ref[:, p * piece : (p + 1) * piece].astype(F32)
                square = square + jnp.sum(part * part, axis=1, keepdims=True)
            rinv = lax.rsqrt(square / width + EPSILON)
        else:
            rinv = jnp.ones((tokens, 1), F32)
        rinv_ref[...] = rinv
        for p in range(pieces):
            cols = slice(p * piece, (p + 1) * piece)
            part = rows_ref[:, cols]
            if with_norm:
                part = (part.astype(F32) * rinv * gain_ref[:, cols]).astype(BF16)
            stack[p * tokens : (p + 1) * tokens, :] = part

    spread = (iota((GROUP, PER_GROUP), 0) // BLOCK == iota((GROUP, PER_GROUP), 1)).astype(F32)
    slot = dot(spread.astype(BF16), slots_ref[...].astype(BF16))
    row = iota((GROUP, tokens), 0)
    for half, out_ref in enumerate(outs):
        hit = slot == (half * slots + row % slots).astype(F32)
        parts = []
        for p in range(pieces):
            own = hit & ((row // slots) % pieces == p)
            parts.append(jnp.where(own, 1.0, 0.0).astype(BF16))
        out_ref[...] = dot(jnp.concatenate(parts, axis=1), stack[...]).astype(BF16)


def dispatch(slots, rows, gain, with_norm, halves):
    experts, tokens = slots.shape
    width = rows.shape[1]
    total = experts * BLOCK
    pieces = BLOCK * halves // CAP
    piece = width // pieces
    whole = lambda shape: pl.BlockSpec(shape, lambda i: (0, 0))
    return pl.pallas_call(
        functools.partial(dispatch_kernel, with_norm),
        grid=(total // GROUP,),
        in_specs=[
            pl.BlockSpec((PER_GROUP, tokens), lambda i: (i, 0)),
            whole((tokens, width)),
            whole((1, width)),
        ],
        out_specs=[pl.BlockSpec((GROUP, piece), lambda i: (i, 0))] * halves + [whole((tokens, 1))],
        out_shape=[jax.ShapeDtypeStruct((total, piece), BF16)] * halves
        + [jax.ShapeDtypeStruct((tokens, 1), F32)],
        scratch_shapes=[pltpu.VMEM((pieces * tokens, piece), BF16)],
        compiler_params=params(60),
        cost_estimate=cost(2 * total * tokens * width * halves, 10 * MB),
        name="dispatch",
    )(slots, rows, gain)


def unpack_kernel(halves, blocks_ref, out_ref):
    piece = blocks_ref.shape[1]
    slots = CAP // halves
    pieces = BLOCK // CAP
    rows = dot(to_rows(slots, halves), blocks_ref[...]).astype(BF16)
    count = PER_GROUP * slots
    for p in range(pieces):
        for half in range(halves):
            first = (p * halves + half) * count
            out_ref[half, :, p * piece : (p + 1) * piece] = rows[first : first + count, :]


def unpack(blocks, halves):
    total, piece = blocks.shape
    pieces = BLOCK // CAP
    count = total // pieces // halves
    return pl.pallas_call(
        functools.partial(unpack_kernel, halves),
        grid=(total // GROUP,),
        in_specs=[pl.BlockSpec((GROUP, piece), lambda i: (i, 0))],
        out_specs=pl.BlockSpec(
            (halves, GROUP // pieces // halves, pieces * piece), lambda i: (0, i, 0)
        ),
        out_shape=jax.ShapeDtypeStruct((halves, count, pieces * piece), BF16),
        compiler_params=params(60),
        cost_estimate=cost(2 * total * GROUP * piece, 8 * MB),
        name="unpack",
    )(blocks)


def neighbours(position, count):
    near = []
    for j in range(1, REACH + 1):
        near.append((position + j < count, j))
        near.append((position >= j, -j))
    return near


def greet(position, count):
    barrier = pltpu.get_barrier_semaphore()
    for present, j in neighbours(position, count):

        @pl.when(present)
        def _():
            pl.semaphore_signal(
                barrier, inc=1, device_id={"ctx": position + j}, device_id_type=MESH
            )

    peers = jnp.minimum(position, REACH) + jnp.minimum(count - 1 - position, REACH)
    pl.semaphore_wait(barrier, peers)


def gather_kernel(count, own_ref, seen_ref, send_sem, recv_sem, own_sem):
    tokens = own_ref.shape[0]
    me = lax.axis_index("ctx")

    def copy(j):
        return pltpu.make_async_remote_copy(
            src_ref=own_ref,
            dst_ref=seen_ref.at[pl.ds((REACH - j) * tokens, tokens)],
            send_sem=send_sem.at[j - 1],
            recv_sem=recv_sem.at[j - 1],
            device_id={"ctx": me + j},
            device_id_type=MESH,
        )

    keep = pltpu.make_async_copy(own_ref, seen_ref.at[pl.ds(REACH * tokens, tokens)], own_sem)
    keep.start()
    greet(me, count)
    for j in range(REACH, 0, -1):

        @pl.when(me + j < count)
        def _():
            copy(j).start()

    for j in range(1, REACH + 1):

        @pl.when(me < j)
        def _():
            seen_ref[(REACH - j) * tokens : (REACH - j + 1) * tokens, :] = jnp.zeros(
                own_ref.shape, own_ref.dtype
            )

    keep.wait()
    for j in range(1, REACH + 1):

        @pl.when(me >= j)
        def _():
            copy(j).wait_recv()

        @pl.when(me + j < count)
        def _():
            copy(j).wait_send()


def gather(own, count):
    tokens, width = own.shape
    vmem = pl.BlockSpec(memory_space=pltpu.VMEM)
    return pl.pallas_call(
        functools.partial(gather_kernel, count),
        in_specs=[vmem],
        out_specs=vmem,
        out_shape=jax.ShapeDtypeStruct(((REACH + 1) * tokens, width), own.dtype),
        scratch_shapes=[
            pltpu.SemaphoreType.DMA((REACH,)),
            pltpu.SemaphoreType.DMA((REACH,)),
            pltpu.SemaphoreType.DMA,
        ],
        compiler_params=pltpu.CompilerParams(
            collective_id=0, has_side_effects=True, vmem_limit_bytes=60 * MB
        ),
        name="gather",
    )(own)


def scatter_kernel(count, kv_heads, *rest):
    terms, (out_ref, landed, send_sem, recv_sem) = rest[:kv_heads], rest[kv_heads:]
    tokens = out_ref.shape[0]
    half = out_ref.shape[1] // 2
    me = lax.axis_index("ctx")

    def copy(j, m):
        return pltpu.make_async_remote_copy(
            src_ref=terms[m].at[pl.ds((REACH - j) * tokens, tokens)],
            dst_ref=landed.at[j - 1, m],
            send_sem=send_sem.at[j - 1, m],
            recv_sem=recv_sem.at[j - 1, m],
            device_id={"ctx": me - j},
            device_id_type=MESH,
        )

    greet(me, count)
    for j in range(REACH, 0, -1):

        @pl.when(me >= j)
        def _():
            for m in range(kv_heads):
                copy(j, m).start()

    for j in range(1, REACH + 1):

        @pl.when(me + j < count)
        def _():
            for m in range(kv_heads):
                copy(j, m).wait_recv()

        @pl.when(me + j >= count)
        def _():
            landed[j - 1] = jnp.zeros(landed.shape[1:], landed.dtype)

        @pl.when(me >= j)
        def _():
            for m in range(kv_heads):
                copy(j, m).wait_send()

    for m in range(kv_heads):
        total = terms[m][REACH * tokens :, :].astype(F32)
        for j in range(REACH):
            total = total + landed[j, m].astype(F32)
        out_ref[:, m * HEAD : (m + 1) * HEAD] = total[:, :HEAD].astype(BF16)
        out_ref[:, half + m * HEAD : half + (m + 1) * HEAD] = total[:, HEAD:].astype(BF16)


def scatter(terms, tokens, count):
    kv_heads = len(terms)
    width = terms[0].shape[1]
    vmem = pl.BlockSpec(memory_space=pltpu.VMEM)
    return pl.pallas_call(
        functools.partial(scatter_kernel, count, kv_heads),
        in_specs=[vmem] * kv_heads,
        out_specs=vmem,
        out_shape=jax.ShapeDtypeStruct((tokens, kv_heads * width), BF16),
        scratch_shapes=[
            pltpu.VMEM((REACH, kv_heads, tokens, width), BF16),
            pltpu.SemaphoreType.DMA((REACH, kv_heads)),
            pltpu.SemaphoreType.DMA((REACH, kv_heads)),
        ],
        compiler_params=pltpu.CompilerParams(
            collective_id=1, has_side_effects=True, vmem_limit_bytes=60 * MB
        ),
        name="scatter",
    )(*terms)


def visible(place_ref, window, tokens):
    kpos = place_ref[0] + iota((window, tokens), 0)
    qpos = place_ref[1] + iota((window, tokens), 1)
    kdoc = jnp.zeros((window, tokens), jnp.int32)
    qdoc = jnp.zeros((window, tokens), jnp.int32)
    for d in range(4):
        end = place_ref[2 + d]
        kdoc = kdoc + (kpos >= end).astype(jnp.int32)
        qdoc = qdoc + (qpos >= end).astype(jnp.int32)
    return (kpos >= 0) & (kpos <= qpos) & (kdoc == qdoc)


def head_pair(ref, h):
    return jnp.concatenate(
        [ref[:, h * HEAD : (h + 1) * HEAD], ref[:, (h + 1) * HEAD : (h + 2) * HEAD]], axis=0
    )


def attend_kernel(heads, per_kv, place_ref, query_ref, keyval_ref, prob_ref, out_ref, bias):
    tokens = query_ref.shape[0]
    window = keyval_ref.shape[0]
    step = pl.program_id(0)
    half = keyval_ref.shape[1] // 2
    scale = HEAD ** (-0.5)

    @pl.when(step == 0)
    def _():
        hidden = jnp.where(visible(place_ref, window, tokens), 0.0, NEGATIVE)
        bias[:, :tokens] = hidden
        bias[:, tokens:] = hidden

    for m in range(half // HEAD):

        @pl.when(step // (per_kv // heads) == m)
        def _():
            keys = keyval_ref[:, m * HEAD : (m + 1) * HEAD]
            values_t = keyval_ref[:, half + m * HEAD : half + (m + 1) * HEAD].T
            for h in range(0, heads, 2):
                raw = contract(keys, head_pair(query_ref, h), 1, 1) * scale + bias[...]
                peak = jnp.max(raw, axis=0, keepdims=True)
                expo = jnp.exp(raw - peak)
                total = jnp.sum(expo, axis=0, keepdims=True)
                prob = (expo * (1.0 / total)).astype(BF16)
                prob_ref[0, :, h * tokens : (h + 2) * tokens] = prob
                mixed = dot(values_t, prob).T.astype(BF16)
                out_ref[:, h * HEAD : (h + 1) * HEAD] = mixed[:tokens]
                out_ref[:, (h + 1) * HEAD : (h + 2) * HEAD] = mixed[tokens:]


def attend(place, query, keyval):
    tokens, width = query.shape
    window = keyval.shape[0]
    kv_heads = keyval.shape[1] // 2 // HEAD
    per_kv = width // HEAD // kv_heads
    heads = 4
    steps = width // HEAD // heads
    return pl.pallas_call(
        functools.partial(attend_kernel, heads, per_kv),
        grid=(steps,),
        in_specs=[
            pl.BlockSpec(memory_space=pltpu.SMEM),
            pl.BlockSpec((tokens, heads * HEAD), lambda i: (0, i)),
            pl.BlockSpec(keyval.shape, lambda i: (0, 0)),
        ],
        out_specs=[
            pl.BlockSpec((1, window, heads * tokens), lambda i: (i, 0, 0)),
            pl.BlockSpec((tokens, heads * HEAD), lambda i: (0, i)),
        ],
        out_shape=[
            jax.ShapeDtypeStruct((steps, window, heads * tokens), BF16),
            jax.ShapeDtypeStruct((tokens, width), BF16),
        ],
        scratch_shapes=[pltpu.VMEM((window, 2 * tokens), F32)],
        compiler_params=params(60),
        cost_estimate=cost(4 * tokens * width * window, 9 * MB, tokens * width * window // HEAD),
        name="attend",
    )(place, query, keyval)


def attend_back_kernel(
    heads, query_ref, grad_ref, prob_ref, keys_ref, values_ref,
    grad_query_ref, grad_keyval_ref, key_sum, value_sum,
):
    step = pl.program_id(0)
    tokens = query_ref.shape[0]
    scale = HEAD ** (-0.5)

    @pl.when(step == 0)
    def _():
        key_sum[...] = jnp.zeros_like(key_sum)
        value_sum[...] = jnp.zeros_like(value_sum)

    keys_t = keys_ref[...].T
    values = values_ref[...]
    for h in range(0, heads, 2):
        grad = head_pair(grad_ref, h)
        prob = prob_ref[0, :, h * tokens : (h + 2) * tokens]
        wide = prob.astype(F32)
        moved = wide * contract(values, grad, 1, 1)
        delta = jnp.sum(moved, axis=0, keepdims=True)
        dscore = (moved - wide * delta).astype(BF16)
        grad_query = (dot(keys_t, dscore) * scale).T.astype(BF16)
        grad_query_ref[:, h * HEAD : (h + 1) * HEAD] = grad_query[:tokens]
        grad_query_ref[:, (h + 1) * HEAD : (h + 2) * HEAD] = grad_query[tokens:]
        key_sum[...] += dot(dscore, head_pair(query_ref, h))
        value_sum[...] += dot(prob, grad)

    @pl.when(step == pl.num_programs(0) - 1)
    def _():
        grad_keyval_ref[:, :HEAD] = (key_sum[...] * scale).astype(BF16)
        grad_keyval_ref[:, HEAD:] = value_sum[...].astype(BF16)


def attend_back(m, query, grad, prob, keyval):
    tokens, width = query.shape
    window = keyval.shape[0]
    kv_heads = keyval.shape[1] // 2 // HEAD
    heads = prob.shape[2] // tokens
    steps = prob.shape[0] // kv_heads
    rows = pl.BlockSpec((tokens, heads * HEAD), lambda i: (0, m * steps + i))
    return pl.pallas_call(
        functools.partial(attend_back_kernel, heads),
        grid=(steps,),
        in_specs=[
            rows,
            rows,
            pl.BlockSpec((1,) + prob.shape[1:], lambda i: (m * steps + i, 0, 0)),
            pl.BlockSpec((window, HEAD), lambda i: (0, m)),
            pl.BlockSpec((window, HEAD), lambda i: (0, kv_heads + m)),
        ],
        out_specs=[
            pl.BlockSpec((tokens, heads * HEAD), lambda i: (0, i)),
            pl.BlockSpec((window, 2 * HEAD), lambda i: (0, 0)),
        ],
        out_shape=[
            jax.ShapeDtypeStruct((tokens, width // kv_heads), BF16),
            jax.ShapeDtypeStruct((window, 2 * HEAD), BF16),
        ],
        scratch_shapes=[pltpu.VMEM((window, HEAD), F32), pltpu.VMEM((window, HEAD), F32)],
        compiler_params=params(60),
        cost_estimate=cost(4 * tokens * width * window, 5 * MB),
        name="attend_back",
    )(query, grad, prob, keyval, keyval)


def combine_terms(half, halves, tokens, slots_ref, gates_ref, blocks_ref):
    step = pl.program_id(0)
    count = blocks_ref.shape[0]
    experts = slots_ref.shape[1]
    slots = CAP // halves
    pieces = BLOCK // slots
    spread = (
        iota((experts, count), 0) == step * (count // BLOCK) + iota((experts, count), 1) // BLOCK
    ).astype(F32).astype(BF16)
    slot = dot(slots_ref[...].astype(BF16), spread)
    gate = dot(gates_ref[...].astype(BF16), spread)
    col = iota((tokens, count), 1)
    gate = jnp.where(slot == (half * slots + col % slots).astype(F32), gate, 0.0)
    parts = []
    for p in range(pieces):
        parts.append(jnp.where((col // slots) % pieces == p, gate, 0.0).astype(BF16))
    return dot(jnp.concatenate(parts, axis=0), blocks_ref[...])


def combine_first_kernel(halves, tokens, slots_ref, gates_ref, blocks_ref, acc_ref):
    part = combine_terms(0, halves, tokens, slots_ref, gates_ref, blocks_ref)

    @pl.when(pl.program_id(0) == 0)
    def _():
        acc_ref[...] = part

    @pl.when(pl.program_id(0) != 0)
    def _():
        acc_ref[...] += part


def combine_last_kernel(
    halves, slots_ref, gates_ref, blocks_ref, first_ref, gain_ref, grad_out_ref, hidden_ref,
    rinv_ref, grad_ref, acc,
):
    step = pl.program_id(0)
    tokens, width = hidden_ref.shape
    pieces = acc.shape[0] // tokens
    piece = width // pieces
    part = combine_terms(halves - 1, halves, tokens, slots_ref, gates_ref, blocks_ref)

    @pl.when(step == 0)
    def _():
        acc[...] = first_ref[...] + part

    @pl.when(step != 0)
    def _():
        acc[...] += part

    @pl.when(step == pl.num_programs(0) - 1)
    def _():
        rinv = rinv_ref[...]
        mean = jnp.zeros((tokens, 1), F32)
        for p in range(pieces):
            cols = slice(p * piece, (p + 1) * piece)
            rows = slice(p * tokens, (p + 1) * tokens)
            scaled = acc[rows, :] * gain_ref[:, cols]
            acc[rows, :] = scaled
            mean = mean + jnp.sum(hidden_ref[:, cols].astype(F32) * scaled, axis=1, keepdims=True)
        mean = mean / width * (rinv * rinv * rinv)
        for p in range(pieces):
            cols = slice(p * piece, (p + 1) * piece)
            rows = slice(p * tokens, (p + 1) * tokens)
            grad = (
                grad_out_ref[:, cols].astype(F32)
                + rinv * acc[rows, :]
                - hidden_ref[:, cols].astype(F32) * mean
            )
            grad_ref[:, cols] = grad.astype(BF16)


def combine_first(slots, gates, blocks, halves):
    tokens = slots.shape[0]
    total, piece = blocks.shape
    pieces = BLOCK * halves // CAP
    rows = 2 * GROUP
    whole = lambda shape: pl.BlockSpec(shape, lambda i: (0, 0))
    return pl.pallas_call(
        functools.partial(combine_first_kernel, halves, tokens),
        grid=(total // rows,),
        in_specs=[
            whole(slots.shape),
            whole(gates.shape),
            pl.BlockSpec((rows, piece), lambda i: (i, 0)),
        ],
        out_specs=whole((pieces * tokens, piece)),
        out_shape=jax.ShapeDtypeStruct((pieces * tokens, piece), F32),
        compiler_params=params(60),
        cost_estimate=cost(1, 1),
        name="combine_first",
    )(slots, gates, blocks)


def combine_last(slots, gates, blocks, first, gain, grad_out, hidden, rinv, halves):
    tokens, width = hidden.shape
    total, piece = blocks.shape
    rows = 2 * GROUP
    whole = lambda shape: pl.BlockSpec(shape, lambda i: (0, 0))
    return pl.pallas_call(
        functools.partial(combine_last_kernel, halves),
        grid=(total // rows,),
        in_specs=[
            whole(slots.shape),
            whole(gates.shape),
            pl.BlockSpec((rows, piece), lambda i: (i, 0)),
            whole(first.shape),
            whole(gain.shape),
            whole(grad_out.shape),
            whole(hidden.shape),
            whole(rinv.shape),
        ],
        out_specs=whole((tokens, width)),
        out_shape=jax.ShapeDtypeStruct((tokens, width), BF16),
        scratch_shapes=[pltpu.VMEM(first.shape, F32)],
        compiler_params=params(60),
        cost_estimate=cost(2 * total * tokens * width, 8 * MB),
        name="combine_last",
    )(slots, gates, blocks, first, gain, grad_out, hidden, rinv)


def expert_kernel(
    slots, blocks_hbm, base_hbm, low_ref, high_ref, scale_ref, grad_hidden_ref,
    out_hbm, inputs_hbm, units_ref, low_act_ref, grad_linear_ref, back_ref, products_ref, mag_ref,
    blocks, base, inputs, linear, out_rows, in_sem, base_sem, row_sem, out_sem,
):
    groups = blocks.shape[0] // GROUP
    piece = blocks.shape[1]
    pieces = BLOCK // slots
    span = PER_GROUP * slots
    ffw = base.shape[2]
    depth = base.shape[1]
    tile = 256
    tiles = ffw // tile
    rank = high_ref.shape[1]

    def load_blocks(g):
        rows = pl.ds(pl.multiple_of(g * GROUP, GROUP), GROUP)
        return pltpu.make_async_copy(blocks_hbm.at[rows], blocks.at[rows], in_sem.at[g])

    def load_base(n):
        cols = pl.ds(pl.multiple_of((n % tiles) * tile, tile), tile)
        j = n // tiles
        return pltpu.make_async_copy(
            base_hbm.at[j, :, cols], base.at[j, :, cols], base_sem.at[n]
        )

    def store_rows(g):
        rows = pl.ds(pl.multiple_of(g * GROUP, GROUP), GROUP)
        return pltpu.make_async_copy(out_rows.at[rows], out_hbm.at[rows], out_sem.at[g])

    for g in range(groups):
        load_blocks(g).start()
    for n in range(2 * tiles):
        load_base(n).start()

    permute = to_rows(slots, 1)

    def unpack_group(g, _):
        load_blocks(g).wait()
        rows = dot(permute, blocks[pl.ds(pl.multiple_of(g * GROUP, GROUP), GROUP), :]).astype(BF16)
        place = pl.ds(pl.multiple_of(g * span, span), span)
        for p in range(pieces):
            inputs[place, p * piece : (p + 1) * piece] = rows[p * span : (p + 1) * span, :]
        return 0

    lax.fori_loop(0, groups, unpack_group, 0)
    keep = pltpu.make_async_copy(inputs, inputs_hbm, row_sem)
    keep.start()

    low_act_ref[...] = dot(inputs[...], low_ref[...]).astype(BF16)

    def forward(n, _):
        load_base(n).wait()
        j = n // tiles
        cols = pl.ds(pl.multiple_of((n % tiles) * tile, tile), tile)
        linear[j, :, cols] = dot(inputs[...], base[j, :, cols])
        return 0

    lax.fori_loop(0, 2 * tiles, forward, 0)

    for n in range(tiles):
        cols = slice(n * tile, (n + 1) * tile)
        gate_linear = linear[0, :, cols] + dot(low_act_ref[:, :rank], high_ref[0, :, cols])
        up_linear = linear[1, :, cols] + dot(low_act_ref[:, rank:], high_ref[1, :, cols])
        gate_scale = scale_ref[0:1, cols]
        up_scale = scale_ref[1:2, cols]
        gate = gate_linear * gate_scale
        up = up_linear * up_scale
        sigmoid = 1.0 / (1.0 + jnp.exp(-gate))
        active = gate * sigmoid
        units = (active * up).astype(BF16)
        units_ref[:, cols] = units
        grad_hidden = grad_hidden_ref[:, cols]
        part = jnp.sum(units.astype(F32) * grad_hidden, axis=1, keepdims=True)
        if n == 0:
            products_ref[...] = part
        else:
            products_ref[...] += part
        grad_gate = grad_hidden * up * sigmoid * (1.0 + gate * (1.0 - sigmoid))
        grad_up = grad_hidden * active
        mag_ref[0:1, cols] = jnp.sum(grad_gate * gate_linear, axis=0, keepdims=True)
        mag_ref[1:2, cols] = jnp.sum(grad_up * up_linear, axis=0, keepdims=True)
        grad_linear_ref[0, :, cols] = (grad_gate * gate_scale).astype(BF16)
        grad_linear_ref[1, :, cols] = (grad_up * up_scale).astype(BF16)

    for j in range(2):
        back_ref[:, j * rank : (j + 1) * rank] = contract(
            grad_linear_ref[j], high_ref[j], 1, 1
        ).astype(BF16)

    keep.wait()

    def backward(n, _):
        rows = pl.ds(pl.multiple_of(n * tile, tile), tile)
        grad = contract(grad_linear_ref[0], base[0, rows, :], 1, 1)
        grad = grad + contract(grad_linear_ref[1], base[1, rows, :], 1, 1)
        grad = grad + contract(back_ref[...], low_ref[rows, :], 1, 1)
        inputs[:, rows] = grad.astype(BF16)
        return 0

    lax.fori_loop(0, depth // tile, backward, 0)

    arrange = to_blocks(slots, 1)

    def pack_group(g, _):
        place = pl.ds(pl.multiple_of(g * span, span), span)
        stack = jnp.concatenate(
            [inputs[place, p * piece : (p + 1) * piece] for p in range(pieces)], axis=0
        )
        rows = pl.ds(pl.multiple_of(g * GROUP, GROUP), GROUP)
        out_rows[rows, :] = dot(arrange, stack).astype(BF16)
        store_rows(g).start()
        return 0

    lax.fori_loop(0, groups, pack_group, 0)
    for g in range(groups):
        store_rows(g).wait()


def expert(slots, blocks, base, low, high, scale, grad_hidden):
    total, piece = blocks.shape
    branches, depth, ffw = base.shape
    count = total * slots // BLOCK
    rank2 = low.shape[1]
    groups = total // GROUP
    vmem = pl.BlockSpec(memory_space=pltpu.VMEM)
    hbm = pl.BlockSpec(memory_space=pl.ANY)
    return pl.pallas_call(
        functools.partial(expert_kernel, slots),
        in_specs=[hbm, hbm, vmem, vmem, vmem, vmem],
        out_specs=[hbm, hbm, vmem, vmem, vmem, vmem, vmem, vmem],
        out_shape=[
            jax.ShapeDtypeStruct((total, piece), BF16),
            jax.ShapeDtypeStruct((count, depth), BF16),
            jax.ShapeDtypeStruct((count, ffw), BF16),
            jax.ShapeDtypeStruct((count, rank2), BF16),
            jax.ShapeDtypeStruct((branches, count, ffw), BF16),
            jax.ShapeDtypeStruct((count, rank2), BF16),
            jax.ShapeDtypeStruct((count, 1), F32),
            jax.ShapeDtypeStruct((branches, ffw), F32),
        ],
        scratch_shapes=[
            pltpu.VMEM((total, piece), BF16),
            pltpu.VMEM(base.shape, BF16),
            pltpu.VMEM((count, depth), BF16),
            pltpu.VMEM((branches, count, ffw), F32),
            pltpu.VMEM((total, piece), BF16),
            pltpu.SemaphoreType.DMA((groups,)),
            pltpu.SemaphoreType.DMA((2 * ffw // 256,)),
            pltpu.SemaphoreType.DMA,
            pltpu.SemaphoreType.DMA((groups,)),
        ],
        compiler_params=params(56),
        cost_estimate=cost(4 * count * depth * ffw * branches, 30 * MB),
        name="expert",
    )(blocks, base, low, high, scale, grad_hidden)


def expert_grads_kernel(
    halves, cotangent_ref, grad_ref, base_ref, high_ref, units_ref, low_out_ref, back_low_ref,
    *rest
):
    inputs = rest[:halves]
    low_acts, grad_linears, backs = (
        rest[halves : 2 * halves], rest[2 * halves : 3 * halves], rest[3 * halves : 4 * halves]
    )
    mag_ref, high_grad_ref, low_in_ref, low_grad_ref, high_in_ref, low_down, low_down_t, back_t = (
        rest[4 * halves :]
    )
    count = units_ref.shape[0] // halves
    rank = low_out_ref.shape[1]

    @pl.when(pl.program_id(0) == 0)
    def _():
        low = dot(units_ref[...], low_out_ref[...])
        low_down[...] = low.astype(BF16)
        low_down_t[...] = low.T.astype(BF16)
        low_grad_ref[...] = dot(back_low_ref[...].astype(F32).T.astype(BF16), units_ref[...])
        high_in_ref[...] = jnp.zeros_like(high_in_ref)
        for h in range(halves):
            back_t[h] = backs[h][...].astype(F32).T.astype(BF16)
            low_act_t = low_acts[h][...].astype(F32).T.astype(BF16)
            for j in range(2):
                high_in_ref[j] += dot(low_act_t[j * rank : (j + 1) * rank], grad_linears[h][j])

    mag = jnp.zeros((1, base_ref.shape[1]), F32)
    low_in = jnp.zeros(low_in_ref.shape, F32)
    for h in range(halves):
        rows = slice(h * count, (h + 1) * count)
        linear = dot(units_ref[rows, :], base_ref[...]) + dot(low_down[rows, :], high_ref[...])
        mag = mag + jnp.sum(linear * cotangent_ref[rows, :].astype(F32), axis=0, keepdims=True)
        low_in = low_in + dot(back_t[h], inputs[h][...])
    mag_ref[...] = mag
    low_in_ref[...] = low_in
    high_grad_ref[...] = dot(low_down_t[...], grad_ref[...])


def expert_grads(
    cotangent, grad_linear, base, high, units, low_out, back_low, inputs, low_acts, grad_linears,
    backs,
):
    halves = len(inputs)
    ffw, width = base.shape
    count, rank = back_low.shape
    tile = 512
    whole = lambda array: pl.BlockSpec(array.shape, lambda i: (0,) * array.ndim)
    part = lambda rows: pl.BlockSpec((rows, tile), lambda i: (0, i))
    fixed = [units, low_out, back_low]
    return pl.pallas_call(
        functools.partial(expert_grads_kernel, halves),
        grid=(width // tile,),
        in_specs=[part(count), part(count), part(ffw), part(rank)]
        + [whole(array) for array in fixed]
        + [part(count // halves)] * halves
        + [whole(array) for array in low_acts + grad_linears + backs],
        out_specs=[
            part(1),
            part(rank),
            part(2 * rank),
            pl.BlockSpec((rank, ffw), lambda i: (0, 0)),
            pl.BlockSpec((2, rank, ffw), lambda i: (0, 0, 0)),
        ],
        out_shape=[
            jax.ShapeDtypeStruct((1, width), F32),
            jax.ShapeDtypeStruct((rank, width), F32),
            jax.ShapeDtypeStruct((2 * rank, width), F32),
            jax.ShapeDtypeStruct((rank, ffw), F32),
            jax.ShapeDtypeStruct((2, rank, ffw), F32),
        ],
        scratch_shapes=[
            pltpu.VMEM((count, rank), BF16),
            pltpu.VMEM((rank, count), BF16),
            pltpu.VMEM((halves, 2 * rank, count // halves), BF16),
        ],
        compiler_params=params(60),
        cost_estimate=cost(1, 1),
        name="expert_grads",
    )(cotangent, grad_linear, base, high, *fixed, *inputs, *low_acts, *grad_linears, *backs)


def square_norm(base, low, high):
    merged = base.astype(F32) + dot(low, high)
    return jnp.sqrt(jnp.sum(merged * merged, axis=0))


def shards(
    query, keyval, doc_lengths, norm_gain, router_logits, expert_ids, grad_out,
    base_in, low_in, high_in, mag_in, base_out, low_out, high_out, mag_out,
):
    query, local_kv, grad_out = query[0], keyval[0], grad_out[0]
    base_in, low_in, high_in, mag_in = base_in[0], low_in[0], high_in[0], mag_in[0]
    base_out, low_out, high_out, mag_out = base_out[0], low_out[0], high_out[0], mag_out[0]
    ids = expert_ids[0]
    tokens, width = query.shape
    top = ids.shape[1]
    experts = lax.axis_size("ctx") * lax.axis_size("ep")
    axes = ("ctx", "ep")
    gain = norm_gain[None, :]
    halves = 2
    slots_each = CAP // halves
    ctx_count = lax.axis_size("ctx")

    def exchange(blocks):
        split = blocks.reshape(experts, BLOCK, blocks.shape[1])
        moved = lax.all_to_all(split, axes, split_axis=0, concat_axis=0, tiled=True)
        return moved.reshape(blocks.shape)

    named = jnp.zeros((experts, tokens), jnp.bool_)
    each = jnp.arange(experts, dtype=jnp.int32)[:, None]
    for k in range(top):
        named = named | (ids[:, k][None, :] == each)
    earlier = jnp.arange(tokens)[:, None] < jnp.arange(tokens)[None, :]
    before = dot(named.astype(BF16), earlier.astype(BF16))
    slots = jnp.where(named, before, -1.0)

    seen = gather(local_kv, ctx_count)
    first = lax.axis_index("ctx") * tokens
    place = jnp.concatenate(
        [
            jnp.stack([first - REACH * tokens, first]).astype(jnp.int32),
            jnp.cumsum(doc_lengths[0]).astype(jnp.int32),
        ]
    )

    outgoing_grad, _ = dispatch(slots, grad_out, gain, False, 1)
    outgoing_grad, seen = lax.optimization_barrier((outgoing_grad, seen))
    arrived_grad = exchange(outgoing_grad)

    prob, hidden = attend(place, query, seen)
    *outgoing, rinv = dispatch(slots, hidden, gain, True, halves)

    norm_in = jnp.stack([square_norm(base_in[j], low_in[j], high_in[j]) for j in range(2)])
    scale_in = mag_in / norm_in
    norm_out = square_norm(base_out, low_out, high_out)
    scale_out = mag_out / norm_out
    cotangent = unpack(arrived_grad, halves).reshape(experts * CAP, width)
    grad_linear_out = (cotangent.astype(F32) * scale_out).astype(BF16)
    back_low = contract(grad_linear_out, high_out, 1, 1).astype(BF16)
    grad_hidden = contract(grad_linear_out, base_out, 1, 1) + contract(back_low, low_out, 1, 1)
    low_pair = jnp.concatenate([low_in[0], low_in[1]], axis=1)
    arrived = [exchange(outgoing[0])]
    second, grad_hidden, scale_in, low_pair, _ = lax.optimization_barrier(
        (outgoing[1], grad_hidden, scale_in, low_pair, arrived[0])
    )
    arrived.append(exchange(second))

    rows_each = experts * slots_each
    returned, results = [], []
    for h in range(halves):
        outgoing_rows, *result = expert(
            slots_each, arrived[h], base_in, low_pair, high_in, scale_in,
            grad_hidden[h * rows_each : (h + 1) * rows_each],
        )
        returned.append(exchange(outgoing_rows))
        results.append(result)
    results, first_returned = lax.optimization_barrier((results, returned[0]))
    returned[0] = first_returned
    inputs, units, low_acts, grad_linears, backs, products, mag_sums = zip(*results)

    mag_sum, grad_high_out, low_in_t, low_out_t, grad_high_in = expert_grads(
        cotangent, grad_linear_out, base_out, high_out, jnp.concatenate(units, axis=0), low_out,
        back_low, inputs, low_acts, grad_linears, backs,
    )
    grad_mag_out = mag_sum[0] / norm_out
    grad_low_out = low_out_t.T
    grad_low_in = low_in_t.reshape(2, -1, width).transpose(0, 2, 1)
    grad_mag_in = sum(mag_sums) / norm_in
    products = jnp.concatenate(
        [part.astype(BF16).reshape(experts, slots_each) for part in products], axis=1
    )

    logits = router_logits[0]
    gate_expo = jnp.exp(logits - jnp.max(logits, axis=-1, keepdims=True))
    gates = gate_expo / jnp.sum(gate_expo, axis=-1, keepdims=True)
    dense_gates = jnp.zeros((tokens, experts), F32)
    chosen = [ids[:, k : k + 1] == each.reshape(1, experts) for k in range(top)]
    for k in range(top):
        dense_gates = dense_gates + jnp.where(chosen[k], gates[:, k : k + 1], 0.0)
    token_slots = slots.T
    partial = combine_first(token_slots, dense_gates, returned[0], halves)
    grad_heads = combine_last(
        token_slots, dense_gates, returned[1], partial, gain, grad_out, hidden, rinv, halves
    )
    products, grad_heads = lax.optimization_barrier((products, grad_heads))
    returned_products = lax.all_to_all(products, axes, split_axis=0, concat_axis=0, tiled=True)
    dense_products = jnp.zeros((tokens, experts), F32)
    for r in range(CAP):
        dense_products = dense_products + jnp.where(
            token_slots == r, returned_products[:, r].astype(F32)[None, :], 0.0
        )
    grad_gate = jnp.stack(
        [jnp.sum(jnp.where(chosen[k], dense_products, 0.0), axis=1) for k in range(top)], axis=1
    )
    grad_logits = gates * (grad_gate - jnp.sum(gates * grad_gate, axis=-1, keepdims=True))

    queries, terms = [], []
    for m in range(local_kv.shape[1] // 2 // HEAD):
        query_part, term = attend_back(m, query, grad_heads, prob, seen)
        queries.append(query_part)
        terms.append(term)
    grad_keyval = scatter(terms, tokens, ctx_count)
    grad_query = jnp.concatenate(queries, axis=1)
    return (
        grad_query[None],
        grad_keyval[None],
        grad_logits[None],
        grad_low_in[None],
        grad_high_in[None],
        grad_mag_in[None],
        grad_low_out[None],
        grad_high_out[None],
        grad_mag_out[None],
    )


def solution(mesh):
    rows = P("ep", "ctx", None)
    own = lambda extra: P(("ctx", "ep"), *([None] * extra))
    in_specs = (
        rows, rows, P("ep", None), P(), rows, rows, rows,
        own(3), own(3), own(3), own(2), own(2), own(2), own(2), own(1),
    )
    out_specs = (rows, rows, rows, own(3), own(3), own(2), own(2), own(2), own(1))
    return jax.shard_map(shards, mesh=mesh, in_specs=in_specs, out_specs=out_specs, check_vma=False)
```

profile of v0, /device:TPU:1, one launch (start us, length us, event | category | flops | bytes accessed | tf_op | source)
XLA Modules:
  0.0 284.7 jit_solution(16788270801330309605)
XLA Ops:
  3.7 17.5 %gather.1.keyval_ref.keys_ref.values_ref = bf16[640,512]{1,0:T(8,128)(2,1)} custom-call(bf16[128,512]{1,0:T(8,128)(2,1)} %bitcast.154), custom_call_target="tpu_custom_call" | custom-call | tf_op jit(solution)/shard_map/gather/pallas_call | solution.py:227
  22.0 7.4 %dispatch.2 = (bf16[2048,1024]{1,0:T(8,128)(2,1)}, f32[128,1]{1,0:T(8,128)}) custom-call(f32[128,128]{1,0:T(8,128)} %get-tuple-element.176.slots_ref, bf16[128,4096]{1,0:T(8,128)(2,1)} %bitcast.169, f32[1,4096]{1,0:T(1,128)} %bitcast.177), custom_call_target="tpu_custom_call" | custom-call | flops 2147483648 | bytes 10485760 | tf_op jit(solution)/shard_map/dispatch/pallas_call | solution.py:111
  29.4 10.3 %all-to-all-start.1 = ((bf16[128,16,1024]{2,1,0:T(8,128)(2,1)}), bf16[128,16,1024]{2,1,0:T(8,128)(2,1)}, u32[]{:S(2)}, u32[]{:S(2)}) async-start(bf16[128,16,1024]{2,1,0:T(8,128)(2,1)} %bitcast.140), calls=%async_computation.1 | async-start | bytes 8388608 | tf_op jit(solution)/shard_map/all_to_all | solution.py:842
  39.8 4.8 %multiply_reduce_fusion = f32[4096]{0:T(1024)S(1)} fusion(bf16[1,768,32]{1,2,0:T(8,128)(2,1)S(1)} %copy-done.8, bf16[1,32,4096]{2,1,0:T(8,128)(2,1)S(1)} %copy-done.7, bf16[1,768,4096]{2,1,0:T(8,128)(2,1)} %param.26), kind=kOutput, calls=%fused_computation.6 | convolution fusion | flops 213905408 | bytes 6619136 | tf_op jit(solution)/shard_map/dot_general | solution.py:37
  53.2 13.7 %attend.1 = (bf16[8,640,512]{2,1,0:T(8,128)(2,1)}, bf16[128,4096]{1,0:T(8,128)(2,1)}) custom-call(s32[6]{0:T(128)} %pad_add_fusion.place_ref, bf16[128,4096]{1,0:T(8,128)(2,1)} %bitcast.135, bf16[640,512]{1,0:T(8,128)(2,1)} %gather.1.keyval_ref.keys_ref.values_ref), custom_call_target="tpu_custom_call" | custom-call | flops 1342177280 | bytes 9437184 | tf_op jit(solution)/shard_map/attend/pallas_call | solution.py:369
  67.5 9.2 %dispatch.3 = (bf16[2048,512]{1,0:T(8,128)(2,1)}, bf16[2048,512]{1,0:T(8,128)(2,1)}, f32[128,1]{1,0:T(8,128)}) custom-call(f32[128,128]{1,0:T(8,128)} %get-tuple-element.176.slots_ref, bf16[128,4096]{1,0:T(8,128)(2,1)} %get-tuple-element.65.rows_ref.hidden_ref, f32[1,4096]{1,0:T(1,128)} %bitcast.178), custom_call_target="tpu_custom_call" | custom-call | flops 4294967296 | bytes 10485760 | tf_op jit(solution)/shard_map/dispatch/pallas_call | solution.py:111
  78.3 13.0 %all-to-all-done.1 = bf16[128,16,1024]{2,1,0:T(8,128)(2,1)} async-done(((bf16[128,16,1024]{2,1,0:T(8,128)(2,1)}), bf16[128,16,1024]{2,1,0:T(8,128)(2,1)}, u32[]{:S(2)}, u32[]{:S(2)}) %all-to-all-start.1) | async-done | bytes 4194336 | tf_op jit(solution)/shard_map/all_to_all | solution.py:842
  91.2 5.5 %all-to-all-start = ((bf16[128,16,512]{2,1,0:T(8,128)(2,1)}), bf16[128,16,512]{2,1,0:T(8,128)(2,1)}, u32[]{:S(2)}, u32[]{:S(2)}) async-start(bf16[128,16,512]{2,1,0:T(8,128)(2,1)} %bitcast.146), calls=%async_computation | async-start | bytes 4194304 | tf_op jit(solution)/shard_map/all_to_all | solution.py:842
  96.8 7.7 %unpack.1 = bf16[2,256,4096]{2,1,0:T(8,128)(2,1)} custom-call(bf16[2048,1024]{1,0:T(8,128)(2,1)} %bitcast.15.blocks_ref), custom_call_target="tpu_custom_call" | custom-call | flops 1073741824 | bytes 8388608 | tf_op jit(solution)/shard_map/unpack/pallas_call | solution.py:145
  113.3 12.8 %all-to-all-done = bf16[128,16,512]{2,1,0:T(8,128)(2,1)} async-done(((bf16[128,16,512]{2,1,0:T(8,128)(2,1)}), bf16[128,16,512]{2,1,0:T(8,128)(2,1)}, u32[]{:S(2)}, u32[]{:S(2)}) %all-to-all-start) | async-done | bytes 2097184 | tf_op jit(solution)/shard_map/all_to_all | solution.py:842
  126.1 5.6 %all-to-all-start.2 = ((bf16[128,16,512]{2,1,0:T(8,128)(2,1)}), bf16[128,16,512]{2,1,0:T(8,128)(2,1)}, u32[]{:S(2)}, u32[]{:S(2)}) async-start(bf16[128,16,512]{2,1,0:T(8,128)(2,1)} %bitcast.144), calls=%async_computation.2 | async-start | bytes 4194304 | tf_op jit(solution)/shard_map/all_to_all | solution.py:842
  132.9 23.7 %expert.2 = (bf16[2048,512]{1,0:T(8,128)(2,1)}, bf16[256,4096]{1,0:T(8,128)(2,1)}, bf16[256,768]{1,0:T(8,128)(2,1)}, bf16[256,64]{1,0:T(8,128)(2,1)}, bf16[2,256...) custom-call(bf16[2048,512]{1,0:T(8,128)(2,1)} %bitcast.12.blocks_hbm, ...), custom_call_target="tpu_custom_call" | custom-call | flops 6442450944 | bytes 31457280 | tf_op jit(solution)/shard_map/expert/pallas_call | solution.py:705
  161.2 5.4 %all-to-all-start.3 = ((bf16[128,16,512]{2,1,0:T(8,128)(2,1)}), bf16[128,16,512]{2,1,0:T(8,128)(2,1)S(1)}, u32[]{:S(2)}, u32[]{:S(2)}) async-start(bf16[128,16,512]{2,1,0:T(8,128)(2,1)} %bitcast.145), calls=%async_computation.3 | async-start | bytes 4194304 | tf_op jit(solution)/shard_map/all_to_all | solution.py:842
  166.6 23.7 %expert.3 = (bf16[2048,512]{1,0:T(8,128)(2,1)}, bf16[256,4096]{1,0:T(8,128)(2,1)}, bf16[256,768]{1,0:T(8,128)(2,1)}, bf16[256,64]{1,0:T(8,128)(2,1)}, bf16[2,256...) custom-call(bf16[2048,512]{1,0:T(8,128)(2,1)} %bitcast.31.blocks_hbm, ...), custom_call_target="tpu_custom_call" | custom-call | flops 6442450944 | bytes 31457280 | tf_op jit(solution)/shard_map/expert/pallas_call | solution.py:705
  190.2 6.0 %all-to-all-done.3 = bf16[128,16,512]{2,1,0:T(8,128)(2,1)S(1)} async-done(((bf16[128,16,512]{2,1,0:T(8,128)(2,1)}), bf16[128,16,512]{2,1,0:T(8,128)(2,1)S(1)}, u32[]{:S(2)}, u32[]{:S(2)}) %all-to-all-start.3) | async-done | bytes 2097184 | tf_op jit(solution)/shard_map/all_to_all | solution.py:842
  196.3 5.6 %all-to-all-start.4 = ((bf16[128,16,512]{2,1,0:T(8,128)(2,1)}), bf16[128,16,512]{2,1,0:T(8,128)(2,1)}, u32[]{:S(2)}, u32[]{:S(2)}) async-start(bf16[128,16,512]{2,1,0:T(8,128)(2,1)} %bitcast.143), calls=%async_computation.4 | async-start | bytes 4194304 | tf_op jit(solution)/shard_map/all_to_all | solution.py:842
  202.7 5.4 %multiply_convert_fusion.grad_ref = bf16[512,4096]{1,0:T(8,128)(2,1)} fusion(f32[4096]{0:T(1024)S(1)} %bitcast.151, bf16[2,256,4096]{2,1,0:T(8,128)(2,1)} %unpack.1), kind=kLoop, calls=%fused_computation.7 | loop fusion | flops 6291456 | bytes 8404992 | tf_op jit(solution)/shard_map/convert_element_type | solution.py:874
  208.1 6.7 %combine_first.1.first_ref = f32[1024,512]{1,0:T(8,128)} custom-call(f32[128,128]{1,0:T(8,128)} %get-tuple-element.177.slots_ref, f32[128,128]{1,0:T(8,128)} %get-tuple-element.175.gates_ref, bf16[2048,512]{1,0:T(8,128)(2,1)} %bitcast.131), custom_call_target="tpu_custom_call" | custom-call | flops 1 | bytes 1 | tf_op jit(solution)/shard_map/combine_first/pallas_call | solution.py:535
  215.8 13.8 %expert_grads.1 = (f32[1,4096]{1,0:T(1,128)}, f32[32,4096]{1,0:T(8,128)}, f32[64,4096]{1,0:T(8,128)}, f32[32,768]{1,0:T(8,128)}, f32[2,32,768]{2,1,0:T(8,128)}) custom-call(bf16[512,4096]{1,0:T(8,128)(2,1)} %bitcast.130, bf16[512,4096]{1,0:T(8,128)(2,1)} %multiply_convert_fusion.grad_ref, bf16[768,4096]{1,0:T(8,128)(2,1)} %bitcast.132, ...), custom_call_target="tpu_custom_call" | custom-call | flops 1 | bytes 1 | tf_op jit(solution)/shard_map/expert_grads/pallas_call | solution.py:786
  232.3 8.6 %combine_last.1.grad_ref = bf16[128,4096]{1,0:T(8,128)(2,1)} custom-call(f32[128,128]{1,0:T(8,128)} %get-tuple-element.177.slots_ref, f32[128,128]{1,0:T(8,128)} %get-tuple-element.175.gates_ref, bf16[2048,512]{1,0:T(8,128)(2,1)} %bitcast.39.blocks_ref, f32[1024,512]{1,0:T(8,128)} %combine_first.1.first_ref, f32[1,4096]{1,0:T(1,128)} %bitcast.179, ...), custom_call_target="tpu_custom_call" | custom-call | flops 2147483648 | bytes 8388608 | tf_op jit(solution)/shard_map/combine_last/pallas_call | solution.py:556
  241.0 7.9 %attend_back.3 = (bf16[128,2048]{1,0:T(8,128)(2,1)}, bf16[640,256]{1,0:T(8,128)(2,1)}) custom-call(bf16[128,4096]{1,0:T(8,128)(2,1)} %bitcast.136, bf16[128,4096]{1,0:T(8,128)(2,1)} %combine_last.1.grad_ref, bf16[8,640,512]{2,1,0:T(8,128)(2,1)} %get-tuple-element.94.prob_ref, bf16[640,512]{1,0:T(8,128)(2,1)} %gather.1.keyval_ref.keys_ref.values_ref, ...), custom_call_target="tpu_custom_call" | custom-call | flops 1342177280 | bytes 5242880 | tf_op jit(solution)/shard_map/attend_back/pallas_call | solution.py:433
  248.9 7.9 %attend_back.2 = (bf16[128,2048]{1,0:T(8,128)(2,1)}, bf16[640,256]{1,0:T(8,128)(2,1)}) custom-call(bf16[128,4096]{1,0:T(8,128)(2,1)} %bitcast.137, bf16[128,4096]{1,0:T(8,128)(2,1)} %combine_last.1.grad_ref, bf16[8,640,512]{2,1,0:T(8,128)(2,1)} %get-tuple-element.94.prob_ref, bf16[640,512]{1,0:T(8,128)(2,1)} %gather.1.keyval_ref.keys_ref.values_ref, ...), custom_call_target="tpu_custom_call" | custom-call | flops 1342177280 | bytes 5242880 | tf_op jit(solution)/shard_map/attend_back/pallas_call | solution.py:433
  257.6 9.9 %all-to-all-start.5 = ((bf16[128,1,4]{2,1,0:T(2,128)(2,1)}), bf16[128,1,4]{2,1,0:T(2,128)(2,1)S(1)}, u32[]{:S(2)}, u32[]{:S(2)}) async-start(bf16[128,1,4]{2,1,0:T(2,128)(2,1)} %copy.65), calls=%async_computation.5 | async-start | bytes 131072 | tf_op jit(solution)/shard_map/all_to_all | solution.py:922
  269.6 12.6 %scatter.1 = bf16[128,512]{1,0:T(8,128)(2,1)} custom-call(bf16[640,256]{1,0:T(8,128)(2,1)} %get-tuple-element.97.rest_0_, bf16[640,256]{1,0:T(8,128)(2,1)} %get-tuple-element.98.rest_1_), custom_call_target="tpu_custom_call" | custom-call | tf_op jit(solution)/shard_map/scatter/pallas_call | solution.py:296
  (99 shorter events, 38.8 us)
Async XLA Ops:
  29.4 10.3 %copy-start.7 = (bf16[1,32,4096]{2,1,0:T(8,128)(2,1)S(1)}, bf16[1,32,4096]{2,1,0:T(8,128)(2,1)}, u32[]{:S(2)}) copy-start(bf16[1,32,4096]{2,1,0:T(8,128)(2,1)} %param.28) | copy-start | bytes 786436
  29.4 10.3 %copy-start.8 = (bf16[1,768,32]{1,2,0:T(8,128)(2,1)S(1)}, bf16[1,768,32]{1,2,0:T(8,128)(2,1)}, u32[]{:S(2)}) copy-start(bf16[1,768,32]{1,2,0:T(8,128)(2,1)} %param.27) | copy-start | bytes 147460
  29.4 61.8 %all-to-all-start.1 = ((bf16[128,16,1024]{2,1,0:T(8,128)(2,1)}), bf16[128,16,1024]{2,1,0:T(8,128)(2,1)}, u32[]{:S(2)}, u32[]{:S(2)}) async-start(bf16[128,16,1024]{2,1,0:T(8,128)(2,1)} %bitcast.140), calls=%async_computation.1 | async-start | bytes 8388608 | tf_op jit(solution)/shard_map/all_to_all | solution.py:842
  39.7 4.9 %copy-start.3 = (bf16[1,2,4096,32]{2,3,1,0:T(8,128)(2,1)S(1)}, bf16[1,2,4096,32]{2,3,1,0:T(8,128)(2,1)}, u32[]{:S(2)}) copy-start(bf16[1,2,4096,32]{2,3,1,0:T(8,128)(2,1)} %param.23) | copy-start | bytes 1572868
  39.7 4.9 %copy-start.16 = (bf16[1,2,32,768]{3,2,1,0:T(8,128)(2,1)S(1)}, bf16[1,2,32,768]{3,2,1,0:T(8,128)(2,1)}, u32[]{:S(2)}) copy-start(bf16[1,2,32,768]{3,2,1,0:T(8,128)(2,1)} %param.24) | copy-start | bytes 294916
  39.7 9.2 %slice-start.2 = ((s8[12582912]{0:T(1024)(128)(4,1)}), s8[4194304]{0:T(1024)(128)(4,1)S(1)}, s32[]{:S(2)}) async-start(s8[12582912]{0:T(1024)(128)(4,1)} %bitcast.167), calls=%async_computation.8 | async-start | bytes 8388608
  39.8 9.2 %slice-start.3 = ((s8[12582912]{0:T(1024)(128)(4,1)}), s8[4194304]{0:T(1024)(128)(4,1)S(1)}, s32[]{:S(2)}) async-start(s8[12582912]{0:T(1024)(128)(4,1)} %bitcast.167), calls=%async_computation.9 | async-start | bytes 8388608
  51.4 15.5 %copy-start.13 = (f32[1,2,768]{2,1,0:T(2,128)S(1)}, f32[1,2,768]{2,1,0:T(2,128)}, u32[]{:S(2)}) copy-start(f32[1,2,768]{2,1,0:T(2,128)} %param.25) | copy-start | bytes 18436
  91.2 34.9 %all-to-all-start = ((bf16[128,16,512]{2,1,0:T(8,128)(2,1)}), bf16[128,16,512]{2,1,0:T(8,128)(2,1)}, u32[]{:S(2)}, u32[]{:S(2)}) async-start(bf16[128,16,512]{2,1,0:T(8,128)(2,1)} %bitcast.146), calls=%async_computation | async-start | bytes 4194304 | tf_op jit(solution)/shard_map/all_to_all | solution.py:842
  96.8 12.5 %slice-start = ((s8[6291456]{0:T(1024)(128)(4,1)}), s8[2097152]{0:T(1024)(128)(4,1)S(1)}, s32[]{:S(2)}) async-start(s8[6291456]{0:T(1024)(128)(4,1)} %bitcast.133), calls=%async_computation.6 | async-start | bytes 4194304
  126.1 35.1 %all-to-all-start.2 = ((bf16[128,16,512]{2,1,0:T(8,128)(2,1)}), bf16[128,16,512]{2,1,0:T(8,128)(2,1)}, u32[]{:S(2)}, u32[]{:S(2)}) async-start(bf16[128,16,512]{2,1,0:T(8,128)(2,1)} %bitcast.144), calls=%async_computation.2 | async-start | bytes 4194304 | tf_op jit(solution)/shard_map/all_to_all | solution.py:842
  161.2 35.1 %all-to-all-start.3 = ((bf16[128,16,512]{2,1,0:T(8,128)(2,1)}), bf16[128,16,512]{2,1,0:T(8,128)(2,1)S(1)}, u32[]{:S(2)}, u32[]{:S(2)}) async-start(bf16[128,16,512]{2,1,0:T(8,128)(2,1)} %bitcast.145), calls=%async_computation.3 | async-start | bytes 4194304 | tf_op jit(solution)/shard_map/all_to_all | solution.py:842
  196.3 11.8 %copy-start = (bf16[128,16,512]{2,1,0:T(8,128)(2,1)}, bf16[128,16,512]{2,1,0:T(8,128)(2,1)S(1)}, u32[]{:S(2)}) copy-start(bf16[128,16,512]{2,1,0:T(8,128)(2,1)S(1)} %all-to-all-done.3) | copy-start | bytes 6291460
  196.3 36.1 %all-to-all-start.4 = ((bf16[128,16,512]{2,1,0:T(8,128)(2,1)}), bf16[128,16,512]{2,1,0:T(8,128)(2,1)}, u32[]{:S(2)}, u32[]{:S(2)}) async-start(bf16[128,16,512]{2,1,0:T(8,128)(2,1)} %bitcast.143), calls=%async_computation.4 | async-start | bytes 4194304 | tf_op jit(solution)/shard_map/all_to_all | solution.py:842
  208.1 6.7 %copy-start.5 = (bf16[256,768]{1,0:T(8,128)(2,1)S(1)}, bf16[256,768]{1,0:T(8,128)(2,1)}, u32[]{:S(2)}) copy-start(bf16[256,768]{1,0:T(8,128)(2,1)} %get-tuple-element.100) | copy-start | bytes 1179652
  208.1 6.7 %copy-start.6 = (bf16[256,768]{1,0:T(8,128)(2,1)S(1)}, bf16[256,768]{1,0:T(8,128)(2,1)}, u32[]{:S(2)}) copy-start(bf16[256,768]{1,0:T(8,128)(2,1)} %get-tuple-element.101) | copy-start | bytes 1179652
  215.8 13.9 %copy-start.9 = (f32[256,1]{1,0:T(8,128)S(1)}, f32[256,1]{1,0:T(8,128)}, u32[]{:S(2)}) copy-start(f32[256,1]{1,0:T(8,128)} %get-tuple-element.88) | copy-start | bytes 3076
  215.8 13.9 %copy-start.10 = (f32[256,1]{1,0:T(8,128)S(1)}, f32[256,1]{1,0:T(8,128)}, u32[]{:S(2)}) copy-start(f32[256,1]{1,0:T(8,128)} %get-tuple-element.89) | copy-start | bytes 3076
  215.8 15.9 %copy-start.14 = (f32[2,768]{1,0:T(2,128)S(1)}, f32[2,768]{1,0:T(2,128)}, u32[]{:S(2)}) copy-start(f32[2,768]{1,0:T(2,128)} %get-tuple-element.112) | copy-start | bytes 18436
  215.8 15.9 %copy-start.15 = (f32[2,768]{1,0:T(2,128)S(1)}, f32[2,768]{1,0:T(2,128)}, u32[]{:S(2)}) copy-start(f32[2,768]{1,0:T(2,128)} %get-tuple-element.113) | copy-start | bytes 18436
  248.9 18.6 %copy-start.4 = (bf16[128,2048]{1,0:T(8,128)(2,1)S(1)}, bf16[128,2048]{1,0:T(8,128)(2,1)}, u32[]{:S(2)}) copy-start(bf16[128,2048]{1,0:T(8,128)(2,1)} %get-tuple-element.96) | copy-start | bytes 1572868
  248.9 33.4 %copy-start.1 = (f32[128,128]{1,0:T(8,128)S(1)}, f32[128,128]{1,0:T(8,128)}, u32[]{:S(2)}) copy-start(f32[128,128]{1,0:T(8,128)} %get-tuple-element.177.slots_ref) | copy-start | bytes 196612
  248.9 33.7 %copy-start.11 = (f32[1,128,3]{1,0,2:T(1,128)S(1)}, f32[1,128,3]{1,0,2:T(1,128)}, u32[]{:S(2)}) copy-start(f32[1,128,3]{1,0,2:T(1,128)} %param.19) | copy-start | bytes 4612
  257.6 24.6 %all-to-all-start.5 = ((bf16[128,1,4]{2,1,0:T(2,128)(2,1)}), bf16[128,1,4]{2,1,0:T(2,128)(2,1)S(1)}, u32[]{:S(2)}, u32[]{:S(2)}) async-start(bf16[128,1,4]{2,1,0:T(2,128)(2,1)} %copy.65), calls=%async_computation.5 | async-start | bytes 131072 | tf_op jit(solution)/shard_map/all_to_all | solution.py:922
  (5 other events, 19.8 us)
where the time goes:
time: 289 us; the launch traced here: 285 us
  Pallas kernels  160 us (55%)
  starting transfers between devices  42.3 us (15%)
  waiting for transfers between devices  36.3 us (13%)
  other arithmetic  20.3 us (7%)
  matrix products  16.8 us (6%)
  local copies, waits for them, and re-layouts  7.48 us (3%)
    pallas_call x2, Pallas kernels, expert(): pl.pallas_call(functools.partial(expert_kernel, slots), in_specs=[hbm, hb...  47.4 us
    all_to_all x5, waiting for transfers between devices, exchange(): moved = lax.all_to_all(split, axes, split_axis=0, concat_axis=0, tiled=True)  36.3 us
    all_to_all x5, starting transfers between devices, exchange(): moved = lax.all_to_all(split, axes, split_axis=0, concat_axis=0, tiled=True)  32.4 us
    pallas_call x1, Pallas kernels, gather(): pl.pallas_call(functools.partial(gather_kernel, count), in_specs=[vmem],...  17.5 us
    pallas_call x2, Pallas kernels, dispatch(): pl.pallas_call(functools.partial(dispatch_kernel, with_norm), grid=(total...  16.6 us
    pallas_call x2, Pallas kernels, attend_back(): pl.pallas_call(functools.partial(attend_back_kernel, heads), grid=(steps,...  15.8 us
    pallas_call x1, Pallas kernels, expert_grads(): pl.pallas_call(functools.partial(expert_grads_kernel, halves), grid=(widt...  13.8 us
    pallas_call x1, Pallas kernels, attend(): pl.pallas_call(functools.partial(attend_kernel, heads, per_kv), grid=(ste...  13.7 us
  transfers between devices with their start and end apart: 6, of which 4 were waited for; matrix products, arithmetic and copies ran while one was open for 13% of the time, Pallas kernels for 39%

commit v1 on v0

--- a/solution.py
+++ b/solution.py
@@ -156,50 +156,66 @@
     )(blocks)
 
 
-def neighbours(position, count):
-    near = []
-    for j in range(1, REACH + 1):
-        near.append((position + j < count, j))
-        near.append((position >= j, -j))
-    return near
-
-
-def greet(position, count):
+def open_kernel(
+    count, own_ref, slots_ref, rows_ref, seen_ref, out_hbm, stack, blocks, send_sem, recv_sem,
+    own_sem, out_sem,
+):
+    tokens, width = rows_ref.shape
+    pieces = BLOCK // CAP
+    piece = width // pieces
+    groups = blocks.shape[0] // GROUP
+    me = lax.axis_index("ctx")
+    core = me % 2
+    other = me + 1 - 2 * core
+
+    def slot(j):
+        return seen_ref.at[pl.ds((REACH - j) * tokens, tokens)]
+
+    def copy(source, j, target, index):
+        return pltpu.make_async_remote_copy(
+            src_ref=source,
+            dst_ref=slot(j),
+            send_sem=send_sem.at[index],
+            recv_sem=recv_sem.at[index],
+            device_id={"ctx": target},
+            device_id_type=MESH,
+        )
+
+    near = copy(own_ref, 2, me + 2, 0)
+    far = copy(own_ref, 4, me + 4, 1)
+    beside = copy(own_ref, 1, other, 2)
+    near_even = copy(slot(2), 3, other, 3)
+    near_odd = copy(slot(2), 1, other, 3)
+    far_odd = copy(slot(4), 3, other, 4)
+
+    keep = pltpu.make_async_copy(own_ref, slot(0), own_sem)
+    keep.start()
     barrier = pltpu.get_barrier_semaphore()
-    for present, j in neighbours(position, count):
+    peers = 1
+    for offset in (2, 4, -2, -4):
+        present = (me + offset >= 0) & (me + offset < count)
+        peers = peers + present.astype(jnp.int32)
 
         @pl.when(present)
         def _():
             pl.semaphore_signal(
-                barrier, inc=1, device_id={"ctx": position + j}, device_id_type=MESH
+                barrier, inc=1, device_id={"ctx": me + offset}, device_id_type=MESH
             )
 
-    peers = jnp.minimum(position, REACH) + jnp.minimum(count - 1 - position, REACH)
+    pl.semaphore_signal(barrier, inc=1, device_id={"ctx": other}, device_id_type=MESH)
     pl.semaphore_wait(barrier, peers)
 
-
-def gather_kernel(count, own_ref, seen_ref, send_sem, recv_sem, own_sem):
-    tokens = own_ref.shape[0]
-    me = lax.axis_index("ctx")
-
-    def copy(j):
-        return pltpu.make_async_remote_copy(
-            src_ref=own_ref,
-            dst_ref=seen_ref.at[pl.ds((REACH - j) * tokens, tokens)],
-            send_sem=send_sem.at[j - 1],
-            recv_sem=recv_sem.at[j - 1],
-            device_id={"ctx": me + j},
-            device_id_type=MESH,
-        )
-
-    keep = pltpu.make_async_copy(own_ref, seen_ref.at[pl.ds(REACH * tokens, tokens)], own_sem)
-    keep.start()
-    greet(me, count)
-    for j in range(REACH, 0, -1):
-
-        @pl.when(me + j < count)
-        def _():
-            copy(j).start()
+    @pl.when(me + 4 < count)
+    def _():
+        far.start()
+
+    @pl.when(me + 2 < count)
+    def _():
+        near.start()
+
+    @pl.when(core == 0)
+    def _():
+        beside.start()
 
     for j in range(1, REACH + 1):
 
@@ -209,105 +225,110 @@
                 own_ref.shape, own_ref.dtype
             )
 
+    for p in range(pieces):
+        stack[p * tokens : (p + 1) * tokens, :] = rows_ref[:, p * piece : (p + 1) * piece]
+    spread = (iota((GROUP, PER_GROUP), 0) // BLOCK == iota((GROUP, PER_GROUP), 1)).astype(F32)
+    spread = spread.astype(BF16)
+    row = iota((GROUP, tokens), 0)
+
+    def store(g):
+        rows = pl.ds(pl.multiple_of(g * GROUP, GROUP), GROUP)
+        return pltpu.make_async_copy(blocks.at[rows], out_hbm.at[rows], out_sem.at[g])
+
+    def pick(g, _):
+        named = slots_ref[pl.ds(pl.multiple_of(g * PER_GROUP, PER_GROUP), PER_GROUP), :]
+        hit = dot(spread, named.astype(BF16)) == (row % CAP).astype(F32)
+        parts = []
+        for p in range(pieces):
+            own = hit & ((row // CAP) % pieces == p)
+            parts.append(jnp.where(own, 1.0, 0.0).astype(BF16))
+        rows = pl.ds(pl.multiple_of(g * GROUP, GROUP), GROUP)
+        blocks[rows, :] = dot(jnp.concatenate(parts, axis=1), stack[...]).astype(BF16)
+        store(g).start()
+        return 0
+
+    lax.fori_loop(0, groups, pick, 0)
+
+    @pl.when(me >= 2)
+    def _():
+        near.wait_recv()
+
+        @pl.when(core == 0)
+        def _():
+            near_even.start()
+
+        @pl.when(core == 1)
+        def _():
+            near_odd.start()
+
+    @pl.when(me >= 4)
+    def _():
+        far.wait_recv()
+
+        @pl.when(core == 1)
+        def _():
+            far_odd.start()
+
+    @pl.when(core == 1)
+    def _():
+        beside.wait_recv()
+
+    @pl.when(core == 0)
+    def _():
+        beside.wait_send()
+
+    @pl.when(me >= 2)
+    def _():
+        near_even.wait_send()
+        near_even.wait_recv()
+
+    @pl.when((me >= 4) & (core == 1))
+    def _():
+        far_odd.wait_send()
+
+    @pl.when((me >= 4) & (core == 0))
+    def _():
+        far_odd.wait_recv()
+
+    @pl.when(me + 4 < count)
+    def _():
+        far.wait_send()
+
+    @pl.when(me + 2 < count)
+    def _():
+        near.wait_send()
+
     keep.wait()
-    for j in range(1, REACH + 1):
-
-        @pl.when(me >= j)
-        def _():
-            copy(j).wait_recv()
-
-        @pl.when(me + j < count)
-        def _():
-            copy(j).wait_send()
-
-
-def gather(own, count):
-    tokens, width = own.shape
+    for g in range(groups):
+        store(g).wait()
+
+
+def open_exchange(own, slots, rows, count):
+    experts, tokens = slots.shape
+    total = experts * BLOCK
+    piece = rows.shape[1] * CAP // BLOCK
     vmem = pl.BlockSpec(memory_space=pltpu.VMEM)
     return pl.pallas_call(
-        functools.partial(gather_kernel, count),
-        in_specs=[vmem],
-        out_specs=vmem,
-        out_shape=jax.ShapeDtypeStruct(((REACH + 1) * tokens, width), own.dtype),
+        functools.partial(open_kernel, count),
+        in_specs=[vmem] * 3,
+        out_specs=[vmem, pl.BlockSpec(memory_space=pl.ANY)],
+        out_shape=[
+            jax.ShapeDtypeStruct(((REACH + 1) * tokens, own.shape[1]), own.dtype),
+            jax.ShapeDtypeStruct((total, piece), BF16),
+        ],
         scratch_shapes=[
-            pltpu.SemaphoreType.DMA((REACH,)),
-            pltpu.SemaphoreType.DMA((REACH,)),
+            pltpu.VMEM((BLOCK // CAP * tokens, piece), BF16),
+            pltpu.VMEM((total, piece), BF16),
+            pltpu.SemaphoreType.DMA((5,)),
+            pltpu.SemaphoreType.DMA((5,)),
             pltpu.SemaphoreType.DMA,
+            pltpu.SemaphoreType.DMA((total // GROUP,)),
         ],
         compiler_params=pltpu.CompilerParams(
             collective_id=0, has_side_effects=True, vmem_limit_bytes=60 * MB
         ),
-        name="gather",
-    )(own)
-
-
-def scatter_kernel(count, kv_heads, *rest):
-    terms, (out_ref, landed, send_sem, recv_sem) = rest[:kv_heads], rest[kv_heads:]
-    tokens = out_ref.shape[0]
-    half = out_ref.shape[1] // 2
-    me = lax.axis_index("ctx")
-
-    def copy(j, m):
-        return pltpu.make_async_remote_copy(
-            src_ref=terms[m].at[pl.ds((REACH - j) * tokens, tokens)],
-            dst_ref=landed.at[j - 1, m],
-            send_sem=send_sem.at[j - 1, m],
-            recv_sem=recv_sem.at[j - 1, m],
-            device_id={"ctx": me - j},
-            device_id_type=MESH,
-        )
-
-    greet(me, count)
-    for j in range(REACH, 0, -1):
-
-        @pl.when(me >= j)
-        def _():
-            for m in range(kv_heads):
-                copy(j, m).start()
-
-    for j in range(1, REACH + 1):
-
-        @pl.when(me + j < count)
-        def _():
-            for m in range(kv_heads):
-                copy(j, m).wait_recv()
-
-        @pl.when(me + j >= count)
-        def _():
-            landed[j - 1] = jnp.zeros(landed.shape[1:], landed.dtype)
-
-        @pl.when(me >= j)
-        def _():
-            for m in range(kv_heads):
-                copy(j, m).wait_send()
-
-    for m in range(kv_heads):
-        total = terms[m][REACH * tokens :, :].astype(F32)
-        for j in range(REACH):
-            total = total + landed[j, m].astype(F32)
-        out_ref[:, m * HEAD : (m + 1) * HEAD] = total[:, :HEAD].astype(BF16)
-        out_ref[:, half + m * HEAD : half + (m + 1) * HEAD] = total[:, HEAD:].astype(BF16)
-
-
-def scatter(terms, tokens, count):
-    kv_heads = len(terms)
-    width = terms[0].shape[1]
-    vmem = pl.BlockSpec(memory_space=pltpu.VMEM)
-    return pl.pallas_call(
-        functools.partial(scatter_kernel, count, kv_heads),
-        in_specs=[vmem] * kv_heads,
-        out_specs=vmem,
-        out_shape=jax.ShapeDtypeStruct((tokens, kv_heads * width), BF16),
-        scratch_shapes=[
-            pltpu.VMEM((REACH, kv_heads, tokens, width), BF16),
-            pltpu.SemaphoreType.DMA((REACH, kv_heads)),
-            pltpu.SemaphoreType.DMA((REACH, kv_heads)),
-        ],
-        compiler_params=pltpu.CompilerParams(
-            collective_id=1, has_side_effects=True, vmem_limit_bytes=60 * MB
-        ),
-        name="scatter",
-    )(*terms)
+        name="open_exchange",
+    )(own, slots, rows)
 
 
 def visible(place_ref, window, tokens):
@@ -389,15 +410,82 @@
     )(place, query, keyval)
 
 
-def attend_back_kernel(
-    heads, query_ref, grad_ref, prob_ref, keys_ref, values_ref,
-    grad_query_ref, grad_keyval_ref, key_sum, value_sum,
+def finish_kernel(
+    heads, steps_per_kv, count, ep_count, query_ref, grad_ref, prob_ref, keys_ref, values_ref,
+    products_ref, grad_query_ref, grad_keyval_ref, returned_ref,
+    key_sum, value_sum, terms, landed, gathered, turned, arrived,
+    send_sem, recv_sem, ctx_send, ctx_recv, ep_send, ep_recv,
 ):
     step = pl.program_id(0)
+    last = pl.num_programs(0) - 1
     tokens = query_ref.shape[0]
+    half = grad_keyval_ref.shape[1] // 2
     scale = HEAD ** (-0.5)
+    me = lax.axis_index("ctx")
+    place = lax.axis_index("ep")
+    barrier = pltpu.get_barrier_semaphore()
+
+    def send_terms(j, m):
+        return pltpu.make_async_remote_copy(
+            src_ref=terms.at[m, pl.ds((REACH - j) * tokens, tokens)],
+            dst_ref=landed.at[j - 1, m],
+            send_sem=send_sem.at[j - 1, m],
+            recv_sem=recv_sem.at[j - 1, m],
+            device_id={"ctx": me - j},
+            device_id_type=MESH,
+        )
+
+    def along_ctx(d):
+        target = (me + d) % count
+        return pltpu.make_async_remote_copy(
+            src_ref=products_ref.at[target],
+            dst_ref=gathered.at[me],
+            send_sem=ctx_send.at[d - 1],
+            recv_sem=ctx_recv.at[d - 1],
+            device_id={"ctx": target},
+            device_id_type=MESH,
+        )
+
+    def along_ep(d):
+        target = (place + d) % ep_count
+        return pltpu.make_async_remote_copy(
+            src_ref=turned.at[target],
+            dst_ref=arrived.at[place],
+            send_sem=ep_send.at[d - 1],
+            recv_sem=ep_recv.at[d - 1],
+            device_id={"ep": target},
+            device_id_type=MESH,
+        )
 
     @pl.when(step == 0)
+    def _():
+        for d in range(1, count):
+            pl.semaphore_signal(
+                barrier, inc=1, device_id={"ctx": (me + d) % count}, device_id_type=MESH
+            )
+        for d in range(1, ep_count):
+            pl.semaphore_signal(
+                barrier, inc=1, device_id={"ep": (place + d) % ep_count}, device_id_type=MESH
+            )
+        gathered[me] = products_ref[me]
+
+    @pl.when(step == 1)
+    def _():
+        pl.semaphore_wait(barrier, count + ep_count - 2)
+        for d in range(1, count):
+            along_ctx(d).start()
+
+    @pl.when(step == steps_per_kv - 1)
+    def _():
+        for d in range(1, count):
+            along_ctx(d).wait_recv()
+        for c in range(count):
+            turned[:, c, :] = gathered[c]
+        arrived[place] = turned[place]
+        for d in range(1, ep_count):
+            along_ep(d).start()
+
+    @pl.when(step % steps_per_kv == 0)
     def _():
         key_sum[...] = jnp.zeros_like(key_sum)
         value_sum[...] = jnp.zeros_like(value_sum)
@@ -417,42 +505,102 @@
         key_sum[...] += dot(dscore, head_pair(query_ref, h))
         value_sum[...] += dot(prob, grad)
 
-    @pl.when(step == pl.num_programs(0) - 1)
-    def _():
-        grad_keyval_ref[:, :HEAD] = (key_sum[...] * scale).astype(BF16)
-        grad_keyval_ref[:, HEAD:] = value_sum[...].astype(BF16)
-
-
-def attend_back(m, query, grad, prob, keyval):
+    for m in range(landed.shape[1]):
+
+        @pl.when(step == (m + 1) * steps_per_kv - 1)
+        def _():
+            terms[m, :, :HEAD] = (key_sum[...] * scale).astype(BF16)
+            terms[m, :, HEAD:] = value_sum[...].astype(BF16)
+            for j in range(REACH, 0, -1):
+
+                @pl.when(me >= j)
+                def _():
+                    send_terms(j, m).start()
+
+    @pl.when(step == last)
+    def _():
+        for d in range(1, count):
+            along_ctx(d).wait_send()
+        for d in range(1, ep_count):
+            along_ep(d).wait_send()
+            along_ep(d).wait_recv()
+        returned_ref[...] = arrived[...]
+        for m in range(landed.shape[1]):
+            for j in range(1, REACH + 1):
+
+                @pl.when(me + j < count)
+                def _():
+                    send_terms(j, m).wait_recv()
+
+                @pl.when(me + j >= count)
+                def _():
+                    landed[j - 1, m] = jnp.zeros(landed.shape[2:], landed.dtype)
+
+            total = terms[m, REACH * tokens :, :].astype(F32)
+            for j in range(REACH):
+                total = total + landed[j, m].astype(F32)
+            grad_keyval_ref[:, m * HEAD : (m + 1) * HEAD] = total[:, :HEAD].astype(BF16)
+            grad_keyval_ref[:, half + m * HEAD : half + (m + 1) * HEAD] = total[:, HEAD:].astype(
+                BF16
+            )
+            for j in range(1, REACH + 1):
+
+                @pl.when(me >= j)
+                def _():
+                    send_terms(j, m).wait_send()
+
+
+def finish(query, grad, prob, keyval, products):
     tokens, width = query.shape
     window = keyval.shape[0]
+    count, ep_count, lanes = products.shape
     kv_heads = keyval.shape[1] // 2 // HEAD
     heads = prob.shape[2] // tokens
-    steps = prob.shape[0] // kv_heads
-    rows = pl.BlockSpec((tokens, heads * HEAD), lambda i: (0, m * steps + i))
+    steps = prob.shape[0]
+    steps_per_kv = steps // kv_heads
+    rows = pl.BlockSpec((tokens, heads * HEAD), lambda i: (0, i))
     return pl.pallas_call(
-        functools.partial(attend_back_kernel, heads),
+        functools.partial(finish_kernel, heads, steps_per_kv, count, ep_count),
         grid=(steps,),
         in_specs=[
             rows,
             rows,
-            pl.BlockSpec((1,) + prob.shape[1:], lambda i: (m * steps + i, 0, 0)),
-            pl.BlockSpec((window, HEAD), lambda i: (0, m)),
-            pl.BlockSpec((window, HEAD), lambda i: (0, kv_heads + m)),
+            pl.BlockSpec((1,) + prob.shape[1:], lambda i: (i, 0, 0)),
+            pl.BlockSpec((window, HEAD), lambda i: (0, i // steps_per_kv)),
+            pl.BlockSpec((window, HEAD), lambda i: (0, kv_heads + i // steps_per_kv)),
+            pl.BlockSpec(products.shape, lambda i: (0, 0, 0)),
         ],
         out_specs=[
-            pl.BlockSpec((tokens, heads * HEAD), lambda i: (0, i)),
-            pl.BlockSpec((window, 2 * HEAD), lambda i: (0, 0)),
+            rows,
+            pl.BlockSpec((tokens, keyval.shape[1]), lambda i: (0, 0)),
+            pl.BlockSpec((ep_count, count, lanes), lambda i: (0, 0, 0)),
         ],
         out_shape=[
-            jax.ShapeDtypeStruct((tokens, width // kv_heads), BF16),
-            jax.ShapeDtypeStruct((window, 2 * HEAD), BF16),
-        ],
-        scratch_shapes=[pltpu.VMEM((window, HEAD), F32), pltpu.VMEM((window, HEAD), F32)],
-        compiler_params=params(60),
-        cost_estimate=cost(4 * tokens * width * window, 5 * MB),
-        name="attend_back",
-    )(query, grad, prob, keyval, keyval)
+            jax.ShapeDtypeStruct((tokens, width), BF16),
+            jax.ShapeDtypeStruct((tokens, keyval.shape[1]), BF16),
+            jax.ShapeDtypeStruct((ep_count, count, lanes), F32),
+        ],
+        scratch_shapes=[
+            pltpu.VMEM((window, HEAD), F32),
+            pltpu.VMEM((window, HEAD), F32),
+            pltpu.VMEM((kv_heads, window, 2 * HEAD), BF16),
+            pltpu.VMEM((REACH, kv_heads, tokens, 2 * HEAD), BF16),
+            pltpu.VMEM((count, ep_count, lanes), F32),
+            pltpu.VMEM((ep_count, count, lanes), F32),
+            pltpu.VMEM((ep_count, count, lanes), F32),
+            pltpu.SemaphoreType.DMA((REACH, kv_heads)),
+            pltpu.SemaphoreType.DMA((REACH, kv_heads)),
+            pltpu.SemaphoreType.DMA((count - 1,)),
+            pltpu.SemaphoreType.DMA((count - 1,)),
+            pltpu.SemaphoreType.DMA((ep_count - 1,)),
+            pltpu.SemaphoreType.DMA((ep_count - 1,)),
+        ],
+        compiler_params=pltpu.CompilerParams(
+            collective_id=1, has_side_effects=True, vmem_limit_bytes=60 * MB
+        ),
+        cost_estimate=cost(8 * tokens * width * window, 10 * MB),
+        name="finish",
+    )(query, grad, prob, keyval, keyval, products)
 
 
 def combine_terms(half, halves, tokens, slots_ref, gates_ref, blocks_ref):
@@ -487,18 +635,30 @@
 
 
 def combine_last_kernel(
-    halves, slots_ref, gates_ref, blocks_ref, first_ref, gain_ref, grad_out_ref, hidden_ref,
-    rinv_ref, grad_ref, acc,
+    halves, slots_ref, gates_ref, blocks_ref, gain_ref, rinv_ref, first_hbm, grad_out_hbm,
+    hidden_hbm, grad_ref, acc, first_ref, grad_out_ref, hidden_ref, sem,
 ):
     step = pl.program_id(0)
     tokens, width = hidden_ref.shape
+    loads = [
+        pltpu.make_async_copy(source, target, sem.at[i])
+        for i, (source, target) in enumerate(
+            [(first_hbm, first_ref), (grad_out_hbm, grad_out_ref), (hidden_hbm, hidden_ref)]
+        )
+    ]
+
+    @pl.when(step == 0)
+    def _():
+        for load in loads:
+            load.start()
+
     pieces = acc.shape[0] // tokens
     piece = width // pieces
     part = combine_terms(halves - 1, halves, tokens, slots_ref, gates_ref, blocks_ref)
 
     @pl.when(step == 0)
     def _():
-        acc[...] = first_ref[...] + part
+        acc[...] = part
 
     @pl.when(step != 0)
     def _():
@@ -506,12 +666,14 @@
 
     @pl.when(step == pl.num_programs(0) - 1)
     def _():
+        for load in loads:
+            load.wait()
         rinv = rinv_ref[...]
         mean = jnp.zeros((tokens, 1), F32)
         for p in range(pieces):
             cols = slice(p * piece, (p + 1) * piece)
             rows = slice(p * tokens, (p + 1) * tokens)
-            scaled = acc[rows, :] * gain_ref[:, cols]
+            scaled = (acc[rows, :] + first_ref[rows, :]) * gain_ref[:, cols]
             acc[rows, :] = scaled
             mean = mean + jnp.sum(hidden_ref[:, cols].astype(F32) * scaled, axis=1, keepdims=True)
         mean = mean / width * (rinv * rinv * rinv)
@@ -560,19 +722,23 @@
             whole(slots.shape),
             whole(gates.shape),
             pl.BlockSpec((rows, piece), lambda i: (i, 0)),
-            whole(first.shape),
             whole(gain.shape),
-            whole(grad_out.shape),
-            whole(hidden.shape),
             whole(rinv.shape),
-        ],
+        ]
+        + [pl.BlockSpec(memory_space=pl.ANY)] * 3,
         out_specs=whole((tokens, width)),
         out_shape=jax.ShapeDtypeStruct((tokens, width), BF16),
-        scratch_shapes=[pltpu.VMEM(first.shape, F32)],
+        scratch_shapes=[
+            pltpu.VMEM(first.shape, F32),
+            pltpu.VMEM(first.shape, F32),
+            pltpu.VMEM(grad_out.shape, BF16),
+            pltpu.VMEM(hidden.shape, BF16),
+            pltpu.SemaphoreType.DMA((3,)),
+        ],
         compiler_params=params(60),
         cost_estimate=cost(2 * total * tokens * width, 8 * MB),
         name="combine_last",
-    )(slots, gates, blocks, first, gain, grad_out, hidden, rinv)
+    )(slots, gates, blocks, gain, rinv, first, grad_out, hidden)
 
 
 def expert_kernel(
@@ -734,7 +900,7 @@
 
 
 def expert_grads_kernel(
-    halves, cotangent_ref, grad_ref, base_ref, high_ref, units_ref, low_out_ref, back_low_ref,
+    halves, cotangent_ref, scale_ref, base_ref, high_ref, units_ref, low_out_ref, back_low_ref,
     *rest
 ):
     inputs = rest[:halves]
@@ -769,11 +935,12 @@
         low_in = low_in + dot(back_t[h], inputs[h][...])
     mag_ref[...] = mag
     low_in_ref[...] = low_in
-    high_grad_ref[...] = dot(low_down_t[...], grad_ref[...])
+    grad = (cotangent_ref[...].astype(F32) * scale_ref[...]).astype(BF16)
+    high_grad_ref[...] = dot(low_down_t[...], grad)
 
 
 def expert_grads(
-    cotangent, grad_linear, base, high, units, low_out, back_low, inputs, low_acts, grad_linears,
+    cotangent, scale, base, high, units, low_out, back_low, inputs, low_acts, grad_linears,
     backs,
 ):
     halves = len(inputs)
@@ -786,7 +953,7 @@
     return pl.pallas_call(
         functools.partial(expert_grads_kernel, halves),
         grid=(width // tile,),
-        in_specs=[part(count), part(count), part(ffw), part(rank)]
+        in_specs=[part(count), part(1), part(ffw), part(rank)]
         + [whole(array) for array in fixed]
         + [part(count // halves)] * halves
         + [whole(array) for array in low_acts + grad_linears + backs],
@@ -812,7 +979,7 @@
         compiler_params=params(60),
         cost_estimate=cost(1, 1),
         name="expert_grads",
-    )(cotangent, grad_linear, base, high, *fixed, *inputs, *low_acts, *grad_linears, *backs)
+    )(cotangent, scale, base, high, *fixed, *inputs, *low_acts, *grad_linears, *backs)
 
 
 def square_norm(base, low, high):
@@ -850,7 +1017,7 @@
     before = dot(named.astype(BF16), earlier.astype(BF16))
     slots = jnp.where(named, before, -1.0)
 
-    seen = gather(local_kv, ctx_count)
+    seen, outgoing_grad = open_exchange(local_kv, slots, grad_out, ctx_count)
     first = lax.axis_index("ctx") * tokens
     place = jnp.concatenate(
         [
@@ -859,8 +1026,6 @@
         ]
     )
 
-    outgoing_grad, _ = dispatch(slots, grad_out, gain, False, 1)
-    outgoing_grad, seen = lax.optimization_barrier((outgoing_grad, seen))
     arrived_grad = exchange(outgoing_grad)
 
     prob, hidden = attend(place, query, seen)
@@ -895,7 +1060,7 @@
     inputs, units, low_acts, grad_linears, backs, products, mag_sums = zip(*results)
 
     mag_sum, grad_high_out, low_in_t, low_out_t, grad_high_in = expert_grads(
-        cotangent, grad_linear_out, base_out, high_out, jnp.concatenate(units, axis=0), low_out,
+        cotangent, scale_out[None, :], base_out, high_out, jnp.concatenate(units, axis=0), low_out,
         back_low, inputs, low_acts, grad_linears, backs,
     )
     grad_mag_out = mag_sum[0] / norm_out
@@ -903,8 +1068,9 @@
     grad_low_in = low_in_t.reshape(2, -1, width).transpose(0, 2, 1)
     grad_mag_in = sum(mag_sums) / norm_in
     products = jnp.concatenate(
-        [part.astype(BF16).reshape(experts, slots_each) for part in products], axis=1
-    )
+        [part.astype(BF16).astype(F32).reshape(experts, slots_each) for part in products], axis=1
+    )
+    products = jnp.pad(products, ((0, 0), (0, HEAD - CAP))).reshape(ctx_count, -1, HEAD)
 
     logits = router_logits[0]
     gate_expo = jnp.exp(logits - jnp.max(logits, axis=-1, keepdims=True))
@@ -918,25 +1084,18 @@
     grad_heads = combine_last(
         token_slots, dense_gates, returned[1], partial, gain, grad_out, hidden, rinv, halves
     )
-    products, grad_heads = lax.optimization_barrier((products, grad_heads))
-    returned_products = lax.all_to_all(products, axes, split_axis=0, concat_axis=0, tiled=True)
+    grad_query, grad_keyval, arrived_products = finish(query, grad_heads, prob, seen, products)
+    returned_products = arrived_products.transpose(1, 0, 2).reshape(experts, HEAD)
     dense_products = jnp.zeros((tokens, experts), F32)
     for r in range(CAP):
         dense_products = dense_products + jnp.where(
-            token_slots == r, returned_products[:, r].astype(F32)[None, :], 0.0
+            token_slots == r, returned_products[:, r][None, :], 0.0
         )
     grad_gate = jnp.stack(
         [jnp.sum(jnp.where(chosen[k], dense_products, 0.0), axis=1) for k in range(top)], axis=1
     )
     grad_logits = gates * (grad_gate - jnp.sum(gates * grad_gate, axis=-1, keepdims=True))
 
-    queries, terms = [], []
-    for m in range(local_kv.shape[1] // 2 // HEAD):
-        query_part, term = attend_back(m, query, grad_heads, prob, seen)
-        queries.append(query_part)
-        terms.append(term)
-    grad_keyval = scatter(terms, tokens, ctx_count)
-    grad_query = jnp.concatenate(queries, axis=1)
     return (
         grad_query[None],
         grad_keyval[None],

time: 289 us -> 258 us (0.89)
  Pallas kernels: 160 us -> 139 us
  starting transfers between devices: 42.3 us -> 34.6 us
  other arithmetic: 20.3 us -> 12.7 us
  waiting for transfers between devices: 36.3 us -> 40.8 us
  local copies, waits for them, and re-layouts: 7.48 us -> 10.8 us
    pallas_call x4 -> x2, Pallas kernels: 45.9 us -> 34 us  [the longest x1 21.9 us: finish(): pl.pallas_call(functools.partial(finish_kernel, heads, steps_per_kv, coun...]
    all_to_all x1 -> x0, starting transfers between devices: 9.9 us -> none  [shards(): lax.all_to_all(products, axes, split_axis=0, concat_axis=0, tiled=True)]
    pallas_call x2 -> x1, Pallas kernels: 16.6 us -> 9.19 us  [dispatch(): pl.pallas_call(functools.partial(dispatch_kernel, with_norm), grid=(total...]
    convert_element_type x2 -> x1, other arithmetic: 8.92 us -> 3.54 us  [shards(): grad_linear_out = (cotangent.astype(F32) * scale_out).astype(BF16)]
    all_to_all x5, waiting for transfers between devices: 36.3 us -> 40.8 us  [exchange(): moved = lax.all_to_all(split, axes, split_axis=0, concat_axis=0, tiled=True)]
    unnamed x52 -> x53, local copies, waits for them, and re-layouts: 4.72 us -> 6.99 us
  transfers between devices with their start and end apart: 6 -> 5, of which waited for: 4 -> 5; matrix products, arithmetic and copies ran while one was open for 13% -> 12% of each run, Pallas kernels for 39% -> 38%
where the time goes in v1:
time: 258 us; the launch traced here: 256 us
  Pallas kernels  139 us (54%)
  waiting for transfers between devices  40.8 us (16%)
  starting transfers between devices  34.6 us (13%)
  matrix products  16.8 us (7%)
  other arithmetic  12.7 us (5%)
  local copies, waits for them, and re-layouts  10.8 us (4%)
    pallas_call x2, Pallas kernels, expert(): pl.pallas_call(functools.partial(expert_kernel, slots), in_specs=[hbm, hb...  47.4 us
    all_to_all x5, waiting for transfers between devices, exchange(): moved = lax.all_to_all(split, axes, split_axis=0, concat_axis=0, tiled=True)  40.8 us
    all_to_all x5, starting transfers between devices, exchange(): moved = lax.all_to_all(split, axes, split_axis=0, concat_axis=0, tiled=True)  34.6 us
    pallas_call x1, Pallas kernels, finish(): pl.pallas_call(functools.partial(finish_kernel, heads, steps_per_kv, coun...  21.9 us
    pallas_call x1, Pallas kernels, attend(): pl.pallas_call(functools.partial(attend_kernel, heads, per_kv), grid=(ste...  13.7 us
    pallas_call x1, Pallas kernels, expert_grads(): pl.pallas_call(functools.partial(expert_grads_kernel, halves), grid=(widt...  13.1 us
    pallas_call x1, Pallas kernels, open_exchange(): pl.pallas_call(functools.partial(open_kernel, count), in_specs=[vmem] * 3...  12.1 us
    dot_general x4, matrix products, dot(): return jnp.dot(left, right, preferred_element_type=F32)  11.6 us
  transfers between devices with their start and end apart: 5, of which 5 were waited for; matrix products, arithmetic and copies ran while one was open for 12% of the time, Pallas kernels for 38%

profile of v1, /device:TPU:1, one launch (start us, length us, event | category | flops | bytes accessed | tf_op | source)
XLA Modules:
  0.0 256.3 jit_solution(11263290593248908365)
XLA Ops:
  4.5 12.1 %open_exchange.1 = (bf16[640,512]{1,0:T(8,128)(2,1)}, bf16[2048,1024]{1,0:T(8,128)(2,1)}) custom-call(bf16[128,512]{1,0:T(8,128)(2,1)} %bitcast.140, f32[128,128]{1,0:T(8,128)} %get-tuple-element.162.slots_ref, bf16[128,4096]{1,0:T(8,128)(2,1)} %bitcast.132), custom_call_target="tpu_custom_call" | custom-call | tf_op jit(solution)/shard_map/open_exchange/pallas_call | solution.py:311
  16.6 12.4 %all-to-all-start = ((bf16[128,16,1024]{2,1,0:T(8,128)(2,1)}), bf16[128,16,1024]{2,1,0:T(8,128)(2,1)}, u32[]{:S(2)}, u32[]{:S(2)}) async-start(bf16[128,16,1024]{2,1,0:T(8,128)(2,1)} %bitcast.124), calls=%async_computation | async-start | bytes 8388608 | tf_op jit(solution)/shard_map/all_to_all | solution.py:1009
  29.0 4.8 %multiply_reduce_fusion = f32[4096]{0:T(1024)S(1)} fusion(bf16[1,768,32]{1,2,0:T(8,128)(2,1)S(1)} %copy-done.7, bf16[1,32,4096]{2,1,0:T(8,128)(2,1)S(1)} %copy-done.6, bf16[1,768,4096]{2,1,0:T(8,128)(2,1)} %param.26), kind=kOutput, calls=%fused_computation.6 | convolution fusion | flops 213905408 | bytes 6619136 | tf_op jit(solution)/shard_map/dot_general | solution.py:37
  33.9 4.3 %fusion.1 = f32[768]{0:T(1024)S(1)} fusion(bf16[1,2,4096,768]{3,2,1,0:T(8,128)(2,1)} %param.22, bf16[1,2,32,768]{3,2,1,0:T(8,128)(2,1)S(1)} %copy-done.16, bf16[1,2,4096,32]{2,3,1,0:T(8,128)(2,1)S(1)} %copy-done.3), kind=kOutput, calls=%fused_computation.2 | convolution fusion | flops 213908736 | bytes 6605824 | tf_op jit(solution)/shard_map/dot_general | solution.py:37
  42.5 13.7 %attend.1 = (bf16[8,640,512]{2,1,0:T(8,128)(2,1)}, bf16[128,4096]{1,0:T(8,128)(2,1)}) custom-call(s32[6]{0:T(128)} %pad_add_fusion.place_ref, bf16[128,4096]{1,0:T(8,128)(2,1)} %bitcast.156, bf16[640,512]{1,0:T(8,128)(2,1)} %get-tuple-element.59.keyval_ref.keys_ref.values_ref), custom_call_target="tpu_custom_call" | custom-call | flops 1342177280 | bytes 9437184 | tf_op jit(solution)/shard_map/attend/pallas_call | solution.py:390
  56.8 9.2 %dispatch.1 = (bf16[2048,512]{1,0:T(8,128)(2,1)}, bf16[2048,512]{1,0:T(8,128)(2,1)}, f32[128,1]{1,0:T(8,128)}) custom-call(f32[128,128]{1,0:T(8,128)} %get-tuple-element.162.slots_ref, bf16[128,4096]{1,0:T(8,128)(2,1)} %get-tuple-element.60.rows_ref.hidden_hbm, f32[1,4096]{1,0:T(1,128)} %bitcast.164), custom_call_target="tpu_custom_call" | custom-call | flops 4294967296 | bytes 10485760 | tf_op jit(solution)/shard_map/dispatch/pallas_call | solution.py:111
  67.6 12.9 %all-to-all-done = bf16[128,16,1024]{2,1,0:T(8,128)(2,1)} async-done(((bf16[128,16,1024]{2,1,0:T(8,128)(2,1)}), bf16[128,16,1024]{2,1,0:T(8,128)(2,1)}, u32[]{:S(2)}, u32[]{:S(2)}) %all-to-all-start) | async-done | bytes 4194336 | tf_op jit(solution)/shard_map/all_to_all | solution.py:1009
  80.5 5.5 %all-to-all-start.1 = ((bf16[128,16,512]{2,1,0:T(8,128)(2,1)}), bf16[128,16,512]{2,1,0:T(8,128)(2,1)}, u32[]{:S(2)}, u32[]{:S(2)}) async-start(bf16[128,16,512]{2,1,0:T(8,128)(2,1)} %bitcast.130), calls=%async_computation.1 | async-start | bytes 4194304 | tf_op jit(solution)/shard_map/all_to_all | solution.py:1009
  86.0 7.7 %unpack.1 = bf16[2,256,4096]{2,1,0:T(8,128)(2,1)} custom-call(bf16[2048,1024]{1,0:T(8,128)(2,1)} %bitcast.16.blocks_ref), custom_call_target="tpu_custom_call" | custom-call | flops 1073741824 | bytes 8388608 | tf_op jit(solution)/shard_map/unpack/pallas_call | solution.py:145
  93.8 3.5 %multiply_convert_fusion = bf16[2,256,4096]{2,1,0:T(8,128)(2,1)S(1)} fusion(bf16[2,256,4096]{2,1,0:T(8,128)(2,1)} %unpack.1, f32[4096]{0:T(1024)S(1)} %bitcast.137), kind=kLoop, calls=%fused_computation.7 | loop fusion | flops 6291456 | bytes 8404992 | tf_op jit(solution)/shard_map/convert_element_type | solution.py:1039
  98.6 3.6 %fusion.31 = f32[512,768]{1,0:T(8,128)S(1)} fusion(bf16[512,4096]{1,0:T(8,128)(2,1)S(1)} %bitcast.126, bf16[1,768,4096]{2,1,0:T(8,128)(2,1)S(1)} %bitcast.121), kind=kOutput, calls=%fused_computation.75 | convolution fusion | flops 3221225472 | bytes 12058624 | tf_op jit(solution)/shard_map/dot_general | solution.py:41
  102.6 12.8 %all-to-all-done.1 = bf16[128,16,512]{2,1,0:T(8,128)(2,1)} async-done(((bf16[128,16,512]{2,1,0:T(8,128)(2,1)}), bf16[128,16,512]{2,1,0:T(8,128)(2,1)}, u32[]{:S(2)}, u32[]{:S(2)}) %all-to-all-start.1) | async-done | bytes 2097184 | tf_op jit(solution)/shard_map/all_to_all | solution.py:1009
  115.4 5.6 %all-to-all-start.2 = ((bf16[128,16,512]{2,1,0:T(8,128)(2,1)}), bf16[128,16,512]{2,1,0:T(8,128)(2,1)}, u32[]{:S(2)}, u32[]{:S(2)}) async-start(bf16[128,16,512]{2,1,0:T(8,128)(2,1)} %bitcast.128), calls=%async_computation.2 | async-start | bytes 4194304 | tf_op jit(solution)/shard_map/all_to_all | solution.py:1009
  122.2 23.7 %expert.3 = (bf16[2048,512]{1,0:T(8,128)(2,1)}, bf16[256,4096]{1,0:T(8,128)(2,1)}, bf16[256,768]{1,0:T(8,128)(2,1)}, bf16[256,64]{1,0:T(8,128)(2,1)}, bf16[2,256...) custom-call(bf16[2048,512]{1,0:T(8,128)(2,1)} %bitcast.31.blocks_hbm, ...), custom_call_target="tpu_custom_call" | custom-call | flops 6442450944 | bytes 31457280 | tf_op jit(solution)/shard_map/expert/pallas_call | solution.py:871
  145.9 4.5 %all-to-all-done.2 = bf16[128,16,512]{2,1,0:T(8,128)(2,1)} async-done(((bf16[128,16,512]{2,1,0:T(8,128)(2,1)}), bf16[128,16,512]{2,1,0:T(8,128)(2,1)}, u32[]{:S(2)}, u32[]{:S(2)}) %all-to-all-start.2) | async-done | bytes 2097184 | tf_op jit(solution)/shard_map/all_to_all | solution.py:1009
  150.4 5.4 %all-to-all-start.4 = ((bf16[128,16,512]{2,1,0:T(8,128)(2,1)}), bf16[128,16,512]{2,1,0:T(8,128)(2,1)S(1)}, u32[]{:S(2)}, u32[]{:S(2)}) async-start(bf16[128,16,512]{2,1,0:T(8,128)(2,1)} %bitcast.129), calls=%async_computation.4 | async-start | bytes 4194304 | tf_op jit(solution)/shard_map/all_to_all | solution.py:1009
  155.9 23.7 %expert.2 = (bf16[2048,512]{1,0:T(8,128)(2,1)}, bf16[256,4096]{1,0:T(8,128)(2,1)}, bf16[256,768]{1,0:T(8,128)(2,1)}, bf16[256,64]{1,0:T(8,128)(2,1)}, bf16[2,256...) custom-call(bf16[2048,512]{1,0:T(8,128)(2,1)} %bitcast.33.blocks_hbm, ...), custom_call_target="tpu_custom_call" | custom-call | flops 6442450944 | bytes 31457280 | tf_op jit(solution)/shard_map/expert/pallas_call | solution.py:871
  179.5 6.0 %all-to-all-done.4 = bf16[128,16,512]{2,1,0:T(8,128)(2,1)S(1)} async-done(((bf16[128,16,512]{2,1,0:T(8,128)(2,1)}), bf16[128,16,512]{2,1,0:T(8,128)(2,1)S(1)}, u32[]{:S(2)}, u32[]{:S(2)}) %all-to-all-start.4) | async-done | bytes 2097184 | tf_op jit(solution)/shard_map/all_to_all | solution.py:1009
  185.6 5.8 %all-to-all-start.3 = ((bf16[128,16,512]{2,1,0:T(8,128)(2,1)}), bf16[128,16,512]{2,1,0:T(8,128)(2,1)}, u32[]{:S(2)}, u32[]{:S(2)}) async-start(bf16[128,16,512]{2,1,0:T(8,128)(2,1)} %bitcast.127), calls=%async_computation.3 | async-start | bytes 4194304 | tf_op jit(solution)/shard_map/all_to_all | solution.py:1009
  192.2 6.6 %combine_first.1.first_hbm = f32[1024,512]{1,0:T(8,128)} custom-call(f32[128,128]{1,0:T(8,128)} %get-tuple-element.164.slots_ref, f32[128,128]{1,0:T(8,128)} %get-tuple-element.163.gates_ref, bf16[2048,512]{1,0:T(8,128)(2,1)} %bitcast.118), custom_call_target="tpu_custom_call" | custom-call | flops 1 | bytes 1 | tf_op jit(solution)/shard_map/combine_first/pallas_call | solution.py:697
  199.7 13.1 %expert_grads.1 = (f32[1,4096]{1,0:T(1,128)}, f32[32,4096]{1,0:T(8,128)}, f32[64,4096]{1,0:T(8,128)}, f32[32,768]{1,0:T(8,128)}, f32[2,32,768]{2,1,0:T(8,128)}) custom-call(bf16[512,4096]{1,0:T(8,128)(2,1)} %bitcast.117, f32[1,4096]{1,0:T(1,128)} %copy-done.8, bf16[768,4096]{1,0:T(8,128)(2,1)} %bitcast.119, bf16[32,4096]{1,0:T(8,128)(2,1)} %bitcast.136, ...), custom_call_target="tpu_custom_call" | custom-call | flops 1 | bytes 1 | tf_op jit(solution)/shard_map/expert_grads/pallas_call | solution.py:953
  216.3 4.6 %all-to-all-done.3 = bf16[128,16,512]{2,1,0:T(8,128)(2,1)} async-done(((bf16[128,16,512]{2,1,0:T(8,128)(2,1)}), bf16[128,16,512]{2,1,0:T(8,128)(2,1)}, u32[]{:S(2)}, u32[]{:S(2)}) %all-to-all-start.3) | async-done | bytes 2097184 | tf_op jit(solution)/shard_map/all_to_all | solution.py:1009
  220.8 7.7 %combine_last.1.grad_ref = bf16[128,4096]{1,0:T(8,128)(2,1)} custom-call(f32[128,128]{1,0:T(8,128)} %get-tuple-element.164.slots_ref, f32[128,128]{1,0:T(8,128)} %get-tuple-element.163.gates_ref, bf16[2048,512]{1,0:T(8,128)(2,1)} %bitcast.37.blocks_ref, f32[1,4096]{1,0:T(1,128)} %bitcast.165, f32[128,1]{1,0:T(8,128)} %get-tuple-element.69.rinv_ref, ...), custom_call_target="tpu_custom_call" | custom-call | flops 2147483648 | bytes 8388608 | tf_op jit(solution)/shard_map/combine_last/pallas_call | solution.py:718
  228.5 21.9 %finish.1 = (bf16[128,4096]{1,0:T(8,128)(2,1)}, bf16[128,512]{1,0:T(8,128)(2,1)}, f32[16,8,128]{2,1,0:T(8,128)}) custom-call(bf16[128,4096]{1,0:T(8,128)(2,1)} %bitcast.157, bf16[128,4096]{1,0:T(8,128)(2,1)} %combine_last.1.grad_ref, bf16[8,640,512]{2,1,0:T(8,128)(2,1)} %get-tuple-element.86.prob_ref, ...), custom_call_target="tpu_custom_call" | custom-call | flops 2684354560 | bytes 10485760 | tf_op jit(solution)/shard_map/finish/pallas_call | solution.py:562
  (93 shorter events, 24.0 us)
Async XLA Ops:
  16.6 12.4 %copy-start.6 = (bf16[1,32,4096]{2,1,0:T(8,128)(2,1)S(1)}, bf16[1,32,4096]{2,1,0:T(8,128)(2,1)}, u32[]{:S(2)}) copy-start(bf16[1,32,4096]{2,1,0:T(8,128)(2,1)} %param.28) | copy-start | bytes 786436
  16.6 12.4 %copy-start.7 = (bf16[1,768,32]{1,2,0:T(8,128)(2,1)S(1)}, bf16[1,768,32]{1,2,0:T(8,128)(2,1)}, u32[]{:S(2)}) copy-start(bf16[1,768,32]{1,2,0:T(8,128)(2,1)} %param.27) | copy-start | bytes 147460
  16.6 63.9 %all-to-all-start = ((bf16[128,16,1024]{2,1,0:T(8,128)(2,1)}), bf16[128,16,1024]{2,1,0:T(8,128)(2,1)}, u32[]{:S(2)}, u32[]{:S(2)}) async-start(bf16[128,16,1024]{2,1,0:T(8,128)(2,1)} %bitcast.124), calls=%async_computation | async-start | bytes 8388608 | tf_op jit(solution)/shard_map/all_to_all | solution.py:1009
  29.0 4.9 %copy-start.3 = (bf16[1,2,4096,32]{2,3,1,0:T(8,128)(2,1)S(1)}, bf16[1,2,4096,32]{2,3,1,0:T(8,128)(2,1)}, u32[]{:S(2)}) copy-start(bf16[1,2,4096,32]{2,3,1,0:T(8,128)(2,1)} %param.23) | copy-start | bytes 1572868
  29.0 4.9 %copy-start.16 = (bf16[1,2,32,768]{3,2,1,0:T(8,128)(2,1)S(1)}, bf16[1,2,32,768]{3,2,1,0:T(8,128)(2,1)}, u32[]{:S(2)}) copy-start(bf16[1,2,32,768]{3,2,1,0:T(8,128)(2,1)} %param.24) | copy-start | bytes 294916
  29.0 9.2 %slice-start.2 = ((s8[12582912]{0:T(1024)(128)(4,1)}), s8[4194304]{0:T(1024)(128)(4,1)S(1)}, s32[]{:S(2)}) async-start(s8[12582912]{0:T(1024)(128)(4,1)} %bitcast.154), calls=%async_computation.7 | async-start | bytes 8388608
  29.0 9.2 %slice-start.3 = ((s8[12582912]{0:T(1024)(128)(4,1)}), s8[4194304]{0:T(1024)(128)(4,1)S(1)}, s32[]{:S(2)}) async-start(s8[12582912]{0:T(1024)(128)(4,1)} %bitcast.154), calls=%async_computation.8 | async-start | bytes 8388608
  40.6 15.6 %copy-start.13 = (f32[1,2,768]{2,1,0:T(2,128)S(1)}, f32[1,2,768]{2,1,0:T(2,128)}, u32[]{:S(2)}) copy-start(f32[1,2,768]{2,1,0:T(2,128)} %param.25) | copy-start | bytes 18436
  41.9 51.9 %copy-start.8 = (f32[1,4096]{1,0:T(1,128)}, f32[1,4096]{1,0:T(1,128)S(1)}, u32[]{:S(2)}) copy-start(f32[1,4096]{1,0:T(1,128)S(1)} %div.29.scale_ref) | copy-start | bytes 49156
  80.5 34.9 %all-to-all-start.1 = ((bf16[128,16,512]{2,1,0:T(8,128)(2,1)}), bf16[128,16,512]{2,1,0:T(8,128)(2,1)}, u32[]{:S(2)}, u32[]{:S(2)}) async-start(bf16[128,16,512]{2,1,0:T(8,128)(2,1)} %bitcast.130), calls=%async_computation.1 | async-start | bytes 4194304 | tf_op jit(solution)/shard_map/all_to_all | solution.py:1009
  86.0 12.5 %slice-start = ((s8[6291456]{0:T(1024)(128)(4,1)}), s8[2097152]{0:T(1024)(128)(4,1)S(1)}, s32[]{:S(2)}) async-start(s8[6291456]{0:T(1024)(128)(4,1)} %bitcast.120), calls=%async_computation.5 | async-start | bytes 4194304
  93.8 4.8 %slice-start.1 = ((s8[6291456]{0:T(1024)(128)(4,1)}), s8[4194304]{0:T(1024)(128)(4,1)S(1)}, s32[]{:S(2)}) async-start(s8[6291456]{0:T(1024)(128)(4,1)} %bitcast.120), calls=%async_computation.6 | async-start | bytes 8388608
  115.4 35.1 %all-to-all-start.2 = ((bf16[128,16,512]{2,1,0:T(8,128)(2,1)}), bf16[128,16,512]{2,1,0:T(8,128)(2,1)}, u32[]{:S(2)}, u32[]{:S(2)}) async-start(bf16[128,16,512]{2,1,0:T(8,128)(2,1)} %bitcast.128), calls=%async_computation.2 | async-start | bytes 4194304 | tf_op jit(solution)/shard_map/all_to_all | solution.py:1009
  150.4 35.1 %all-to-all-start.4 = ((bf16[128,16,512]{2,1,0:T(8,128)(2,1)}), bf16[128,16,512]{2,1,0:T(8,128)(2,1)S(1)}, u32[]{:S(2)}, u32[]{:S(2)}) async-start(bf16[128,16,512]{2,1,0:T(8,128)(2,1)} %bitcast.129), calls=%async_computation.4 | async-start | bytes 4194304 | tf_op jit(solution)/shard_map/all_to_all | solution.py:1009
  185.6 6.6 %copy-start = (bf16[128,16,512]{2,1,0:T(8,128)(2,1)}, bf16[128,16,512]{2,1,0:T(8,128)(2,1)S(1)}, u32[]{:S(2)}) copy-start(bf16[128,16,512]{2,1,0:T(8,128)(2,1)S(1)} %all-to-all-done.4) | copy-start | bytes 6291460
  185.6 13.2 %copy-start.4 = (bf16[256,768]{1,0:T(8,128)(2,1)S(1)}, bf16[256,768]{1,0:T(8,128)(2,1)}, u32[]{:S(2)}) copy-start(bf16[256,768]{1,0:T(8,128)(2,1)} %get-tuple-element.92) | copy-start | bytes 1179652
  185.6 13.2 %copy-start.5 = (bf16[256,768]{1,0:T(8,128)(2,1)S(1)}, bf16[256,768]{1,0:T(8,128)(2,1)}, u32[]{:S(2)}) copy-start(bf16[256,768]{1,0:T(8,128)(2,1)} %get-tuple-element.93) | copy-start | bytes 1179652
  185.6 35.3 %all-to-all-start.3 = ((bf16[128,16,512]{2,1,0:T(8,128)(2,1)}), bf16[128,16,512]{2,1,0:T(8,128)(2,1)}, u32[]{:S(2)}, u32[]{:S(2)}) async-start(bf16[128,16,512]{2,1,0:T(8,128)(2,1)} %bitcast.127), calls=%async_computation.3 | async-start | bytes 4194304 | tf_op jit(solution)/shard_map/all_to_all | solution.py:1009
  199.7 13.1 %copy-start.9 = (f32[256,1]{1,0:T(8,128)S(1)}, f32[256,1]{1,0:T(8,128)}, u32[]{:S(2)}) copy-start(f32[256,1]{1,0:T(8,128)} %get-tuple-element.87) | copy-start | bytes 3076
  199.7 13.2 %copy-start.10 = (f32[256,1]{1,0:T(8,128)S(1)}, f32[256,1]{1,0:T(8,128)}, u32[]{:S(2)}) copy-start(f32[256,1]{1,0:T(8,128)} %get-tuple-element.88) | copy-start | bytes 3076
  199.7 15.9 %copy-start.14 = (f32[2,768]{1,0:T(2,128)S(1)}, f32[2,768]{1,0:T(2,128)}, u32[]{:S(2)}) copy-start(f32[2,768]{1,0:T(2,128)} %get-tuple-element.104) | copy-start | bytes 18436
  199.7 15.9 %copy-start.15 = (f32[2,768]{1,0:T(2,128)S(1)}, f32[2,768]{1,0:T(2,128)}, u32[]{:S(2)}) copy-start(f32[2,768]{1,0:T(2,128)} %get-tuple-element.105) | copy-start | bytes 18436
  228.5 23.1 %copy-start.1 = (f32[128,128]{1,0:T(8,128)S(1)}, f32[128,128]{1,0:T(8,128)}, u32[]{:S(2)}) copy-start(f32[128,128]{1,0:T(8,128)} %get-tuple-element.164.slots_ref) | copy-start | bytes 196612
  228.5 23.3 %copy-start.11 = (f32[1,128,3]{1,0,2:T(1,128)S(1)}, f32[1,128,3]{1,0,2:T(1,128)}, u32[]{:S(2)}) copy-start(f32[1,128,3]{1,0,2:T(1,128)} %param.19) | copy-start | bytes 4612
  (4 other events, 15.0 us)

commit v2 on v1

--- a/solution.py
+++ b/solution.py
@@ -343,6 +343,10 @@
     return (kpos >= 0) & (kpos <= qpos) & (kdoc == qdoc)
 
 
+def stack_heads(ref, heads):
+    return jnp.concatenate([ref[:, h * HEAD : (h + 1) * HEAD] for h in range(heads)], axis=0)
+
+
 def head_pair(ref, h):
     return jnp.concatenate(
         [ref[:, h * HEAD : (h + 1) * HEAD], ref[:, (h + 1) * HEAD : (h + 2) * HEAD]], axis=0
@@ -385,7 +389,7 @@
     window = keyval.shape[0]
     kv_heads = keyval.shape[1] // 2 // HEAD
     per_kv = width // HEAD // kv_heads
-    heads = 4
+    heads = 8
     steps = width // HEAD // heads
     return pl.pallas_call(
         functools.partial(attend_kernel, heads, per_kv),
@@ -475,7 +479,7 @@
         for d in range(1, count):
             along_ctx(d).start()
 
-    @pl.when(step == steps_per_kv - 1)
+    @pl.when(step == last - 1)
     def _():
         for d in range(1, count):
             along_ctx(d).wait_recv()
@@ -490,20 +494,17 @@
         key_sum[...] = jnp.zeros_like(key_sum)
         value_sum[...] = jnp.zeros_like(value_sum)
 
-    keys_t = keys_ref[...].T
-    values = values_ref[...]
-    for h in range(0, heads, 2):
-        grad = head_pair(grad_ref, h)
-        prob = prob_ref[0, :, h * tokens : (h + 2) * tokens]
-        wide = prob.astype(F32)
-        moved = wide * contract(values, grad, 1, 1)
-        delta = jnp.sum(moved, axis=0, keepdims=True)
-        dscore = (moved - wide * delta).astype(BF16)
-        grad_query = (dot(keys_t, dscore) * scale).T.astype(BF16)
-        grad_query_ref[:, h * HEAD : (h + 1) * HEAD] = grad_query[:tokens]
-        grad_query_ref[:, (h + 1) * HEAD : (h + 2) * HEAD] = grad_query[tokens:]
-        key_sum[...] += dot(dscore, head_pair(query_ref, h))
-        value_sum[...] += dot(prob, grad)
+    grad = stack_heads(grad_ref, heads)
+    prob = prob_ref[0]
+    wide = prob.astype(F32)
+    moved = wide * contract(values_ref[...], grad, 1, 1)
+    delta = jnp.sum(moved, axis=0, keepdims=True)
+    dscore = (moved - wide * delta).astype(BF16)
+    grad_query = (dot(keys_ref[...].T, dscore) * scale).T.astype(BF16)
+    for h in range(heads):
+        grad_query_ref[:, h * HEAD : (h + 1) * HEAD] = grad_query[h * tokens : (h + 1) * tokens]
+    key_sum[...] += dot(dscore, stack_heads(query_ref, heads))
+    value_sum[...] += dot(prob, grad)
 
     for m in range(landed.shape[1]):
 
@@ -603,40 +604,40 @@
     )(query, grad, prob, keyval, keyval, products)
 
 
-def combine_terms(half, halves, tokens, slots_ref, gates_ref, blocks_ref):
-    step = pl.program_id(0)
-    count = blocks_ref.shape[0]
-    experts = slots_ref.shape[1]
-    slots = CAP // halves
+def gather_rows(slots, blocks_ref, rows):
     pieces = BLOCK // slots
-    spread = (
-        iota((experts, count), 0) == step * (count // BLOCK) + iota((experts, count), 1) // BLOCK
-    ).astype(F32).astype(BF16)
+    span = PER_GROUP * slots
+    moved = dot(to_rows(slots, 1), blocks_ref[...]).astype(BF16)
+    place = pl.ds(pl.multiple_of(pl.program_id(0) * span, span), span)
+    for p in range(pieces):
+        rows[p, place, :] = moved[p * span : (p + 1) * span, :]
+
+
+def gate_rows(half, slots, slots_ref, gates_ref):
+    tokens, experts = slots_ref.shape
+    count = experts * slots
+    spread = (iota((experts, count), 0) == iota((experts, count), 1) // slots).astype(F32)
+    spread = spread.astype(BF16)
     slot = dot(slots_ref[...].astype(BF16), spread)
     gate = dot(gates_ref[...].astype(BF16), spread)
-    col = iota((tokens, count), 1)
-    gate = jnp.where(slot == (half * slots + col % slots).astype(F32), gate, 0.0)
-    parts = []
-    for p in range(pieces):
-        parts.append(jnp.where((col // slots) % pieces == p, gate, 0.0).astype(BF16))
-    return dot(jnp.concatenate(parts, axis=0), blocks_ref[...])
-
-
-def combine_first_kernel(halves, tokens, slots_ref, gates_ref, blocks_ref, acc_ref):
-    part = combine_terms(0, halves, tokens, slots_ref, gates_ref, blocks_ref)
-
-    @pl.when(pl.program_id(0) == 0)
-    def _():
-        acc_ref[...] = part
-
-    @pl.when(pl.program_id(0) != 0)
-    def _():
-        acc_ref[...] += part
+    own = (half * slots + iota((tokens, count), 1) % slots).astype(F32)
+    return jnp.where(slot == own, gate, 0.0).astype(BF16)
+
+
+def combine_first_kernel(halves, slots_ref, gates_ref, blocks_ref, acc_ref, rows):
+    slots = CAP // halves
+    gather_rows(slots, blocks_ref, rows)
+
+    @pl.when(pl.program_id(0) == pl.num_programs(0) - 1)
+    def _():
+        gate = gate_rows(0, slots, slots_ref, gates_ref)
+        for p in range(rows.shape[0]):
+            acc_ref[p] = dot(gate, rows[p])
 
 
 def combine_last_kernel(
     halves, slots_ref, gates_ref, blocks_ref, gain_ref, rinv_ref, first_hbm, grad_out_hbm,
-    hidden_hbm, grad_ref, acc, first_ref, grad_out_ref, hidden_ref, sem,
+    hidden_hbm, grad_ref, rows, acc, first_ref, grad_out_ref, hidden_ref, sem,
 ):
     step = pl.program_id(0)
     tokens, width = hidden_ref.shape
@@ -652,58 +653,49 @@
         for load in loads:
             load.start()
 
-    pieces = acc.shape[0] // tokens
-    piece = width // pieces
-    part = combine_terms(halves - 1, halves, tokens, slots_ref, gates_ref, blocks_ref)
-
-    @pl.when(step == 0)
-    def _():
-        acc[...] = part
-
-    @pl.when(step != 0)
-    def _():
-        acc[...] += part
+    slots = CAP // halves
+    pieces, _, piece = acc.shape
+    gather_rows(slots, blocks_ref, rows)
 
     @pl.when(step == pl.num_programs(0) - 1)
     def _():
+        gate = gate_rows(halves - 1, slots, slots_ref, gates_ref)
         for load in loads:
             load.wait()
         rinv = rinv_ref[...]
         mean = jnp.zeros((tokens, 1), F32)
         for p in range(pieces):
             cols = slice(p * piece, (p + 1) * piece)
-            rows = slice(p * tokens, (p + 1) * tokens)
-            scaled = (acc[rows, :] + first_ref[rows, :]) * gain_ref[:, cols]
-            acc[rows, :] = scaled
+            scaled = (dot(gate, rows[p]) + first_ref[p]) * gain_ref[:, cols]
+            acc[p] = scaled
             mean = mean + jnp.sum(hidden_ref[:, cols].astype(F32) * scaled, axis=1, keepdims=True)
         mean = mean / width * (rinv * rinv * rinv)
         for p in range(pieces):
             cols = slice(p * piece, (p + 1) * piece)
-            rows = slice(p * tokens, (p + 1) * tokens)
             grad = (
                 grad_out_ref[:, cols].astype(F32)
-                + rinv * acc[rows, :]
+                + rinv * acc[p]
                 - hidden_ref[:, cols].astype(F32) * mean
             )
             grad_ref[:, cols] = grad.astype(BF16)
 
 
 def combine_first(slots, gates, blocks, halves):
-    tokens = slots.shape[0]
+    tokens, experts = slots.shape
     total, piece = blocks.shape
     pieces = BLOCK * halves // CAP
-    rows = 2 * GROUP
-    whole = lambda shape: pl.BlockSpec(shape, lambda i: (0, 0))
+    whole = lambda shape: pl.BlockSpec(shape, lambda i: (0,) * len(shape))
     return pl.pallas_call(
-        functools.partial(combine_first_kernel, halves, tokens),
-        grid=(total // rows,),
+        functools.partial(combine_first_kernel, halves),
+        grid=(total // GROUP,),
         in_specs=[
             whole(slots.shape),
             whole(gates.shape),
-            pl.BlockSpec((rows, piece), lambda i: (i, 0)),
-        ],
-        out_specs=whole((pieces * tokens, piece)),
-        out_shape=jax.ShapeDtypeStruct((pieces * tokens, piece), F32),
+            pl.BlockSpec((GROUP, piece), lambda i: (i, 0)),
+        ],
+        out_specs=whole((pieces, tokens, piece)),
+        out_shape=jax.ShapeDtypeStruct((pieces, tokens, piece), F32),
+        scratch_shapes=[pltpu.VMEM((pieces, experts * CAP // halves, piece), BF16)],
         compiler_params=params(60),
         cost_estimate=cost(1, 1),
         name="combine_first",
@@ -713,15 +705,14 @@
 def combine_last(slots, gates, blocks, first, gain, grad_out, hidden, rinv, halves):
     tokens, width = hidden.shape
     total, piece = blocks.shape
-    rows = 2 * GROUP
     whole = lambda shape: pl.BlockSpec(shape, lambda i: (0, 0))
     return pl.pallas_call(
         functools.partial(combine_last_kernel, halves),
-        grid=(total // rows,),
+        grid=(total // GROUP,),
         in_specs=[
             whole(slots.shape),
             whole(gates.shape),
-            pl.BlockSpec((rows, piece), lambda i: (i, 0)),
+            pl.BlockSpec((GROUP, piece), lambda i: (i, 0)),
             whole(gain.shape),
             whole(rinv.shape),
         ]
@@ -729,6 +720,7 @@
         out_specs=whole((tokens, width)),
         out_shape=jax.ShapeDtypeStruct((tokens, width), BF16),
         scratch_shapes=[
+            pltpu.VMEM((first.shape[0], slots.shape[1] * CAP // halves, piece), BF16),
             pltpu.VMEM(first.shape, F32),
             pltpu.VMEM(first.shape, F32),
             pltpu.VMEM(grad_out.shape, BF16),
@@ -1072,7 +1064,7 @@
     )
     products = jnp.pad(products, ((0, 0), (0, HEAD - CAP))).reshape(ctx_count, -1, HEAD)
 
-    logits = router_logits[0]
+    logits, hidden = lax.optimization_barrier((router_logits[0], hidden))
     gate_expo = jnp.exp(logits - jnp.max(logits, axis=-1, keepdims=True))
     gates = gate_expo / jnp.sum(gate_expo, axis=-1, keepdims=True)
     dense_gates = jnp.zeros((tokens, experts), F32)

time: 258 us -> 253 us (0.981)
    pallas_call x1, Pallas kernels: 21.9 us -> 19.4 us  [finish(): pl.pallas_call(functools.partial(finish_kernel, heads, steps_per_kv, coun...]
    unnamed x53 -> x48, local copies, waits for them, and re-layouts: 6.99 us -> 6.98 us
  transfers between devices with their start and end apart: 5 -> 5, of which waited for: 5 -> 5; matrix products, arithmetic and copies ran while one was open for 12% -> 13% of each run, Pallas kernels for 38% -> 39%
where the time goes in v2:
time: 253 us; the launch traced here: 252 us
  Pallas kernels  138 us (55%)
  waiting for transfers between devices  38.4 us (15%)
  starting transfers between devices  34.6 us (14%)
  matrix products  19 us (8%)
  local copies, waits for them, and re-layouts  10.7 us (4%)
  other arithmetic  10.7 us (4%)
    pallas_call x2, Pallas kernels, expert(): pl.pallas_call(functools.partial(expert_kernel, slots), in_specs=[hbm, hb...  47.3 us
    all_to_all x5, waiting for transfers between devices, exchange(): moved = lax.all_to_all(split, axes, split_axis=0, concat_axis=0, tiled=True)  38.4 us
    all_to_all x5, starting transfers between devices, exchange(): moved = lax.all_to_all(split, axes, split_axis=0, concat_axis=0, tiled=True)  34.6 us
    pallas_call x1, Pallas kernels, finish(): pl.pallas_call(functools.partial(finish_kernel, heads, steps_per_kv, coun...  19.4 us
    dot_general x4, matrix products, dot(): return jnp.dot(left, right, preferred_element_type=F32)  13.8 us
    pallas_call x1, Pallas kernels, attend(): pl.pallas_call(functools.partial(attend_kernel, heads, per_kv), grid=(ste...  13.2 us
    pallas_call x1, Pallas kernels, expert_grads(): pl.pallas_call(functools.partial(expert_grads_kernel, halves), grid=(widt...  13.1 us
    pallas_call x1, Pallas kernels, open_exchange(): pl.pallas_call(functools.partial(open_kernel, count), in_specs=[vmem] * 3...  12.1 us
  transfers between devices with their start and end apart: 5, of which 5 were waited for; matrix products, arithmetic and copies ran while one was open for 13% of the time, Pallas kernels for 39%

profile of v2, /device:TPU:1, one launch (start us, length us, event | category | flops | bytes accessed | tf_op | source)
XLA Modules:
  0.0 252.1 jit_solution(7068538239908269288)
XLA Ops:
  2.1 12.1 %open_exchange.1 = (bf16[640,512]{1,0:T(8,128)(2,1)}, bf16[2048,1024]{1,0:T(8,128)(2,1)}) custom-call(bf16[128,512]{1,0:T(8,128)(2,1)} %bitcast.130, f32[128,128]{1,0:T(8,128)} %get-tuple-element.168.slots_ref, bf16[128,4096]{1,0:T(8,128)(2,1)} %bitcast.122), custom_call_target="tpu_custom_call" | custom-call | tf_op jit(solution)/shard_map/open_exchange/pallas_call | solution.py:311
  14.2 12.3 %all-to-all-start = ((bf16[128,16,1024]{2,1,0:T(8,128)(2,1)}), bf16[128,16,1024]{2,1,0:T(8,128)(2,1)}, u32[]{:S(2)}, u32[]{:S(2)}) async-start(bf16[128,16,1024]{2,1,0:T(8,128)(2,1)} %bitcast.114), calls=%async_computation | async-start | bytes 8388608 | tf_op jit(solution)/shard_map/all_to_all | solution.py:1001
  26.6 4.7 %multiply_reduce_fusion = f32[4096]{0:T(1024)S(1)} fusion(bf16[1,768,32]{1,2,0:T(8,128)(2,1)S(1)} %copy-done.7, bf16[1,32,4096]{2,1,0:T(8,128)(2,1)S(1)} %copy-done.6, bf16[1,768,4096]{2,1,0:T(8,128)(2,1)} %param.26), kind=kOutput, calls=%fused_computation.6 | convolution fusion | flops 213905408 | bytes 6619136 | tf_op jit(solution)/shard_map/dot_general | solution.py:37
  32.4 4.1 %fusion.3 = f32[768]{0:T(1024)S(1)} fusion(bf16[1,2,4096,768]{3,2,1,0:T(8,128)(2,1)} %param.22, bf16[1,2,32,768]{3,2,1,0:T(8,128)(2,1)S(1)} %copy-done.16, bf16[1,2,4096,32]{2,3,1,0:T(8,128)(2,1)S(1)} %copy-done.3), kind=kOutput, calls=%fused_computation.5 | convolution fusion | flops 213908736 | bytes 6605824 | tf_op jit(solution)/shard_map/dot_general | solution.py:37
  36.6 4.1 %fusion.1 = f32[768]{0:T(1024)S(1)} fusion(bf16[1,2,4096,768]{3,2,1,0:T(8,128)(2,1)} %param.22, bf16[1,2,32,768]{3,2,1,0:T(8,128)(2,1)S(1)} %copy-done.16, bf16[1,2,4096,32]{2,3,1,0:T(8,128)(2,1)S(1)} %copy-done.3), kind=kOutput, calls=%fused_computation.2 | convolution fusion | flops 213908736 | bytes 6605824 | tf_op jit(solution)/shard_map/dot_general | solution.py:37
  41.6 13.2 %attend.1 = (bf16[4,640,1024]{2,1,0:T(8,128)(2,1)}, bf16[128,4096]{1,0:T(8,128)(2,1)}) custom-call(s32[6]{0:T(128)} %pad_add_fusion.place_ref, bf16[128,4096]{1,0:T(8,128)(2,1)} %bitcast.149, bf16[640,512]{1,0:T(8,128)(2,1)} %get-tuple-element.61.keyval_ref.keys_ref.values_ref), custom_call_target="tpu_custom_call" | custom-call | flops 1342177280 | bytes 9437184 | tf_op jit(solution)/shard_map/attend/pallas_call | solution.py:394
  55.5 9.2 %dispatch.1 = (bf16[2048,512]{1,0:T(8,128)(2,1)}, bf16[2048,512]{1,0:T(8,128)(2,1)}, f32[128,1]{1,0:T(8,128)}) custom-call(f32[128,128]{1,0:T(8,128)} %get-tuple-element.168.slots_ref, bf16[128,4096]{1,0:T(8,128)(2,1)} %get-tuple-element.89.rows_ref.hidden_hbm, f32[1,4096]{1,0:T(1,128)} %bitcast.157), custom_call_target="tpu_custom_call" | custom-call | flops 4294967296 | bytes 10485760 | tf_op jit(solution)/shard_map/dispatch/pallas_call | solution.py:111
  66.2 11.9 %all-to-all-done = bf16[128,16,1024]{2,1,0:T(8,128)(2,1)} async-done(((bf16[128,16,1024]{2,1,0:T(8,128)(2,1)}), bf16[128,16,1024]{2,1,0:T(8,128)(2,1)}, u32[]{:S(2)}, u32[]{:S(2)}) %all-to-all-start) | async-done | bytes 4194336 | tf_op jit(solution)/shard_map/all_to_all | solution.py:1001
  78.1 5.5 %all-to-all-start.1 = ((bf16[128,16,512]{2,1,0:T(8,128)(2,1)}), bf16[128,16,512]{2,1,0:T(8,128)(2,1)}, u32[]{:S(2)}, u32[]{:S(2)}) async-start(bf16[128,16,512]{2,1,0:T(8,128)(2,1)} %bitcast.120), calls=%async_computation.1 | async-start | bytes 4194304 | tf_op jit(solution)/shard_map/all_to_all | solution.py:1001
  83.7 7.8 %unpack.1 = bf16[2,256,4096]{2,1,0:T(8,128)(2,1)} custom-call(bf16[2048,1024]{1,0:T(8,128)(2,1)} %bitcast.16.blocks_ref), custom_call_target="tpu_custom_call" | custom-call | flops 1073741824 | bytes 8388608 | tf_op jit(solution)/shard_map/unpack/pallas_call | solution.py:145
  91.5 3.5 %multiply_convert_fusion = bf16[2,256,4096]{2,1,0:T(8,128)(2,1)S(1)} fusion(bf16[2,256,4096]{2,1,0:T(8,128)(2,1)} %unpack.1, f32[4096]{0:T(1024)S(1)} %bitcast.127), kind=kLoop, calls=%fused_computation.7 | loop fusion | flops 6291456 | bytes 8404992 | tf_op jit(solution)/shard_map/convert_element_type | solution.py:1031
  96.3 3.6 %fusion.27 = f32[512,768]{1,0:T(8,128)S(1)} fusion(bf16[512,4096]{1,0:T(8,128)(2,1)S(1)} %bitcast.116, bf16[1,768,4096]{2,1,0:T(8,128)(2,1)S(1)} %bitcast.111), kind=kOutput, calls=%fused_computation.71 | convolution fusion | flops 3221225472 | bytes 12058624 | tf_op jit(solution)/shard_map/dot_general | solution.py:41
  100.3 12.7 %all-to-all-done.1 = bf16[128,16,512]{2,1,0:T(8,128)(2,1)} async-done(((bf16[128,16,512]{2,1,0:T(8,128)(2,1)}), bf16[128,16,512]{2,1,0:T(8,128)(2,1)}, u32[]{:S(2)}, u32[]{:S(2)}) %all-to-all-start.1) | async-done | bytes 2097184 | tf_op jit(solution)/shard_map/all_to_all | solution.py:1001
  113.0 5.6 %all-to-all-start.2 = ((bf16[128,16,512]{2,1,0:T(8,128)(2,1)}), bf16[128,16,512]{2,1,0:T(8,128)(2,1)}, u32[]{:S(2)}, u32[]{:S(2)}) async-start(bf16[128,16,512]{2,1,0:T(8,128)(2,1)} %bitcast.118), calls=%async_computation.2 | async-start | bytes 4194304 | tf_op jit(solution)/shard_map/all_to_all | solution.py:1001
  119.9 23.7 %expert.3 = (bf16[2048,512]{1,0:T(8,128)(2,1)}, bf16[256,4096]{1,0:T(8,128)(2,1)}, bf16[256,768]{1,0:T(8,128)(2,1)}, bf16[256,64]{1,0:T(8,128)(2,1)}, bf16[2,256...) custom-call(bf16[2048,512]{1,0:T(8,128)(2,1)} %bitcast.31.blocks_hbm, ...), custom_call_target="tpu_custom_call" | custom-call | flops 6442450944 | bytes 31457280 | tf_op jit(solution)/shard_map/expert/pallas_call | solution.py:863
  143.5 4.5 %all-to-all-done.2 = bf16[128,16,512]{2,1,0:T(8,128)(2,1)} async-done(((bf16[128,16,512]{2,1,0:T(8,128)(2,1)}), bf16[128,16,512]{2,1,0:T(8,128)(2,1)}, u32[]{:S(2)}, u32[]{:S(2)}) %all-to-all-start.2) | async-done | bytes 2097184 | tf_op jit(solution)/shard_map/all_to_all | solution.py:1001
  148.1 5.4 %all-to-all-start.4 = ((bf16[128,16,512]{2,1,0:T(8,128)(2,1)}), bf16[128,16,512]{2,1,0:T(8,128)(2,1)S(1)}, u32[]{:S(2)}, u32[]{:S(2)}) async-start(bf16[128,16,512]{2,1,0:T(8,128)(2,1)} %bitcast.119), calls=%async_computation.4 | async-start | bytes 4194304 | tf_op jit(solution)/shard_map/all_to_all | solution.py:1001
  153.5 23.7 %expert.2 = (bf16[2048,512]{1,0:T(8,128)(2,1)}, bf16[256,4096]{1,0:T(8,128)(2,1)}, bf16[256,768]{1,0:T(8,128)(2,1)}, bf16[256,64]{1,0:T(8,128)(2,1)}, bf16[2,256...) custom-call(bf16[2048,512]{1,0:T(8,128)(2,1)} %bitcast.33.blocks_hbm, ...), custom_call_target="tpu_custom_call" | custom-call | flops 6442450944 | bytes 31457280 | tf_op jit(solution)/shard_map/expert/pallas_call | solution.py:863
  177.2 6.0 %all-to-all-done.4 = bf16[128,16,512]{2,1,0:T(8,128)(2,1)S(1)} async-done(((bf16[128,16,512]{2,1,0:T(8,128)(2,1)}), bf16[128,16,512]{2,1,0:T(8,128)(2,1)S(1)}, u32[]{:S(2)}, u32[]{:S(2)}) %all-to-all-start.4) | async-done | bytes 2097184 | tf_op jit(solution)/shard_map/all_to_all | solution.py:1001
  183.2 5.8 %all-to-all-start.3 = ((bf16[128,16,512]{2,1,0:T(8,128)(2,1)}), bf16[128,16,512]{2,1,0:T(8,128)(2,1)}, u32[]{:S(2)}, u32[]{:S(2)}) async-start(bf16[128,16,512]{2,1,0:T(8,128)(2,1)} %bitcast.117), calls=%async_computation.3 | async-start | bytes 4194304 | tf_op jit(solution)/shard_map/all_to_all | solution.py:1001
  190.8 7.0 %combine_first.1.first_hbm = f32[8,128,512]{2,1,0:T(8,128)} custom-call(f32[128,128]{1,0:T(8,128)} %get-tuple-element.167.slots_ref, f32[128,128]{1,0:T(8,128)} %get-tuple-element.166.gates_ref, bf16[2048,512]{1,0:T(8,128)(2,1)} %bitcast.108), custom_call_target="tpu_custom_call" | custom-call | flops 1 | bytes 1 | tf_op jit(solution)/shard_map/combine_first/pallas_call | solution.py:688
  198.7 13.1 %expert_grads.1 = (f32[1,4096]{1,0:T(1,128)}, f32[32,4096]{1,0:T(8,128)}, f32[64,4096]{1,0:T(8,128)}, f32[32,768]{1,0:T(8,128)}, f32[2,32,768]{2,1,0:T(8,128)}) custom-call(bf16[512,4096]{1,0:T(8,128)(2,1)} %bitcast.107, f32[1,4096]{1,0:T(1,128)} %copy-done.8, bf16[768,4096]{1,0:T(8,128)(2,1)} %bitcast.109, bf16[32,4096]{1,0:T(8,128)(2,1)} %bitcast.126, ...), custom_call_target="tpu_custom_call" | custom-call | flops 1 | bytes 1 | tf_op jit(solution)/shard_map/expert_grads/pallas_call | solution.py:945
  218.4 8.4 %combine_last.1.grad_ref = bf16[128,4096]{1,0:T(8,128)(2,1)} custom-call(f32[128,128]{1,0:T(8,128)} %get-tuple-element.167.slots_ref, f32[128,128]{1,0:T(8,128)} %get-tuple-element.166.gates_ref, bf16[2048,512]{1,0:T(8,128)(2,1)} %bitcast.37.blocks_ref, f32[1,4096]{1,0:T(1,128)} %bitcast.158, f32[128,1]{1,0:T(8,128)} %get-tuple-element.72.rinv_ref, ...), custom_call_target="tpu_custom_call" | custom-call | flops 2147483648 | bytes 8388608 | tf_op jit(solution)/shard_map/combine_last/pallas_call | solution.py:709
  226.9 19.4 %finish.1 = (bf16[128,4096]{1,0:T(8,128)(2,1)}, bf16[128,512]{1,0:T(8,128)(2,1)}, f32[16,8,128]{2,1,0:T(8,128)}) custom-call(bf16[128,4096]{1,0:T(8,128)(2,1)} %bitcast.150, bf16[128,4096]{1,0:T(8,128)(2,1)} %combine_last.1.grad_ref, bf16[4,640,1024]{2,1,0:T(8,128)(2,1)} %get-tuple-element.90.prob_ref, ...), custom_call_target="tpu_custom_call" | custom-call | flops 2684354560 | bytes 10485760 | tf_op jit(solution)/shard_map/finish/pallas_call | solution.py:563
  (87 shorter events, 23.5 us)
Async XLA Ops:
  14.2 12.4 %copy-start.6 = (bf16[1,32,4096]{2,1,0:T(8,128)(2,1)S(1)}, bf16[1,32,4096]{2,1,0:T(8,128)(2,1)}, u32[]{:S(2)}) copy-start(bf16[1,32,4096]{2,1,0:T(8,128)(2,1)} %param.28) | copy-start | bytes 786436
  14.2 12.4 %copy-start.7 = (bf16[1,768,32]{1,2,0:T(8,128)(2,1)S(1)}, bf16[1,768,32]{1,2,0:T(8,128)(2,1)}, u32[]{:S(2)}) copy-start(bf16[1,768,32]{1,2,0:T(8,128)(2,1)} %param.27) | copy-start | bytes 147460
  14.2 63.9 %all-to-all-start = ((bf16[128,16,1024]{2,1,0:T(8,128)(2,1)}), bf16[128,16,1024]{2,1,0:T(8,128)(2,1)}, u32[]{:S(2)}, u32[]{:S(2)}) async-start(bf16[128,16,1024]{2,1,0:T(8,128)(2,1)} %bitcast.114), calls=%async_computation | async-start | bytes 8388608 | tf_op jit(solution)/shard_map/all_to_all | solution.py:1001
  26.6 4.8 %copy-start.3 = (bf16[1,2,4096,32]{2,3,1,0:T(8,128)(2,1)S(1)}, bf16[1,2,4096,32]{2,3,1,0:T(8,128)(2,1)}, u32[]{:S(2)}) copy-start(bf16[1,2,4096,32]{2,3,1,0:T(8,128)(2,1)} %param.23) | copy-start | bytes 1572868
  26.6 5.8 %copy-start.16 = (bf16[1,2,32,768]{3,2,1,0:T(8,128)(2,1)S(1)}, bf16[1,2,32,768]{3,2,1,0:T(8,128)(2,1)}, u32[]{:S(2)}) copy-start(bf16[1,2,32,768]{3,2,1,0:T(8,128)(2,1)} %param.24) | copy-start | bytes 294916
  36.6 4.2 %copy-start.11 = (f32[1,4096]{1,0:T(1,128)S(1)}, f32[1,4096]{1,0:T(1,128)}, u32[]{:S(2)}) copy-start(f32[1,4096]{1,0:T(1,128)} %param.29) | copy-start | bytes 49156
  36.6 4.2 %copy-start.17 = (s32[1,4]{1,0:T(1,128)S(1)}, s32[1,4]{1,0:T(1,128)}, u32[]{:S(2)}) copy-start(s32[1,4]{1,0:T(1,128)} %param.17) | copy-start | bytes 52
  40.8 14.1 %copy-start.12 = (f32[1,2,768]{2,1,0:T(2,128)S(1)}, f32[1,2,768]{2,1,0:T(2,128)}, u32[]{:S(2)}) copy-start(f32[1,2,768]{2,1,0:T(2,128)} %param.25) | copy-start | bytes 18436
  40.8 50.6 %copy-start.8 = (f32[1,4096]{1,0:T(1,128)}, f32[1,4096]{1,0:T(1,128)S(1)}, u32[]{:S(2)}) copy-start(f32[1,4096]{1,0:T(1,128)S(1)} %div.24.scale_ref) | copy-start | bytes 49156
  78.1 34.9 %all-to-all-start.1 = ((bf16[128,16,512]{2,1,0:T(8,128)(2,1)}), bf16[128,16,512]{2,1,0:T(8,128)(2,1)}, u32[]{:S(2)}, u32[]{:S(2)}) async-start(bf16[128,16,512]{2,1,0:T(8,128)(2,1)} %bitcast.120), calls=%async_computation.1 | async-start | bytes 4194304 | tf_op jit(solution)/shard_map/all_to_all | solution.py:1001
  83.6 12.6 %slice-start = ((s8[6291456]{0:T(1024)(128)(4,1)}), s8[2097152]{0:T(1024)(128)(4,1)S(1)}, s32[]{:S(2)}) async-start(s8[6291456]{0:T(1024)(128)(4,1)} %bitcast.110), calls=%async_computation.5 | async-start | bytes 4194304
  91.5 4.8 %slice-start.1 = ((s8[6291456]{0:T(1024)(128)(4,1)}), s8[4194304]{0:T(1024)(128)(4,1)S(1)}, s32[]{:S(2)}) async-start(s8[6291456]{0:T(1024)(128)(4,1)} %bitcast.110), calls=%async_computation.6 | async-start | bytes 8388608
  113.0 35.1 %all-to-all-start.2 = ((bf16[128,16,512]{2,1,0:T(8,128)(2,1)}), bf16[128,16,512]{2,1,0:T(8,128)(2,1)}, u32[]{:S(2)}, u32[]{:S(2)}) async-start(bf16[128,16,512]{2,1,0:T(8,128)(2,1)} %bitcast.118), calls=%async_computation.2 | async-start | bytes 4194304 | tf_op jit(solution)/shard_map/all_to_all | solution.py:1001
  148.1 35.1 %all-to-all-start.4 = ((bf16[128,16,512]{2,1,0:T(8,128)(2,1)}), bf16[128,16,512]{2,1,0:T(8,128)(2,1)S(1)}, u32[]{:S(2)}, u32[]{:S(2)}) async-start(bf16[128,16,512]{2,1,0:T(8,128)(2,1)} %bitcast.119), calls=%async_computation.4 | async-start | bytes 4194304 | tf_op jit(solution)/shard_map/all_to_all | solution.py:1001
  177.1 12.6 %copy-start.15 = (f32[1,128,3]{1,0,2:T(1,128)S(1)}, f32[1,128,3]{1,0,2:T(1,128)}, u32[]{:S(2)}) copy-start(f32[1,128,3]{1,0,2:T(1,128)} %param.19) | copy-start | bytes 4612
  183.2 7.6 %copy-start = (bf16[128,16,512]{2,1,0:T(8,128)(2,1)}, bf16[128,16,512]{2,1,0:T(8,128)(2,1)S(1)}, u32[]{:S(2)}) copy-start(bf16[128,16,512]{2,1,0:T(8,128)(2,1)S(1)} %all-to-all-done.4) | copy-start | bytes 6291460
  183.2 14.6 %copy-start.4 = (bf16[256,768]{1,0:T(8,128)(2,1)S(1)}, bf16[256,768]{1,0:T(8,128)(2,1)}, u32[]{:S(2)}) copy-start(bf16[256,768]{1,0:T(8,128)(2,1)} %get-tuple-element.96) | copy-start | bytes 1179652
  183.2 14.6 %copy-start.5 = (bf16[256,768]{1,0:T(8,128)(2,1)S(1)}, bf16[256,768]{1,0:T(8,128)(2,1)}, u32[]{:S(2)}) copy-start(bf16[256,768]{1,0:T(8,128)(2,1)} %get-tuple-element.97) | copy-start | bytes 1179652
  183.2 35.3 %all-to-all-start.3 = ((bf16[128,16,512]{2,1,0:T(8,128)(2,1)}), bf16[128,16,512]{2,1,0:T(8,128)(2,1)}, u32[]{:S(2)}, u32[]{:S(2)}) async-start(bf16[128,16,512]{2,1,0:T(8,128)(2,1)} %bitcast.117), calls=%async_computation.3 | async-start | bytes 4194304 | tf_op jit(solution)/shard_map/all_to_all | solution.py:1001
  198.7 14.5 %copy-start.9 = (f32[256,1]{1,0:T(8,128)S(1)}, f32[256,1]{1,0:T(8,128)}, u32[]{:S(2)}) copy-start(f32[256,1]{1,0:T(8,128)} %get-tuple-element.91) | copy-start | bytes 3076
  198.7 14.5 %copy-start.10 = (f32[256,1]{1,0:T(8,128)S(1)}, f32[256,1]{1,0:T(8,128)}, u32[]{:S(2)}) copy-start(f32[256,1]{1,0:T(8,128)} %get-tuple-element.92) | copy-start | bytes 3076
  198.7 15.9 %copy-start.13 = (f32[2,768]{1,0:T(2,128)S(1)}, f32[2,768]{1,0:T(2,128)}, u32[]{:S(2)}) copy-start(f32[2,768]{1,0:T(2,128)} %get-tuple-element.108) | copy-start | bytes 18436
  198.7 15.9 %copy-start.14 = (f32[2,768]{1,0:T(2,128)S(1)}, f32[2,768]{1,0:T(2,128)}, u32[]{:S(2)}) copy-start(f32[2,768]{1,0:T(2,128)} %get-tuple-element.109) | copy-start | bytes 18436
  226.9 20.5 %copy-start.1 = (f32[128,128]{1,0:T(8,128)S(1)}, f32[128,128]{1,0:T(8,128)}, u32[]{:S(2)}) copy-start(f32[128,128]{1,0:T(8,128)} %get-tuple-element.167.slots_ref) | copy-start | bytes 196612
  (1 other events, 3.6 us)

commit v3 on v2

--- a/solution.py
+++ b/solution.py
@@ -429,15 +429,27 @@
     place = lax.axis_index("ep")
     barrier = pltpu.get_barrier_semaphore()
 
-    def send_terms(j, m):
+    def send_terms(j, m, part):
         return pltpu.make_async_remote_copy(
-            src_ref=terms.at[m, pl.ds((REACH - j) * tokens, tokens)],
-            dst_ref=landed.at[j - 1, m],
-            send_sem=send_sem.at[j - 1, m],
-            recv_sem=recv_sem.at[j - 1, m],
+            src_ref=terms.at[m, part, pl.ds((REACH - j) * tokens, tokens)],
+            dst_ref=landed.at[j - 1, m, part],
+            send_sem=send_sem.at[j - 1, m, part],
+            recv_sem=recv_sem.at[j - 1, m, part],
             device_id={"ctx": me - j},
             device_id_type=MESH,
         )
+
+    def send_part(part, total):
+        for m in range(landed.shape[1]):
+
+            @pl.when(step == (m + 1) * steps_per_kv - 1)
+            def _():
+                terms[m, part] = total().astype(BF16)
+                for j in range(REACH, 0, -1):
+
+                    @pl.when(me >= j)
+                    def _():
+                        send_terms(j, m, part).start()
 
     def along_ctx(d):
         target = (me + d) % count
@@ -496,27 +508,17 @@
 
     grad = stack_heads(grad_ref, heads)
     prob = prob_ref[0]
+    value_sum[...] += dot(prob, grad)
+    send_part(1, lambda: value_sum[...])
     wide = prob.astype(F32)
     moved = wide * contract(values_ref[...], grad, 1, 1)
     delta = jnp.sum(moved, axis=0, keepdims=True)
     dscore = (moved - wide * delta).astype(BF16)
-    grad_query = (dot(keys_ref[...].T, dscore) * scale).T.astype(BF16)
+    key_sum[...] += dot(dscore, stack_heads(query_ref, heads))
+    send_part(0, lambda: key_sum[...] * scale)
+    grad_query = dot(keys_ref[...].T, dscore).T.astype(BF16)
     for h in range(heads):
         grad_query_ref[:, h * HEAD : (h + 1) * HEAD] = grad_query[h * tokens : (h + 1) * tokens]
-    key_sum[...] += dot(dscore, stack_heads(query_ref, heads))
-    value_sum[...] += dot(prob, grad)
-
-    for m in range(landed.shape[1]):
-
-        @pl.when(step == (m + 1) * steps_per_kv - 1)
-        def _():
-            terms[m, :, :HEAD] = (key_sum[...] * scale).astype(BF16)
-            terms[m, :, HEAD:] = value_sum[...].astype(BF16)
-            for j in range(REACH, 0, -1):
-
-                @pl.when(me >= j)
-                def _():
-                    send_terms(j, m).start()
 
     @pl.when(step == last)
     def _():
@@ -527,28 +529,27 @@
             along_ep(d).wait_recv()
         returned_ref[...] = arrived[...]
         for m in range(landed.shape[1]):
-            for j in range(1, REACH + 1):
-
-                @pl.when(me + j < count)
-                def _():
-                    send_terms(j, m).wait_recv()
-
-                @pl.when(me + j >= count)
-                def _():
-                    landed[j - 1, m] = jnp.zeros(landed.shape[2:], landed.dtype)
-
-            total = terms[m, REACH * tokens :, :].astype(F32)
-            for j in range(REACH):
-                total = total + landed[j, m].astype(F32)
-            grad_keyval_ref[:, m * HEAD : (m + 1) * HEAD] = total[:, :HEAD].astype(BF16)
-            grad_keyval_ref[:, half + m * HEAD : half + (m + 1) * HEAD] = total[:, HEAD:].astype(
-                BF16
-            )
-            for j in range(1, REACH + 1):
-
-                @pl.when(me >= j)
-                def _():
-                    send_terms(j, m).wait_send()
+            for part in (1, 0):
+                for j in range(1, REACH + 1):
+
+                    @pl.when(me + j < count)
+                    def _():
+                        send_terms(j, m, part).wait_recv()
+
+                    @pl.when(me + j >= count)
+                    def _():
+                        landed[j - 1, m, part] = jnp.zeros(landed.shape[3:], landed.dtype)
+
+                total = terms[m, part, REACH * tokens :, :].astype(F32)
+                for j in range(REACH):
+                    total = total + landed[j, m, part].astype(F32)
+                first = part * half + m * HEAD
+                grad_keyval_ref[:, first : first + HEAD] = total.astype(BF16)
+                for j in range(1, REACH + 1):
+
+                    @pl.when(me >= j)
+                    def _():
+                        send_terms(j, m, part).wait_send()
 
 
 def finish(query, grad, prob, keyval, products):
@@ -584,13 +585,13 @@
         scratch_shapes=[
             pltpu.VMEM((window, HEAD), F32),
             pltpu.VMEM((window, HEAD), F32),
-            pltpu.VMEM((kv_heads, window, 2 * HEAD), BF16),
-            pltpu.VMEM((REACH, kv_heads, tokens, 2 * HEAD), BF16),
+            pltpu.VMEM((kv_heads, 2, window, HEAD), BF16),
+            pltpu.VMEM((REACH, kv_heads, 2, tokens, HEAD), BF16),
             pltpu.VMEM((count, ep_count, lanes), F32),
             pltpu.VMEM((ep_count, count, lanes), F32),
             pltpu.VMEM((ep_count, count, lanes), F32),
-            pltpu.SemaphoreType.DMA((REACH, kv_heads)),
-            pltpu.SemaphoreType.DMA((REACH, kv_heads)),
+            pltpu.SemaphoreType.DMA((REACH, kv_heads, 2)),
+            pltpu.SemaphoreType.DMA((REACH, kv_heads, 2)),
             pltpu.SemaphoreType.DMA((count - 1,)),
             pltpu.SemaphoreType.DMA((count - 1,)),
             pltpu.SemaphoreType.DMA((ep_count - 1,)),
@@ -604,13 +605,20 @@
     )(query, grad, prob, keyval, keyval, products)
 
 
-def gather_rows(slots, blocks_ref, rows):
+def gather_rows(slots, blocks_ref, rows, order):
     pieces = BLOCK // slots
     span = PER_GROUP * slots
-    moved = dot(to_rows(slots, 1), blocks_ref[...]).astype(BF16)
-    place = pl.ds(pl.multiple_of(pl.program_id(0) * span, span), span)
-    for p in range(pieces):
-        rows[p, place, :] = moved[p * span : (p + 1) * span, :]
+    groups = blocks_ref.shape[0] // GROUP
+
+    @pl.when(pl.program_id(0) == 0)
+    def _():
+        order[...] = to_rows(slots, 1)
+
+    for g in range(groups):
+        moved = dot(order[...], blocks_ref[g * GROUP : (g + 1) * GROUP, :]).astype(BF16)
+        place = pl.ds(pl.multiple_of((pl.program_id(0) * groups + g) * span, span), span)
+        for p in range(pieces):
+            rows[p, place, :] = moved[p * span : (p + 1) * span, :]
 
 
 def gate_rows(half, slots, slots_ref, gates_ref):
@@ -624,9 +632,9 @@
     return jnp.where(slot == own, gate, 0.0).astype(BF16)
 
 
-def combine_first_kernel(halves, slots_ref, gates_ref, blocks_ref, acc_ref, rows):
+def combine_first_kernel(halves, slots_ref, gates_ref, blocks_ref, acc_ref, rows, order):
     slots = CAP // halves
-    gather_rows(slots, blocks_ref, rows)
+    gather_rows(slots, blocks_ref, rows, order)
 
     @pl.when(pl.program_id(0) == pl.num_programs(0) - 1)
     def _():
@@ -637,7 +645,7 @@
 
 def combine_last_kernel(
     halves, slots_ref, gates_ref, blocks_ref, gain_ref, rinv_ref, first_hbm, grad_out_hbm,
-    hidden_hbm, grad_ref, rows, acc, first_ref, grad_out_ref, hidden_ref, sem,
+    hidden_hbm, grad_ref, rows, order, acc, first_ref, grad_out_ref, hidden_ref, sem,
 ):
     step = pl.program_id(0)
     tokens, width = hidden_ref.shape
@@ -655,7 +663,7 @@
 
     slots = CAP // halves
     pieces, _, piece = acc.shape
-    gather_rows(slots, blocks_ref, rows)
+    gather_rows(slots, blocks_ref, rows, order)
 
     @pl.when(step == pl.num_programs(0) - 1)
     def _():
@@ -687,15 +695,18 @@
     whole = lambda shape: pl.BlockSpec(shape, lambda i: (0,) * len(shape))
     return pl.pallas_call(
         functools.partial(combine_first_kernel, halves),
-        grid=(total // GROUP,),
+        grid=(total // (4 * GROUP),),
         in_specs=[
             whole(slots.shape),
             whole(gates.shape),
-            pl.BlockSpec((GROUP, piece), lambda i: (i, 0)),
+            pl.BlockSpec((4 * GROUP, piece), lambda i: (i, 0)),
         ],
         out_specs=whole((pieces, tokens, piece)),
         out_shape=jax.ShapeDtypeStruct((pieces, tokens, piece), F32),
-        scratch_shapes=[pltpu.VMEM((pieces, experts * CAP // halves, piece), BF16)],
+        scratch_shapes=[
+            pltpu.VMEM((pieces, experts * CAP // halves, piece), BF16),
+            pltpu.VMEM((GROUP, GROUP), BF16),
+        ],
         compiler_params=params(60),
         cost_estimate=cost(1, 1),
         name="combine_first",
@@ -708,11 +719,11 @@
     whole = lambda shape: pl.BlockSpec(shape, lambda i: (0, 0))
     return pl.pallas_call(
         functools.partial(combine_last_kernel, halves),
-        grid=(total // GROUP,),
+        grid=(total // (4 * GROUP),),
         in_specs=[
             whole(slots.shape),
             whole(gates.shape),
-            pl.BlockSpec((GROUP, piece), lambda i: (i, 0)),
+            pl.BlockSpec((4 * GROUP, piece), lambda i: (i, 0)),
             whole(gain.shape),
             whole(rinv.shape),
         ]
@@ -721,6 +732,7 @@
         out_shape=jax.ShapeDtypeStruct((tokens, width), BF16),
         scratch_shapes=[
             pltpu.VMEM((first.shape[0], slots.shape[1] * CAP // halves, piece), BF16),
+            pltpu.VMEM((GROUP, GROUP), BF16),
             pltpu.VMEM(first.shape, F32),
             pltpu.VMEM(first.shape, F32),
             pltpu.VMEM(grad_out.shape, BF16),
@@ -1023,6 +1035,15 @@
     prob, hidden = attend(place, query, seen)
     *outgoing, rinv = dispatch(slots, hidden, gain, True, halves)
 
+    logits, hidden = lax.optimization_barrier((router_logits[0], hidden))
+    gate_expo = jnp.exp(logits - jnp.max(logits, axis=-1, keepdims=True))
+    gates = gate_expo / jnp.sum(gate_expo, axis=-1, keepdims=True)
+    dense_gates = jnp.zeros((tokens, experts), F32)
+    chosen = [ids[:, k : k + 1] == each.reshape(1, experts) for k in range(top)]
+    for k in range(top):
+        dense_gates = dense_gates + jnp.where(chosen[k], gates[:, k : k + 1], 0.0)
+    token_slots = slots.T
+
     norm_in = jnp.stack([square_norm(base_in[j], low_in[j], high_in[j]) for j in range(2)])
     scale_in = mag_in / norm_in
     norm_out = square_norm(base_out, low_out, high_out)
@@ -1033,8 +1054,8 @@
     grad_hidden = contract(grad_linear_out, base_out, 1, 1) + contract(back_low, low_out, 1, 1)
     low_pair = jnp.concatenate([low_in[0], low_in[1]], axis=1)
     arrived = [exchange(outgoing[0])]
-    second, grad_hidden, scale_in, low_pair, _ = lax.optimization_barrier(
-        (outgoing[1], grad_hidden, scale_in, low_pair, arrived[0])
+    second, grad_hidden, scale_in, low_pair, dense_gates, token_slots, _ = lax.optimization_barrier(
+        (outgoing[1], grad_hidden, scale_in, low_pair, dense_gates, token_slots, arrived[0])
     )
     arrived.append(exchange(second))
 
@@ -1064,19 +1085,12 @@
     )
     products = jnp.pad(products, ((0, 0), (0, HEAD - CAP))).reshape(ctx_count, -1, HEAD)
 
-    logits, hidden = lax.optimization_barrier((router_logits[0], hidden))
-    gate_expo = jnp.exp(logits - jnp.max(logits, axis=-1, keepdims=True))
-    gates = gate_expo / jnp.sum(gate_expo, axis=-1, keepdims=True)
-    dense_gates = jnp.zeros((tokens, experts), F32)
-    chosen = [ids[:, k : k + 1] == each.reshape(1, experts) for k in range(top)]
-    for k in range(top):
-        dense_gates = dense_gates + jnp.where(chosen[k], gates[:, k : k + 1], 0.0)
-    token_slots = slots.T
     partial = combine_first(token_slots, dense_gates, returned[0], halves)
     grad_heads = combine_last(
         token_slots, dense_gates, returned[1], partial, gain, grad_out, hidden, rinv, halves
     )
     grad_query, grad_keyval, arrived_products = finish(query, grad_heads, prob, seen, products)
+    grad_query = (grad_query.astype(F32) * HEAD ** (-0.5)).astype(BF16)
     returned_products = arrived_products.transpose(1, 0, 2).reshape(experts, HEAD)
     dense_products = jnp.zeros((tokens, experts), F32)
     for r in range(CAP):

time: 253 us -> 249 us (0.984)
  Pallas kernels: 138 us -> 130 us
  waiting for transfers between devices: 38.4 us -> 42.9 us
  other arithmetic: 10.7 us -> 13.8 us
    all_to_all x5, waiting for transfers between devices: 38.4 us -> 42.9 us  [exchange(): moved = lax.all_to_all(split, axes, split_axis=0, concat_axis=0, tiled=True)]
    pallas_call x1, Pallas kernels: 6.97 us -> 4.08 us  [combine_first(): pl.pallas_call(functools.partial(combine_first_kernel, halves), grid=(tot...]
    pallas_call x1, Pallas kernels: 8.44 us -> 5.56 us  [combine_last(): pl.pallas_call(functools.partial(combine_last_kernel, halves), grid=(tota...]
    unnamed x48 -> x53, local copies, waits for them, and re-layouts: 6.98 us -> 4.71 us
  transfers between devices with their start and end apart: 5 -> 5, of which waited for: 5 -> 5; matrix products, arithmetic and copies ran while one was open for 13% -> 13% of each run, Pallas kernels for 39% -> 38%
where the time goes in v3:
time: 249 us; the launch traced here: 248 us
  Pallas kernels  130 us (52%)
  waiting for transfers between devices  42.9 us (17%)
  starting transfers between devices  34.6 us (14%)
  matrix products  16.8 us (7%)
  other arithmetic  13.8 us (6%)
  local copies, waits for them, and re-layouts  8.49 us (3%)
    pallas_call x2, Pallas kernels, expert(): pl.pallas_call(functools.partial(expert_kernel, slots), in_specs=[hbm, hb...  47.4 us
    all_to_all x5, waiting for transfers between devices, exchange(): moved = lax.all_to_all(split, axes, split_axis=0, concat_axis=0, tiled=True)  42.9 us
    all_to_all x5, starting transfers between devices, exchange(): moved = lax.all_to_all(split, axes, split_axis=0, concat_axis=0, tiled=True)  34.6 us
    pallas_call x1, Pallas kernels, finish(): pl.pallas_call(functools.partial(finish_kernel, heads, steps_per_kv, coun...  18 us
    pallas_call x1, Pallas kernels, attend(): pl.pallas_call(functools.partial(attend_kernel, heads, per_kv), grid=(ste...  13.2 us
    pallas_call x1, Pallas kernels, expert_grads(): pl.pallas_call(functools.partial(expert_grads_kernel, halves), grid=(widt...  13.1 us
    pallas_call x1, Pallas kernels, open_exchange(): pl.pallas_call(functools.partial(open_kernel, count), in_specs=[vmem] * 3...  12.1 us
    dot_general x4, matrix products, dot(): return jnp.dot(left, right, preferred_element_type=F32)  11.6 us
  transfers between devices with their start and end apart: 5, of which 5 were waited for; matrix products, arithmetic and copies ran while one was open for 13% of the time, Pallas kernels for 38%

profile of v3, /device:TPU:1, one launch (start us, length us, event | category | flops | bytes accessed | tf_op | source)
XLA Modules:
  0.0 248.2 jit_solution(9777786537389426471)
XLA Ops:
  2.3 12.1 %open_exchange.1 = (bf16[640,512]{1,0:T(8,128)(2,1)}, bf16[2048,1024]{1,0:T(8,128)(2,1)}) custom-call(bf16[128,512]{1,0:T(8,128)(2,1)} %bitcast.130, f32[128,128]{1,0:T(8,128)} %get-tuple-element.171.slots_ref, bf16[128,4096]{1,0:T(8,128)(2,1)} %bitcast.123), custom_call_target="tpu_custom_call" | custom-call | tf_op jit(solution)/shard_map/open_exchange/pallas_call | solution.py:311
  14.4 12.4 %all-to-all-start = ((bf16[128,16,1024]{2,1,0:T(8,128)(2,1)}), bf16[128,16,1024]{2,1,0:T(8,128)(2,1)}, u32[]{:S(2)}, u32[]{:S(2)}) async-start(bf16[128,16,1024]{2,1,0:T(8,128)(2,1)} %bitcast.115), calls=%async_computation | async-start | bytes 8388608 | tf_op jit(solution)/shard_map/all_to_all | solution.py:1013
  26.9 4.8 %multiply_reduce_fusion = f32[4096]{0:T(1024)S(1)} fusion(bf16[1,768,32]{1,2,0:T(8,128)(2,1)S(1)} %copy-done.7, bf16[1,32,4096]{2,1,0:T(8,128)(2,1)S(1)} %copy-done.6, bf16[1,768,4096]{2,1,0:T(8,128)(2,1)} %param.26), kind=kOutput, calls=%fused_computation.6 | convolution fusion | flops 213905408 | bytes 6619136 | tf_op jit(solution)/shard_map/dot_general | solution.py:37
  31.7 4.3 %fusion.1 = f32[768]{0:T(1024)S(1)} fusion(bf16[1,2,4096,768]{3,2,1,0:T(8,128)(2,1)} %param.22, bf16[1,2,32,768]{3,2,1,0:T(8,128)(2,1)S(1)} %copy-done.16, bf16[1,2,4096,32]{2,3,1,0:T(8,128)(2,1)S(1)} %copy-done.3), kind=kOutput, calls=%fused_computation.2 | convolution fusion | flops 213908736 | bytes 6605824 | tf_op jit(solution)/shard_map/dot_general | solution.py:37
  40.3 13.2 %attend.1 = (bf16[4,640,1024]{2,1,0:T(8,128)(2,1)}, bf16[128,4096]{1,0:T(8,128)(2,1)}) custom-call(s32[6]{0:T(128)} %pad_add_fusion.place_ref, bf16[128,4096]{1,0:T(8,128)(2,1)} %bitcast.151, bf16[640,512]{1,0:T(8,128)(2,1)} %get-tuple-element.63.keyval_ref.keys_ref.values_ref), custom_call_target="tpu_custom_call" | custom-call | flops 1342177280 | bytes 9437184 | tf_op jit(solution)/shard_map/attend/pallas_call | solution.py:394
  55.1 9.2 %dispatch.1 = (bf16[2048,512]{1,0:T(8,128)(2,1)}, bf16[2048,512]{1,0:T(8,128)(2,1)}, f32[128,1]{1,0:T(8,128)}) custom-call(f32[128,128]{1,0:T(8,128)} %get-tuple-element.171.slots_ref, bf16[128,4096]{1,0:T(8,128)(2,1)} %get-tuple-element.93.rows_ref.hidden_hbm, f32[1,4096]{1,0:T(1,128)} %bitcast.159), custom_call_target="tpu_custom_call" | custom-call | flops 4294967296 | bytes 10485760 | tf_op jit(solution)/shard_map/dispatch/pallas_call | solution.py:111
  65.8 12.5 %all-to-all-done = bf16[128,16,1024]{2,1,0:T(8,128)(2,1)} async-done(((bf16[128,16,1024]{2,1,0:T(8,128)(2,1)}), bf16[128,16,1024]{2,1,0:T(8,128)(2,1)}, u32[]{:S(2)}, u32[]{:S(2)}) %all-to-all-start) | async-done | bytes 4194336 | tf_op jit(solution)/shard_map/all_to_all | solution.py:1013
  78.3 5.5 %all-to-all-start.1 = ((bf16[128,16,512]{2,1,0:T(8,128)(2,1)}), bf16[128,16,512]{2,1,0:T(8,128)(2,1)}, u32[]{:S(2)}, u32[]{:S(2)}) async-start(bf16[128,16,512]{2,1,0:T(8,128)(2,1)} %bitcast.121), calls=%async_computation.1 | async-start | bytes 4194304 | tf_op jit(solution)/shard_map/all_to_all | solution.py:1013
  83.9 7.7 %unpack.1 = bf16[2,256,4096]{2,1,0:T(8,128)(2,1)} custom-call(bf16[2048,1024]{1,0:T(8,128)(2,1)} %bitcast.12.blocks_ref), custom_call_target="tpu_custom_call" | custom-call | flops 1073741824 | bytes 8388608 | tf_op jit(solution)/shard_map/unpack/pallas_call | solution.py:145
  91.6 3.5 %multiply_convert_fusion = bf16[2,256,4096]{2,1,0:T(8,128)(2,1)S(1)} fusion(bf16[2,256,4096]{2,1,0:T(8,128)(2,1)} %unpack.1, f32[4096]{0:T(1024)S(1)} %bitcast.127), kind=kLoop, calls=%fused_computation.7 | loop fusion | flops 6291456 | bytes 8404992 | tf_op jit(solution)/shard_map/convert_element_type | solution.py:1052
  96.4 3.6 %fusion.28 = f32[512,768]{1,0:T(8,128)S(1)} fusion(bf16[512,4096]{1,0:T(8,128)(2,1)S(1)} %bitcast.117, bf16[1,768,4096]{2,1,0:T(8,128)(2,1)S(1)} %bitcast.112), kind=kOutput, calls=%fused_computation.73 | convolution fusion | flops 3221225472 | bytes 12058624 | tf_op jit(solution)/shard_map/dot_general | solution.py:41
  100.4 12.8 %all-to-all-done.1 = bf16[128,16,512]{2,1,0:T(8,128)(2,1)} async-done(((bf16[128,16,512]{2,1,0:T(8,128)(2,1)}), bf16[128,16,512]{2,1,0:T(8,128)(2,1)}, u32[]{:S(2)}, u32[]{:S(2)}) %all-to-all-start.1) | async-done | bytes 2097184 | tf_op jit(solution)/shard_map/all_to_all | solution.py:1013
  113.2 5.6 %all-to-all-start.2 = ((bf16[128,16,512]{2,1,0:T(8,128)(2,1)}), bf16[128,16,512]{2,1,0:T(8,128)(2,1)}, u32[]{:S(2)}, u32[]{:S(2)}) async-start(bf16[128,16,512]{2,1,0:T(8,128)(2,1)} %bitcast.119), calls=%async_computation.2 | async-start | bytes 4194304 | tf_op jit(solution)/shard_map/all_to_all | solution.py:1013
  120.1 23.7 %expert.3 = (bf16[2048,512]{1,0:T(8,128)(2,1)}, bf16[256,4096]{1,0:T(8,128)(2,1)}, bf16[256,768]{1,0:T(8,128)(2,1)}, bf16[256,64]{1,0:T(8,128)(2,1)}, bf16[2,256...) custom-call(bf16[2048,512]{1,0:T(8,128)(2,1)} %bitcast.31.blocks_hbm, ...), custom_call_target="tpu_custom_call" | custom-call | flops 6442450944 | bytes 31457280 | tf_op jit(solution)/shard_map/expert/pallas_call | solution.py:875
  143.8 4.5 %all-to-all-done.2 = bf16[128,16,512]{2,1,0:T(8,128)(2,1)} async-done(((bf16[128,16,512]{2,1,0:T(8,128)(2,1)}), bf16[128,16,512]{2,1,0:T(8,128)(2,1)}, u32[]{:S(2)}, u32[]{:S(2)}) %all-to-all-start.2) | async-done | bytes 2097184 | tf_op jit(solution)/shard_map/all_to_all | solution.py:1013
  148.3 5.4 %all-to-all-start.4 = ((bf16[128,16,512]{2,1,0:T(8,128)(2,1)}), bf16[128,16,512]{2,1,0:T(8,128)(2,1)S(1)}, u32[]{:S(2)}, u32[]{:S(2)}) async-start(bf16[128,16,512]{2,1,0:T(8,128)(2,1)} %bitcast.120), calls=%async_computation.4 | async-start | bytes 4194304 | tf_op jit(solution)/shard_map/all_to_all | solution.py:1013
  153.7 23.7 %expert.2 = (bf16[2048,512]{1,0:T(8,128)(2,1)}, bf16[256,4096]{1,0:T(8,128)(2,1)}, bf16[256,768]{1,0:T(8,128)(2,1)}, bf16[256,64]{1,0:T(8,128)(2,1)}, bf16[2,256...) custom-call(bf16[2048,512]{1,0:T(8,128)(2,1)} %bitcast.33.blocks_hbm, ...), custom_call_target="tpu_custom_call" | custom-call | flops 6442450944 | bytes 31457280 | tf_op jit(solution)/shard_map/expert/pallas_call | solution.py:875
  177.4 6.0 %all-to-all-done.4 = bf16[128,16,512]{2,1,0:T(8,128)(2,1)S(1)} async-done(((bf16[128,16,512]{2,1,0:T(8,128)(2,1)}), bf16[128,16,512]{2,1,0:T(8,128)(2,1)S(1)}, u32[]{:S(2)}, u32[]{:S(2)}) %all-to-all-start.4) | async-done | bytes 2097184 | tf_op jit(solution)/shard_map/all_to_all | solution.py:1013
  183.4 5.8 %all-to-all-start.3 = ((bf16[128,16,512]{2,1,0:T(8,128)(2,1)}), bf16[128,16,512]{2,1,0:T(8,128)(2,1)}, u32[]{:S(2)}, u32[]{:S(2)}) async-start(bf16[128,16,512]{2,1,0:T(8,128)(2,1)} %bitcast.118), calls=%async_computation.3 | async-start | bytes 4194304 | tf_op jit(solution)/shard_map/all_to_all | solution.py:1013
  190.0 4.1 %combine_first.1.first_hbm = f32[8,128,512]{2,1,0:T(8,128)} custom-call(f32[128,128]{1,0:T(8,128)} %get-tuple-element.69.slots_ref, f32[128,128]{1,0:T(8,128)} %select_add_fusion.1.gates_ref, bf16[2048,512]{1,0:T(8,128)(2,1)} %bitcast.109), custom_call_target="tpu_custom_call" | custom-call | flops 1 | bytes 1 | tf_op jit(solution)/shard_map/combine_first/pallas_call | solution.py:696
  195.0 13.1 %expert_grads.1 = (f32[1,4096]{1,0:T(1,128)}, f32[32,4096]{1,0:T(8,128)}, f32[64,4096]{1,0:T(8,128)}, f32[32,768]{1,0:T(8,128)}, f32[2,32,768]{2,1,0:T(8,128)}) custom-call(bf16[512,4096]{1,0:T(8,128)(2,1)} %bitcast.108, f32[1,4096]{1,0:T(1,128)} %copy-done.8, bf16[768,4096]{1,0:T(8,128)(2,1)} %bitcast.110, bf16[32,4096]{1,0:T(8,128)(2,1)} %bitcast.126, ...), custom_call_target="tpu_custom_call" | custom-call | flops 1 | bytes 1 | tf_op jit(solution)/shard_map/expert_grads/pallas_call | solution.py:957
  211.6 7.1 %all-to-all-done.3 = bf16[128,16,512]{2,1,0:T(8,128)(2,1)} async-done(((bf16[128,16,512]{2,1,0:T(8,128)(2,1)}), bf16[128,16,512]{2,1,0:T(8,128)(2,1)}, u32[]{:S(2)}, u32[]{:S(2)}) %all-to-all-start.3) | async-done | bytes 2097184 | tf_op jit(solution)/shard_map/all_to_all | solution.py:1013
  218.7 5.6 %combine_last.1.grad_ref = bf16[128,4096]{1,0:T(8,128)(2,1)} custom-call(f32[128,128]{1,0:T(8,128)} %get-tuple-element.69.slots_ref, f32[128,128]{1,0:T(8,128)} %select_add_fusion.1.gates_ref, bf16[2048,512]{1,0:T(8,128)(2,1)} %bitcast.37.blocks_ref, f32[1,4096]{1,0:T(1,128)} %bitcast.160, f32[128,1]{1,0:T(8,128)} %get-tuple-element.76.rinv_ref, ...), custom_call_target="tpu_custom_call" | custom-call | flops 2147483648 | bytes 8388608 | tf_op jit(solution)/shard_map/combine_last/pallas_call | solution.py:720
  224.2 18.0 %finish.1 = (bf16[128,4096]{1,0:T(8,128)(2,1)}, bf16[128,512]{1,0:T(8,128)(2,1)}, f32[16,8,128]{2,1,0:T(8,128)}) custom-call(bf16[128,4096]{1,0:T(8,128)(2,1)} %bitcast.152, bf16[128,4096]{1,0:T(8,128)(2,1)} %combine_last.1.grad_ref, bf16[4,640,1024]{2,1,0:T(8,128)(2,1)} %get-tuple-element.94.prob_ref, ...), custom_call_target="tpu_custom_call" | custom-call | flops 2684354560 | bytes 10485760 | tf_op jit(solution)/shard_map/finish/pallas_call | solution.py:564
  (95 shorter events, 22.8 us)
Async XLA Ops:
  14.4 12.4 %copy-start.6 = (bf16[1,32,4096]{2,1,0:T(8,128)(2,1)S(1)}, bf16[1,32,4096]{2,1,0:T(8,128)(2,1)}, u32[]{:S(2)}) copy-start(bf16[1,32,4096]{2,1,0:T(8,128)(2,1)} %param.28) | copy-start | bytes 786436
  14.4 12.4 %copy-start.7 = (bf16[1,768,32]{1,2,0:T(8,128)(2,1)S(1)}, bf16[1,768,32]{1,2,0:T(8,128)(2,1)}, u32[]{:S(2)}) copy-start(bf16[1,768,32]{1,2,0:T(8,128)(2,1)} %param.27) | copy-start | bytes 147460
  14.4 63.9 %all-to-all-start = ((bf16[128,16,1024]{2,1,0:T(8,128)(2,1)}), bf16[128,16,1024]{2,1,0:T(8,128)(2,1)}, u32[]{:S(2)}, u32[]{:S(2)}) async-start(bf16[128,16,1024]{2,1,0:T(8,128)(2,1)} %bitcast.115), calls=%async_computation | async-start | bytes 8388608 | tf_op jit(solution)/shard_map/all_to_all | solution.py:1013
  26.8 4.9 %copy-start.3 = (bf16[1,2,4096,32]{2,3,1,0:T(8,128)(2,1)S(1)}, bf16[1,2,4096,32]{2,3,1,0:T(8,128)(2,1)}, u32[]{:S(2)}) copy-start(bf16[1,2,4096,32]{2,3,1,0:T(8,128)(2,1)} %param.23) | copy-start | bytes 1572868
  26.8 4.9 %copy-start.16 = (bf16[1,2,32,768]{3,2,1,0:T(8,128)(2,1)S(1)}, bf16[1,2,32,768]{3,2,1,0:T(8,128)(2,1)}, u32[]{:S(2)}) copy-start(bf16[1,2,32,768]{3,2,1,0:T(8,128)(2,1)} %param.24) | copy-start | bytes 294916
  26.8 9.2 %slice-start.2 = ((s8[12582912]{0:T(1024)(128)(4,1)}), s8[4194304]{0:T(1024)(128)(4,1)S(1)}, s32[]{:S(2)}) async-start(s8[12582912]{0:T(1024)(128)(4,1)} %bitcast.149), calls=%async_computation.7 | async-start | bytes 8388608
  26.9 9.2 %slice-start.3 = ((s8[12582912]{0:T(1024)(128)(4,1)}), s8[4194304]{0:T(1024)(128)(4,1)S(1)}, s32[]{:S(2)}) async-start(s8[12582912]{0:T(1024)(128)(4,1)} %bitcast.149), calls=%async_computation.8 | async-start | bytes 8388608
  38.5 15.1 %copy-start.11 = (f32[1,4096]{1,0:T(1,128)S(1)}, f32[1,4096]{1,0:T(1,128)}, u32[]{:S(2)}) copy-start(f32[1,4096]{1,0:T(1,128)} %param.29) | copy-start | bytes 49156
  38.5 15.2 %copy-start.12 = (f32[1,2,768]{2,1,0:T(2,128)S(1)}, f32[1,2,768]{2,1,0:T(2,128)}, u32[]{:S(2)}) copy-start(f32[1,2,768]{2,1,0:T(2,128)} %param.25) | copy-start | bytes 18436
  53.6 38.0 %copy-start.8 = (f32[1,4096]{1,0:T(1,128)}, f32[1,4096]{1,0:T(1,128)S(1)}, u32[]{:S(2)}) copy-start(f32[1,4096]{1,0:T(1,128)S(1)} %div.22.scale_ref) | copy-start | bytes 49156
  78.3 34.9 %all-to-all-start.1 = ((bf16[128,16,512]{2,1,0:T(8,128)(2,1)}), bf16[128,16,512]{2,1,0:T(8,128)(2,1)}, u32[]{:S(2)}, u32[]{:S(2)}) async-start(bf16[128,16,512]{2,1,0:T(8,128)(2,1)} %bitcast.121), calls=%async_computation.1 | async-start | bytes 4194304 | tf_op jit(solution)/shard_map/all_to_all | solution.py:1013
  83.8 12.5 %slice-start = ((s8[6291456]{0:T(1024)(128)(4,1)}), s8[2097152]{0:T(1024)(128)(4,1)S(1)}, s32[]{:S(2)}) async-start(s8[6291456]{0:T(1024)(128)(4,1)} %bitcast.111), calls=%async_computation.5 | async-start | bytes 4194304
  91.6 4.8 %slice-start.1 = ((s8[6291456]{0:T(1024)(128)(4,1)}), s8[4194304]{0:T(1024)(128)(4,1)S(1)}, s32[]{:S(2)}) async-start(s8[6291456]{0:T(1024)(128)(4,1)} %bitcast.111), calls=%async_computation.6 | async-start | bytes 8388608
  113.2 35.1 %all-to-all-start.2 = ((bf16[128,16,512]{2,1,0:T(8,128)(2,1)}), bf16[128,16,512]{2,1,0:T(8,128)(2,1)}, u32[]{:S(2)}, u32[]{:S(2)}) async-start(bf16[128,16,512]{2,1,0:T(8,128)(2,1)} %bitcast.119), calls=%async_computation.2 | async-start | bytes 4194304 | tf_op jit(solution)/shard_map/all_to_all | solution.py:1013
  148.3 35.1 %all-to-all-start.4 = ((bf16[128,16,512]{2,1,0:T(8,128)(2,1)}), bf16[128,16,512]{2,1,0:T(8,128)(2,1)S(1)}, u32[]{:S(2)}, u32[]{:S(2)}) async-start(bf16[128,16,512]{2,1,0:T(8,128)(2,1)} %bitcast.120), calls=%async_computation.4 | async-start | bytes 4194304 | tf_op jit(solution)/shard_map/all_to_all | solution.py:1013
  183.4 6.6 %copy-start = (bf16[128,16,512]{2,1,0:T(8,128)(2,1)}, bf16[128,16,512]{2,1,0:T(8,128)(2,1)S(1)}, u32[]{:S(2)}) copy-start(bf16[128,16,512]{2,1,0:T(8,128)(2,1)S(1)} %all-to-all-done.4) | copy-start | bytes 6291460
  183.4 10.7 %copy-start.4 = (bf16[256,768]{1,0:T(8,128)(2,1)S(1)}, bf16[256,768]{1,0:T(8,128)(2,1)}, u32[]{:S(2)}) copy-start(bf16[256,768]{1,0:T(8,128)(2,1)} %get-tuple-element.100) | copy-start | bytes 1179652
  183.4 10.7 %copy-start.5 = (bf16[256,768]{1,0:T(8,128)(2,1)S(1)}, bf16[256,768]{1,0:T(8,128)(2,1)}, u32[]{:S(2)}) copy-start(bf16[256,768]{1,0:T(8,128)(2,1)} %get-tuple-element.101) | copy-start | bytes 1179652
  183.4 35.3 %all-to-all-start.3 = ((bf16[128,16,512]{2,1,0:T(8,128)(2,1)}), bf16[128,16,512]{2,1,0:T(8,128)(2,1)}, u32[]{:S(2)}, u32[]{:S(2)}) async-start(bf16[128,16,512]{2,1,0:T(8,128)(2,1)} %bitcast.118), calls=%async_computation.3 | async-start | bytes 4194304 | tf_op jit(solution)/shard_map/all_to_all | solution.py:1013
  195.0 13.1 %copy-start.9 = (f32[256,1]{1,0:T(8,128)S(1)}, f32[256,1]{1,0:T(8,128)}, u32[]{:S(2)}) copy-start(f32[256,1]{1,0:T(8,128)} %get-tuple-element.95) | copy-start | bytes 3076
  195.0 13.2 %copy-start.10 = (f32[256,1]{1,0:T(8,128)S(1)}, f32[256,1]{1,0:T(8,128)}, u32[]{:S(2)}) copy-start(f32[256,1]{1,0:T(8,128)} %get-tuple-element.96) | copy-start | bytes 3076
  195.0 15.9 %copy-start.13 = (f32[2,768]{1,0:T(2,128)S(1)}, f32[2,768]{1,0:T(2,128)}, u32[]{:S(2)}) copy-start(f32[2,768]{1,0:T(2,128)} %get-tuple-element.112) | copy-start | bytes 18436
  195.0 15.9 %copy-start.14 = (f32[2,768]{1,0:T(2,128)S(1)}, f32[2,768]{1,0:T(2,128)}, u32[]{:S(2)}) copy-start(f32[2,768]{1,0:T(2,128)} %get-tuple-element.113) | copy-start | bytes 18436
  224.2 21.5 %copy-start.1 = (f32[128,128]{1,0:T(8,128)S(1)}, f32[128,128]{1,0:T(8,128)}, u32[]{:S(2)}) copy-start(f32[128,128]{1,0:T(8,128)} %get-tuple-element.69.slots_ref) | copy-start | bytes 196612
  (4 other events, 14.8 us)

commit v4 on v3

--- a/solution.py
+++ b/solution.py
@@ -157,8 +157,8 @@
 
 
 def open_kernel(
-    count, own_ref, slots_ref, rows_ref, seen_ref, out_hbm, stack, blocks, send_sem, recv_sem,
-    own_sem, out_sem,
+    count, own_ref, slots_ref, rows_ref, seen_ref, out_hbm, stack, blocks, wanted, masks,
+    send_sem, recv_sem, own_sem, out_sem,
 ):
     tokens, width = rows_ref.shape
     pieces = BLOCK // CAP
@@ -230,6 +230,10 @@
     spread = (iota((GROUP, PER_GROUP), 0) // BLOCK == iota((GROUP, PER_GROUP), 1)).astype(F32)
     spread = spread.astype(BF16)
     row = iota((GROUP, tokens), 0)
+    wanted[...] = (row % CAP).astype(F32)
+    for p in range(pieces):
+        own = (row // CAP) % pieces == p
+        masks[:, p * tokens : (p + 1) * tokens] = own.astype(F32).astype(BF16)
 
     def store(g):
         rows = pl.ds(pl.multiple_of(g * GROUP, GROUP), GROUP)
@@ -237,17 +241,14 @@
 
     def pick(g, _):
         named = slots_ref[pl.ds(pl.multiple_of(g * PER_GROUP, PER_GROUP), PER_GROUP), :]
-        hit = dot(spread, named.astype(BF16)) == (row % CAP).astype(F32)
-        parts = []
-        for p in range(pieces):
-            own = hit & ((row // CAP) % pieces == p)
-            parts.append(jnp.where(own, 1.0, 0.0).astype(BF16))
+        hit = jnp.where(dot(spread, named.astype(BF16)) == wanted[...], 1.0, 0.0).astype(BF16)
+        picker = jnp.concatenate([hit] * pieces, axis=1) * masks[...]
         rows = pl.ds(pl.multiple_of(g * GROUP, GROUP), GROUP)
-        blocks[rows, :] = dot(jnp.concatenate(parts, axis=1), stack[...]).astype(BF16)
+        blocks[rows, :] = dot(picker, stack[...]).astype(BF16)
         store(g).start()
         return 0
 
-    lax.fori_loop(0, groups, pick, 0)
+    lax.fori_loop(0, groups // 2, pick, 0)
 
     @pl.when(me >= 2)
     def _():
@@ -260,6 +261,8 @@
         @pl.when(core == 1)
         def _():
             near_odd.start()
+
+    lax.fori_loop(groups // 2, groups, pick, 0)
 
     @pl.when(me >= 4)
     def _():
@@ -319,6 +322,8 @@
         scratch_shapes=[
             pltpu.VMEM((BLOCK // CAP * tokens, piece), BF16),
             pltpu.VMEM((total, piece), BF16),
+            pltpu.VMEM((GROUP, tokens), F32),
+            pltpu.VMEM((GROUP, BLOCK // CAP * tokens), BF16),
             pltpu.SemaphoreType.DMA((5,)),
             pltpu.SemaphoreType.DMA((5,)),
             pltpu.SemaphoreType.DMA,
@@ -527,7 +532,8 @@
         for d in range(1, ep_count):
             along_ep(d).wait_send()
             along_ep(d).wait_recv()
-        returned_ref[...] = arrived[...]
+        by_expert = jnp.concatenate([arrived[:, c, :] for c in range(count)], axis=0)
+        returned_ref[...] = by_expert.T[: returned_ref.shape[0], :]
         for m in range(landed.shape[1]):
             for part in (1, 0):
                 for j in range(1, REACH + 1):
@@ -575,12 +581,12 @@
         out_specs=[
             rows,
             pl.BlockSpec((tokens, keyval.shape[1]), lambda i: (0, 0)),
-            pl.BlockSpec((ep_count, count, lanes), lambda i: (0, 0, 0)),
+            pl.BlockSpec((8, count * ep_count), lambda i: (0, 0)),
         ],
         out_shape=[
             jax.ShapeDtypeStruct((tokens, width), BF16),
             jax.ShapeDtypeStruct((tokens, keyval.shape[1]), BF16),
-            jax.ShapeDtypeStruct((ep_count, count, lanes), F32),
+            jax.ShapeDtypeStruct((8, count * ep_count), F32),
         ],
         scratch_shapes=[
             pltpu.VMEM((window, HEAD), F32),
@@ -598,7 +604,7 @@
             pltpu.SemaphoreType.DMA((ep_count - 1,)),
         ],
         compiler_params=pltpu.CompilerParams(
-            collective_id=1, has_side_effects=True, vmem_limit_bytes=60 * MB
+            collective_id=1, has_side_effects=True, vmem_limit_bytes=50 * MB
         ),
         cost_estimate=cost(8 * tokens * width * window, 10 * MB),
         name="finish",
@@ -739,7 +745,7 @@
             pltpu.VMEM(hidden.shape, BF16),
             pltpu.SemaphoreType.DMA((3,)),
         ],
-        compiler_params=params(60),
+        compiler_params=params(50),
         cost_estimate=cost(2 * total * tokens * width, 8 * MB),
         name="combine_last",
     )(slots, gates, blocks, gain, rinv, first, grad_out, hidden)
@@ -1091,11 +1097,10 @@
     )
     grad_query, grad_keyval, arrived_products = finish(query, grad_heads, prob, seen, products)
     grad_query = (grad_query.astype(F32) * HEAD ** (-0.5)).astype(BF16)
-    returned_products = arrived_products.transpose(1, 0, 2).reshape(experts, HEAD)
     dense_products = jnp.zeros((tokens, experts), F32)
     for r in range(CAP):
         dense_products = dense_products + jnp.where(
-            token_slots == r, returned_products[:, r][None, :], 0.0
+            token_slots == r, arrived_products[r][None, :], 0.0
         )
     grad_gate = jnp.stack(
         [jnp.sum(jnp.where(chosen[k], dense_products, 0.0), axis=1) for k in range(top)], axis=1

time: 249 us -> 247 us (level)
    unnamed x53 -> x67, local copies, waits for them, and re-layouts: 4.71 us -> 5.04 us
  transfers between devices with their start and end apart: 5 -> 5, of which waited for: 5 -> 5; matrix products, arithmetic and copies ran while one was open for 13% -> 12% of each run, Pallas kernels for 38% -> 39%
where the time goes in v4:
time: 247 us; the launch traced here: 245 us
  Pallas kernels  128 us (52%)
  waiting for transfers between devices  43.5 us (18%)
  starting transfers between devices  36.4 us (15%)
  matrix products  16.8 us (7%)
  other arithmetic  12.6 us (5%)
  local copies, waits for them, and re-layouts  7.05 us (3%)
    pallas_call x2, Pallas kernels, expert(): pl.pallas_call(functools.partial(expert_kernel, slots), in_specs=[hbm, hb...  47.4 us
    all_to_all x5, waiting for transfers between devices, exchange(): moved = lax.all_to_all(split, axes, split_axis=0, concat_axis=0, tiled=True)  43.5 us
    all_to_all x5, starting transfers between devices, exchange(): moved = lax.all_to_all(split, axes, split_axis=0, concat_axis=0, tiled=True)  36.4 us
    pallas_call x1, Pallas kernels, finish(): pl.pallas_call(functools.partial(finish_kernel, heads, steps_per_kv, coun...  16.9 us
    pallas_call x1, Pallas kernels, attend(): pl.pallas_call(functools.partial(attend_kernel, heads, per_kv), grid=(ste...  13.2 us
    pallas_call x1, Pallas kernels, expert_grads(): pl.pallas_call(functools.partial(expert_grads_kernel, halves), grid=(widt...  13.1 us
    pallas_call x1, Pallas kernels, open_exchange(): pl.pallas_call(functools.partial(open_kernel, count), in_specs=[vmem] * 3...  12.2 us
    dot_general x4, matrix products, dot(): return jnp.dot(left, right, preferred_element_type=F32)  11.6 us
  transfers between devices with their start and end apart: 5, of which 5 were waited for; matrix products, arithmetic and copies ran while one was open for 12% of the time, Pallas kernels for 39%

profile of v4, /device:TPU:1, one launch (start us, length us, event | category | flops | bytes accessed | tf_op | source)
XLA Modules:
  0.0 245.4 jit_solution(2521209209157136309)
XLA Ops:
  2.3 12.2 %open_exchange.1 = (bf16[640,512]{1,0:T(8,128)(2,1)}, bf16[2048,1024]{1,0:T(8,128)(2,1)}) custom-call(bf16[128,512]{1,0:T(8,128)(2,1)} %bitcast.141, f32[128,128]{1,0:T(8,128)} %get-tuple-element.162.slots_ref, bf16[128,4096]{1,0:T(8,128)(2,1)} %bitcast.114), custom_call_target="tpu_custom_call" | custom-call | tf_op jit(solution)/shard_map/open_exchange/pallas_call | solution.py:314
  14.5 14.2 %all-to-all-start = ((bf16[128,16,1024]{2,1,0:T(8,128)(2,1)}), bf16[128,16,1024]{2,1,0:T(8,128)(2,1)}, u32[]{:S(2)}, u32[]{:S(2)}) async-start(bf16[128,16,1024]{2,1,0:T(8,128)(2,1)} %bitcast.129), calls=%async_computation | async-start | bytes 8388608 | tf_op jit(solution)/shard_map/all_to_all | solution.py:1019
  28.8 4.8 %multiply_reduce_fusion = f32[4096]{0:T(1024)S(1)} fusion(bf16[1,768,32]{1,2,0:T(8,128)(2,1)S(1)} %copy-done.14, bf16[1,32,4096]{2,1,0:T(8,128)(2,1)S(1)} %copy-done.13, bf16[1,768,4096]{2,1,0:T(8,128)(2,1)} %param.26), kind=kOutput, calls=%fused_computation.6 | convolution fusion | flops 213905408 | bytes 6619136 | tf_op jit(solution)/shard_map/dot_general | solution.py:37
  33.7 4.3 %fusion.1 = f32[768]{0:T(1024)S(1)} fusion(bf16[1,2,4096,768]{3,2,1,0:T(8,128)(2,1)} %param.22, bf16[1,2,32,768]{3,2,1,0:T(8,128)(2,1)S(1)} %copy-done.23, bf16[1,2,4096,32]{2,3,1,0:T(8,128)(2,1)S(1)} %copy-done.10), kind=kOutput, calls=%fused_computation.2 | convolution fusion | flops 213908736 | bytes 6605824 | tf_op jit(solution)/shard_map/dot_general | solution.py:37
  42.2 13.2 %attend.1 = (bf16[4,640,1024]{2,1,0:T(8,128)(2,1)}, bf16[128,4096]{1,0:T(8,128)(2,1)}) custom-call(s32[6]{0:T(128)} %pad_add_fusion.place_ref, bf16[128,4096]{1,0:T(8,128)(2,1)} %bitcast.118, bf16[640,512]{1,0:T(8,128)(2,1)} %get-tuple-element.63.keyval_ref.keys_ref.values_ref), custom_call_target="tpu_custom_call" | custom-call | flops 1342177280 | bytes 9437184 | tf_op jit(solution)/shard_map/attend/pallas_call | solution.py:399
  57.0 9.2 %dispatch.1 = (bf16[2048,512]{1,0:T(8,128)(2,1)}, bf16[2048,512]{1,0:T(8,128)(2,1)}, f32[128,1]{1,0:T(8,128)}) custom-call(f32[128,128]{1,0:T(8,128)} %get-tuple-element.162.slots_ref, bf16[128,4096]{1,0:T(8,128)(2,1)} %get-tuple-element.93.rows_ref.hidden_hbm, f32[1,4096]{1,0:T(1,128)} %bitcast.120), custom_call_target="tpu_custom_call" | custom-call | flops 4294967296 | bytes 10485760 | tf_op jit(solution)/shard_map/dispatch/pallas_call | solution.py:111
  67.7 12.5 %all-to-all-done = bf16[128,16,1024]{2,1,0:T(8,128)(2,1)} async-done(((bf16[128,16,1024]{2,1,0:T(8,128)(2,1)}), bf16[128,16,1024]{2,1,0:T(8,128)(2,1)}, u32[]{:S(2)}, u32[]{:S(2)}) %all-to-all-start) | async-done | bytes 4194336 | tf_op jit(solution)/shard_map/all_to_all | solution.py:1019
  80.3 5.5 %all-to-all-start.1 = ((bf16[128,16,512]{2,1,0:T(8,128)(2,1)}), bf16[128,16,512]{2,1,0:T(8,128)(2,1)}, u32[]{:S(2)}, u32[]{:S(2)}) async-start(bf16[128,16,512]{2,1,0:T(8,128)(2,1)} %bitcast.135), calls=%async_computation.1 | async-start | bytes 4194304 | tf_op jit(solution)/shard_map/all_to_all | solution.py:1019
  85.8 7.8 %unpack.1 = bf16[2,256,4096]{2,1,0:T(8,128)(2,1)} custom-call(bf16[2048,1024]{1,0:T(8,128)(2,1)} %bitcast.12.blocks_ref), custom_call_target="tpu_custom_call" | custom-call | flops 1073741824 | bytes 8388608 | tf_op jit(solution)/shard_map/unpack/pallas_call | solution.py:145
  93.6 3.5 %multiply_convert_fusion = bf16[2,256,4096]{2,1,0:T(8,128)(2,1)S(1)} fusion(bf16[2,256,4096]{2,1,0:T(8,128)(2,1)} %unpack.1, f32[4096]{0:T(1024)S(1)} %bitcast.138), kind=kLoop, calls=%fused_computation.7 | loop fusion | flops 6291456 | bytes 8404992 | tf_op jit(solution)/shard_map/convert_element_type | solution.py:1058
  98.5 3.6 %fusion.28 = f32[512,768]{1,0:T(8,128)S(1)} fusion(bf16[512,4096]{1,0:T(8,128)(2,1)S(1)} %bitcast.131, bf16[1,768,4096]{2,1,0:T(8,128)(2,1)S(1)} %bitcast.126), kind=kOutput, calls=%fused_computation.73 | convolution fusion | flops 3221225472 | bytes 12058624 | tf_op jit(solution)/shard_map/dot_general | solution.py:41
  102.4 12.7 %all-to-all-done.1 = bf16[128,16,512]{2,1,0:T(8,128)(2,1)} async-done(((bf16[128,16,512]{2,1,0:T(8,128)(2,1)}), bf16[128,16,512]{2,1,0:T(8,128)(2,1)}, u32[]{:S(2)}, u32[]{:S(2)}) %all-to-all-start.1) | async-done | bytes 2097184 | tf_op jit(solution)/shard_map/all_to_all | solution.py:1019
  115.1 5.6 %all-to-all-start.2 = ((bf16[128,16,512]{2,1,0:T(8,128)(2,1)}), bf16[128,16,512]{2,1,0:T(8,128)(2,1)}, u32[]{:S(2)}, u32[]{:S(2)}) async-start(bf16[128,16,512]{2,1,0:T(8,128)(2,1)} %bitcast.133), calls=%async_computation.2 | async-start | bytes 4194304 | tf_op jit(solution)/shard_map/all_to_all | solution.py:1019
  122.0 23.7 %expert.3 = (bf16[2048,512]{1,0:T(8,128)(2,1)}, bf16[256,4096]{1,0:T(8,128)(2,1)}, bf16[256,768]{1,0:T(8,128)(2,1)}, bf16[256,64]{1,0:T(8,128)(2,1)}, bf16[2,256...) custom-call(bf16[2048,512]{1,0:T(8,128)(2,1)} %bitcast.31.blocks_hbm, ...), custom_call_target="tpu_custom_call" | custom-call | flops 6442450944 | bytes 31457280 | tf_op jit(solution)/shard_map/expert/pallas_call | solution.py:881
  145.7 4.5 %all-to-all-done.2 = bf16[128,16,512]{2,1,0:T(8,128)(2,1)} async-done(((bf16[128,16,512]{2,1,0:T(8,128)(2,1)}), bf16[128,16,512]{2,1,0:T(8,128)(2,1)}, u32[]{:S(2)}, u32[]{:S(2)}) %all-to-all-start.2) | async-done | bytes 2097184 | tf_op jit(solution)/shard_map/all_to_all | solution.py:1019
  150.2 5.4 %all-to-all-start.4 = ((bf16[128,16,512]{2,1,0:T(8,128)(2,1)}), bf16[128,16,512]{2,1,0:T(8,128)(2,1)S(1)}, u32[]{:S(2)}, u32[]{:S(2)}) async-start(bf16[128,16,512]{2,1,0:T(8,128)(2,1)} %bitcast.134), calls=%async_computation.4 | async-start | bytes 4194304 | tf_op jit(solution)/shard_map/all_to_all | solution.py:1019
  155.6 23.7 %expert.2 = (bf16[2048,512]{1,0:T(8,128)(2,1)}, bf16[256,4096]{1,0:T(8,128)(2,1)}, bf16[256,768]{1,0:T(8,128)(2,1)}, bf16[256,64]{1,0:T(8,128)(2,1)}, bf16[2,256...) custom-call(bf16[2048,512]{1,0:T(8,128)(2,1)} %bitcast.33.blocks_hbm, ...), custom_call_target="tpu_custom_call" | custom-call | flops 6442450944 | bytes 31457280 | tf_op jit(solution)/shard_map/expert/pallas_call | solution.py:881
  179.3 6.0 %all-to-all-done.4 = bf16[128,16,512]{2,1,0:T(8,128)(2,1)S(1)} async-done(((bf16[128,16,512]{2,1,0:T(8,128)(2,1)}), bf16[128,16,512]{2,1,0:T(8,128)(2,1)S(1)}, u32[]{:S(2)}, u32[]{:S(2)}) %all-to-all-start.4) | async-done | bytes 2097184 | tf_op jit(solution)/shard_map/all_to_all | solution.py:1019
  185.3 5.8 %all-to-all-start.3 = ((bf16[128,16,512]{2,1,0:T(8,128)(2,1)}), bf16[128,16,512]{2,1,0:T(8,128)(2,1)}, u32[]{:S(2)}, u32[]{:S(2)}) async-start(bf16[128,16,512]{2,1,0:T(8,128)(2,1)} %bitcast.132), calls=%async_computation.3 | async-start | bytes 4194304 | tf_op jit(solution)/shard_map/all_to_all | solution.py:1019
  191.9 4.0 %combine_first.1.first_hbm = f32[8,128,512]{2,1,0:T(8,128)} custom-call(f32[128,128]{1,0:T(8,128)} %get-tuple-element.69.slots_ref, f32[128,128]{1,0:T(8,128)} %select_add_fusion.1.gates_ref, bf16[2048,512]{1,0:T(8,128)(2,1)} %bitcast.123), custom_call_target="tpu_custom_call" | custom-call | flops 1 | bytes 1 | tf_op jit(solution)/shard_map/combine_first/pallas_call | solution.py:702
  196.9 13.1 %expert_grads.1 = (f32[1,4096]{1,0:T(1,128)}, f32[32,4096]{1,0:T(8,128)}, f32[64,4096]{1,0:T(8,128)}, f32[32,768]{1,0:T(8,128)}, f32[2,32,768]{2,1,0:T(8,128)}) custom-call(bf16[512,4096]{1,0:T(8,128)(2,1)} %bitcast.122, f32[1,4096]{1,0:T(1,128)} %copy-done.15, bf16[768,4096]{1,0:T(8,128)(2,1)} %bitcast.124, bf16[32,4096]{1,0:T(8,128)(2,1)} %bitcast.137, ...), custom_call_target="tpu_custom_call" | custom-call | flops 1 | bytes 1 | tf_op jit(solution)/shard_map/expert_grads/pallas_call | solution.py:963
  212.9 7.7 %all-to-all-done.3 = bf16[128,16,512]{2,1,0:T(8,128)(2,1)} async-done(((bf16[128,16,512]{2,1,0:T(8,128)(2,1)}), bf16[128,16,512]{2,1,0:T(8,128)(2,1)}, u32[]{:S(2)}, u32[]{:S(2)}) %all-to-all-start.3) | async-done | bytes 2097184 | tf_op jit(solution)/shard_map/all_to_all | solution.py:1019
  221.8 4.0 %combine_last.1.grad_ref = bf16[128,4096]{1,0:T(8,128)(2,1)S(1)} custom-call(f32[128,128]{1,0:T(8,128)S(1)} %copy-done.1, f32[128,128]{1,0:T(8,128)S(1)} %copy-done.2, bf16[2048,512]{1,0:T(8,128)(2,1)} %bitcast.37.blocks_ref, f32[1,4096]{1,0:T(1,128)S(1)} %bitcast.121, f32[128,1]{1,0:T(8,128)S(1)} %copy-done.7, f32[8,128,512]{2,1,0:T(8,128)} %combine_first.1.first_hbm, ...), custom_call_target="tpu_custom_call" | custom-call | flops 2147483648 | bytes 8388608 | tf_op jit(solution)/shard_map/combine_last/pallas_call | solution.py:726
  225.9 16.9 %finish.1 = (bf16[128,4096]{1,0:T(8,128)(2,1)S(1)}, bf16[128,512]{1,0:T(8,128)(2,1)S(1)}, f32[8,128]{1,0:T(8,128)S(1)}) custom-call(bf16[128,4096]{1,0:T(8,128)(2,1)S(1)} %bitcast.119, bf16[128,4096]{1,0:T(8,128)(2,1)S(1)} %combine_last.1.grad_ref, bf16[4,640,1024]{2,1,0:T(8,128)(2,1)} %get-tuple-element.94.prob_ref, bf16[640,512]{1,0:T(8,128)(2,1)S(1)} %copy-done.4, ...), custom_call_target="tpu_custom_call" | custom-call | flops 2684354560 | bytes 10485760 | tf_op jit(solution)/shard_map/finish/pallas_call | solution.py:570
  (108 shorter events, 20.1 us)
Async XLA Ops:
  14.5 14.2 %copy-start.13 = (bf16[1,32,4096]{2,1,0:T(8,128)(2,1)S(1)}, bf16[1,32,4096]{2,1,0:T(8,128)(2,1)}, u32[]{:S(2)}) copy-start(bf16[1,32,4096]{2,1,0:T(8,128)(2,1)} %param.28) | copy-start | bytes 786436
  14.5 14.2 %copy-start.14 = (bf16[1,768,32]{1,2,0:T(8,128)(2,1)S(1)}, bf16[1,768,32]{1,2,0:T(8,128)(2,1)}, u32[]{:S(2)}) copy-start(bf16[1,768,32]{1,2,0:T(8,128)(2,1)} %param.27) | copy-start | bytes 147460
  14.5 65.7 %all-to-all-start = ((bf16[128,16,1024]{2,1,0:T(8,128)(2,1)}), bf16[128,16,1024]{2,1,0:T(8,128)(2,1)}, u32[]{:S(2)}, u32[]{:S(2)}) async-start(bf16[128,16,1024]{2,1,0:T(8,128)(2,1)} %bitcast.129), calls=%async_computation | async-start | bytes 8388608 | tf_op jit(solution)/shard_map/all_to_all | solution.py:1019
  40.4 15.1 %copy-start.18 = (f32[1,4096]{1,0:T(1,128)S(1)}, f32[1,4096]{1,0:T(1,128)}, u32[]{:S(2)}) copy-start(f32[1,4096]{1,0:T(1,128)} %param.29) | copy-start | bytes 49156
  40.4 15.2 %copy-start.19 = (f32[1,2,768]{2,1,0:T(2,128)S(1)}, f32[1,2,768]{2,1,0:T(2,128)}, u32[]{:S(2)}) copy-start(f32[1,2,768]{2,1,0:T(2,128)} %param.25) | copy-start | bytes 18436
  55.5 38.1 %copy-start.15 = (f32[1,4096]{1,0:T(1,128)}, f32[1,4096]{1,0:T(1,128)S(1)}, u32[]{:S(2)}) copy-start(f32[1,4096]{1,0:T(1,128)S(1)} %div.22.scale_ref) | copy-start | bytes 49156
  80.3 34.9 %all-to-all-start.1 = ((bf16[128,16,512]{2,1,0:T(8,128)(2,1)}), bf16[128,16,512]{2,1,0:T(8,128)(2,1)}, u32[]{:S(2)}, u32[]{:S(2)}) async-start(bf16[128,16,512]{2,1,0:T(8,128)(2,1)} %bitcast.135), calls=%async_computation.1 | async-start | bytes 4194304 | tf_op jit(solution)/shard_map/all_to_all | solution.py:1019
  85.8 12.6 %slice-start = ((s8[6291456]{0:T(1024)(128)(4,1)}), s8[2097152]{0:T(1024)(128)(4,1)S(1)}, s32[]{:S(2)}) async-start(s8[6291456]{0:T(1024)(128)(4,1)} %bitcast.125), calls=%async_computation.5 | async-start | bytes 4194304
  115.1 35.1 %all-to-all-start.2 = ((bf16[128,16,512]{2,1,0:T(8,128)(2,1)}), bf16[128,16,512]{2,1,0:T(8,128)(2,1)}, u32[]{:S(2)}, u32[]{:S(2)}) async-start(bf16[128,16,512]{2,1,0:T(8,128)(2,1)} %bitcast.133), calls=%async_computation.2 | async-start | bytes 4194304 | tf_op jit(solution)/shard_map/all_to_all | solution.py:1019
  150.2 35.1 %all-to-all-start.4 = ((bf16[128,16,512]{2,1,0:T(8,128)(2,1)}), bf16[128,16,512]{2,1,0:T(8,128)(2,1)S(1)}, u32[]{:S(2)}, u32[]{:S(2)}) async-start(bf16[128,16,512]{2,1,0:T(8,128)(2,1)} %bitcast.134), calls=%async_computation.4 | async-start | bytes 4194304 | tf_op jit(solution)/shard_map/all_to_all | solution.py:1019
  185.3 10.6 %copy-start.11 = (bf16[256,768]{1,0:T(8,128)(2,1)S(1)}, bf16[256,768]{1,0:T(8,128)(2,1)}, u32[]{:S(2)}) copy-start(bf16[256,768]{1,0:T(8,128)(2,1)} %get-tuple-element.100) | copy-start | bytes 1179652
  185.3 10.6 %copy-start.12 = (bf16[256,768]{1,0:T(8,128)(2,1)S(1)}, bf16[256,768]{1,0:T(8,128)(2,1)}, u32[]{:S(2)}) copy-start(bf16[256,768]{1,0:T(8,128)(2,1)} %get-tuple-element.101) | copy-start | bytes 1179652
  185.3 35.3 %all-to-all-start.3 = ((bf16[128,16,512]{2,1,0:T(8,128)(2,1)}), bf16[128,16,512]{2,1,0:T(8,128)(2,1)}, u32[]{:S(2)}, u32[]{:S(2)}) async-start(bf16[128,16,512]{2,1,0:T(8,128)(2,1)} %bitcast.132), calls=%async_computation.3 | async-start | bytes 4194304 | tf_op jit(solution)/shard_map/all_to_all | solution.py:1019
  196.9 13.2 %copy-start.16 = (f32[256,1]{1,0:T(8,128)S(1)}, f32[256,1]{1,0:T(8,128)}, u32[]{:S(2)}) copy-start(f32[256,1]{1,0:T(8,128)} %get-tuple-element.95) | copy-start | bytes 3076
  196.9 13.2 %copy-start.17 = (f32[256,1]{1,0:T(8,128)S(1)}, f32[256,1]{1,0:T(8,128)}, u32[]{:S(2)}) copy-start(f32[256,1]{1,0:T(8,128)} %get-tuple-element.96) | copy-start | bytes 3076
  196.9 15.4 %copy-start.20 = (f32[2,768]{1,0:T(2,128)S(1)}, f32[2,768]{1,0:T(2,128)}, u32[]{:S(2)}) copy-start(f32[2,768]{1,0:T(2,128)} %get-tuple-element.112) | copy-start | bytes 18436
  196.9 15.4 %copy-start.21 = (f32[2,768]{1,0:T(2,128)S(1)}, f32[2,768]{1,0:T(2,128)}, u32[]{:S(2)}) copy-start(f32[2,768]{1,0:T(2,128)} %get-tuple-element.113) | copy-start | bytes 18436
  196.9 23.7 %copy-start = (bf16[1,128,4096]{2,1,0:T(8,128)(2,1)S(1)}, bf16[1,128,4096]{2,1,0:T(8,128)(2,1)}, u32[]{:S(2)}) copy-start(bf16[1,128,4096]{2,1,0:T(8,128)(2,1)} %param.21) | copy-start | bytes 3145732
  196.9 23.7 %copy-start.1 = (f32[128,128]{1,0:T(8,128)S(1)}, f32[128,128]{1,0:T(8,128)}, u32[]{:S(2)}) copy-start(f32[128,128]{1,0:T(8,128)} %get-tuple-element.69.slots_ref) | copy-start | bytes 196612
  196.9 23.7 %copy-start.2 = (f32[128,128]{1,0:T(8,128)S(1)}, f32[128,128]{1,0:T(8,128)}, u32[]{:S(2)}) copy-start(f32[128,128]{1,0:T(8,128)} %select_add_fusion.1.gates_ref) | copy-start | bytes 196612
  196.9 23.7 %copy-start.5 = (f32[4096]{0:T(1024)S(1)}, f32[4096]{0:T(1024)}, u32[]{:S(2)}) copy-start(f32[4096]{0:T(1024)} %param.18) | copy-start | bytes 49156
  196.9 23.7 %copy-start.7 = (f32[128,1]{1,0:T(8,128)S(1)}, f32[128,1]{1,0:T(8,128)}, u32[]{:S(2)}) copy-start(f32[128,1]{1,0:T(8,128)} %get-tuple-element.76.rinv_ref) | copy-start | bytes 1540
  210.3 15.6 %copy-start.3 = (bf16[1,128,4096]{2,1,0:T(8,128)(2,1)S(1)}, bf16[1,128,4096]{2,1,0:T(8,128)(2,1)}, u32[]{:S(2)}) copy-start(bf16[1,128,4096]{2,1,0:T(8,128)(2,1)} %param.15) | copy-start | bytes 3145732
  210.3 15.6 %copy-start.4 = (bf16[640,512]{1,0:T(8,128)(2,1)S(1)}, bf16[640,512]{1,0:T(8,128)(2,1)}, u32[]{:S(2)}) copy-start(bf16[640,512]{1,0:T(8,128)(2,1)} %get-tuple-element.63.keyval_ref.keys_ref.values_ref) | copy-start | bytes 1966084
  (11 other events, 55.6 us)

commit v5 on v4

--- a/solution.py
+++ b/solution.py
@@ -157,7 +157,7 @@
 
 
 def open_kernel(
-    count, own_ref, slots_ref, rows_ref, seen_ref, out_hbm, stack, blocks, wanted, masks,
+    count, own_ref, ids_ref, rows_ref, seen_ref, out_hbm, slots_ref, token_slots_ref, stack, blocks, wanted, masks,
     send_sem, recv_sem, own_sem, out_sem,
 ):
     tokens, width = rows_ref.shape
@@ -203,6 +203,16 @@
             )
 
     pl.semaphore_signal(barrier, inc=1, device_id={"ctx": other}, device_id_type=MESH)
+
+    experts = slots_ref.shape[0]
+    named = jnp.zeros((tokens, experts), F32)
+    for k in range(ids_ref.shape[1]):
+        named = named + (ids_ref[:, k : k + 1] == iota((tokens, experts), 1)).astype(F32)
+    earlier = (iota((tokens, tokens), 1) < iota((tokens, tokens), 0)).astype(F32).astype(BF16)
+    token_slots = jnp.where(named > 0.0, dot(earlier, named.astype(BF16)), -1.0)
+    token_slots_ref[...] = token_slots
+    slots_ref[...] = token_slots.T
+
     pl.semaphore_wait(barrier, peers)
 
     @pl.when(me + 4 < count)
@@ -306,18 +316,20 @@
         store(g).wait()
 
 
-def open_exchange(own, slots, rows, count):
-    experts, tokens = slots.shape
+def open_exchange(own, ids, rows, experts, count):
+    tokens = ids.shape[0]
     total = experts * BLOCK
     piece = rows.shape[1] * CAP // BLOCK
     vmem = pl.BlockSpec(memory_space=pltpu.VMEM)
     return pl.pallas_call(
         functools.partial(open_kernel, count),
         in_specs=[vmem] * 3,
-        out_specs=[vmem, pl.BlockSpec(memory_space=pl.ANY)],
+        out_specs=[vmem, pl.BlockSpec(memory_space=pl.ANY), vmem, vmem],
         out_shape=[
             jax.ShapeDtypeStruct(((REACH + 1) * tokens, own.shape[1]), own.dtype),
             jax.ShapeDtypeStruct((total, piece), BF16),
+            jax.ShapeDtypeStruct((experts, tokens), F32),
+            jax.ShapeDtypeStruct((tokens, experts), F32),
         ],
         scratch_shapes=[
             pltpu.VMEM((BLOCK // CAP * tokens, piece), BF16),
@@ -333,7 +345,7 @@
             collective_id=0, has_side_effects=True, vmem_limit_bytes=60 * MB
         ),
         name="open_exchange",
-    )(own, slots, rows)
+    )(own, ids, rows)
 
 
 def visible(place_ref, window, tokens):
@@ -1019,15 +1031,11 @@
         moved = lax.all_to_all(split, axes, split_axis=0, concat_axis=0, tiled=True)
         return moved.reshape(blocks.shape)
 
-    named = jnp.zeros((experts, tokens), jnp.bool_)
     each = jnp.arange(experts, dtype=jnp.int32)[:, None]
-    for k in range(top):
-        named = named | (ids[:, k][None, :] == each)
-    earlier = jnp.arange(tokens)[:, None] < jnp.arange(tokens)[None, :]
-    before = dot(named.astype(BF16), earlier.astype(BF16))
-    slots = jnp.where(named, before, -1.0)
-
-    seen, outgoing_grad = open_exchange(local_kv, slots, grad_out, ctx_count)
+
+    seen, outgoing_grad, slots, token_slots = open_exchange(
+        local_kv, ids, grad_out, experts, ctx_count
+    )
     first = lax.axis_index("ctx") * tokens
     place = jnp.concatenate(
         [
@@ -1048,7 +1056,6 @@
     chosen = [ids[:, k : k + 1] == each.reshape(1, experts) for k in range(top)]
     for k in range(top):
         dense_gates = dense_gates + jnp.where(chosen[k], gates[:, k : k + 1], 0.0)
-    token_slots = slots.T
 
     norm_in = jnp.stack([square_norm(base_in[j], low_in[j], high_in[j]) for j in range(2)])
     scale_in = mag_in / norm_in

time: 247 us -> 246 us (level)
  matrix products: 16.8 us -> 13.6 us
  local copies, waits for them, and re-layouts: 7.05 us -> 9.63 us
    dot_general x4 -> x3, matrix products: 11.6 us -> 8.45 us  [dot(): return jnp.dot(left, right, preferred_element_type=F32)]
    unnamed x67 -> x73, local copies, waits for them, and re-layouts: 5.04 us -> 7.5 us
  transfers between devices with their start and end apart: 5 -> 5, of which waited for: 5 -> 5; matrix products, arithmetic and copies ran while one was open for 12% -> 11% of each run, Pallas kernels for 39% -> 39%
where the time goes in v5:
time: 246 us; the launch traced here: 245 us
  Pallas kernels  128 us (52%)
  waiting for transfers between devices  44.6 us (18%)
  starting transfers between devices  36.4 us (15%)
  matrix products  13.6 us (6%)
  other arithmetic  11.8 us (5%)
  local copies, waits for them, and re-layouts  9.63 us (4%)
    pallas_call x2, Pallas kernels, expert(): pl.pallas_call(functools.partial(expert_kernel, slots), in_specs=[hbm, hb...  47.4 us
    all_to_all x5, waiting for transfers between devices, exchange(): moved = lax.all_to_all(split, axes, split_axis=0, concat_axis=0, tiled=True)  44.6 us
    all_to_all x5, starting transfers between devices, exchange(): moved = lax.all_to_all(split, axes, split_axis=0, concat_axis=0, tiled=True)  36.4 us
    pallas_call x1, Pallas kernels, finish(): pl.pallas_call(functools.partial(finish_kernel, heads, steps_per_kv, coun...  16.9 us
    pallas_call x1, Pallas kernels, attend(): pl.pallas_call(functools.partial(attend_kernel, heads, per_kv), grid=(ste...  13.2 us
    pallas_call x1, Pallas kernels, expert_grads(): pl.pallas_call(functools.partial(expert_grads_kernel, halves), grid=(widt...  13.1 us
    pallas_call x1, Pallas kernels, open_exchange(): pl.pallas_call(functools.partial(open_kernel, count), in_specs=[vmem] * 3...  12.2 us
    pallas_call x1, Pallas kernels, dispatch(): pl.pallas_call(functools.partial(dispatch_kernel, with_norm), grid=(total...  9.19 us
  transfers between devices with their start and end apart: 5, of which 5 were waited for; matrix products, arithmetic and copies ran while one was open for 11% of the time, Pallas kernels for 39%

profile of v5, /device:TPU:1, one launch (start us, length us, event | category | flops | bytes accessed | tf_op | source)
XLA Modules:
  0.0 245.2 jit_solution(7245028711841856603)
XLA Ops:
  2.1 12.2 %open_exchange.1 = (bf16[640,512]{1,0:T(8,128)(2,1)}, bf16[2048,1024]{1,0:T(8,128)(2,1)}, f32[128,128]{1,0:T(8,128)}, f32[128,128]{1,0:T(8,128)}) custom-call(bf16[128,512]{1,0:T(8,128)(2,1)} %bitcast.135, s32[128,3]{1,0:T(8,128)} %bitcast.128, bf16[128,4096]{1,0:T(8,128)(2,1)} %bitcast.104), custom_call_target="tpu_custom_call" | custom-call | tf_op jit(solution)/shard_map/open_exchange/pallas_call | solution.py:324
  14.3 14.2 %all-to-all-start = ((bf16[128,16,1024]{2,1,0:T(8,128)(2,1)}), bf16[128,16,1024]{2,1,0:T(8,128)(2,1)}, u32[]{:S(2)}, u32[]{:S(2)}) async-start(bf16[128,16,1024]{2,1,0:T(8,128)(2,1)} %bitcast.121), calls=%async_computation | async-start | bytes 8388608 | tf_op jit(solution)/shard_map/all_to_all | solution.py:1031
  28.6 4.3 %fusion.1 = f32[768]{0:T(1024)S(1)} fusion(bf16[1,2,4096,768]{3,2,1,0:T(8,128)(2,1)} %param.22, bf16[1,2,32,768]{3,2,1,0:T(8,128)(2,1)S(1)} %copy-done.24, bf16[1,2,4096,32]{2,3,1,0:T(8,128)(2,1)S(1)} %copy-done.11), kind=kOutput, calls=%fused_computation.2 | convolution fusion | flops 213908736 | bytes 6605824 | tf_op jit(solution)/shard_map/dot_general | solution.py:37
  36.5 2.3 fusion.3
  40.7 13.2 %attend.1 = (bf16[4,640,1024]{2,1,0:T(8,128)(2,1)}, bf16[128,4096]{1,0:T(8,128)(2,1)}) custom-call(s32[6]{0:T(128)} %pad_add_fusion.place_ref, bf16[128,4096]{1,0:T(8,128)(2,1)} %bitcast.108, bf16[640,512]{1,0:T(8,128)(2,1)} %get-tuple-element.66.keyval_ref.keys_ref.values_ref), custom_call_target="tpu_custom_call" | custom-call | flops 1342177280 | bytes 9437184 | tf_op jit(solution)/shard_map/attend/pallas_call | solution.py:411
  55.7 9.2 %dispatch.1 = (bf16[2048,512]{1,0:T(8,128)(2,1)}, bf16[2048,512]{1,0:T(8,128)(2,1)}, f32[128,1]{1,0:T(8,128)}) custom-call(f32[128,128]{1,0:T(8,128)} %get-tuple-element.65.slots_ref, bf16[128,4096]{1,0:T(8,128)(2,1)} %get-tuple-element.97.rows_ref.hidden_hbm, f32[1,4096]{1,0:T(1,128)} %bitcast.110), custom_call_target="tpu_custom_call" | custom-call | flops 4294967296 | bytes 10485760 | tf_op jit(solution)/shard_map/dispatch/pallas_call | solution.py:111
  66.4 13.6 %all-to-all-done = bf16[128,16,1024]{2,1,0:T(8,128)(2,1)} async-done(((bf16[128,16,1024]{2,1,0:T(8,128)(2,1)}), bf16[128,16,1024]{2,1,0:T(8,128)(2,1)}, u32[]{:S(2)}, u32[]{:S(2)}) %all-to-all-start) | async-done | bytes 4194336 | tf_op jit(solution)/shard_map/all_to_all | solution.py:1031
  80.0 5.5 %all-to-all-start.1 = ((bf16[128,16,512]{2,1,0:T(8,128)(2,1)}), bf16[128,16,512]{2,1,0:T(8,128)(2,1)}, u32[]{:S(2)}, u32[]{:S(2)}) async-start(bf16[128,16,512]{2,1,0:T(8,128)(2,1)} %bitcast.127), calls=%async_computation.1 | async-start | bytes 4194304 | tf_op jit(solution)/shard_map/all_to_all | solution.py:1031
  85.5 7.8 %unpack.1 = bf16[2,256,4096]{2,1,0:T(8,128)(2,1)} custom-call(bf16[2048,1024]{1,0:T(8,128)(2,1)} %bitcast.10.blocks_ref), custom_call_target="tpu_custom_call" | custom-call | flops 1073741824 | bytes 8388608 | tf_op jit(solution)/shard_map/unpack/pallas_call | solution.py:145
  93.3 3.5 %multiply_convert_fusion = bf16[2,256,4096]{2,1,0:T(8,128)(2,1)S(1)} fusion(bf16[2,256,4096]{2,1,0:T(8,128)(2,1)} %unpack.1, f32[4096]{0:T(1024)S(1)} %bitcast.132), kind=kLoop, calls=%fused_computation.7 | loop fusion | flops 6291456 | bytes 8404992 | tf_op jit(solution)/shard_map/convert_element_type | solution.py:1065
  98.2 3.6 %fusion.22 = f32[512,768]{1,0:T(8,128)S(1)} fusion(bf16[512,4096]{1,0:T(8,128)(2,1)S(1)} %bitcast.123, bf16[1,768,4096]{2,1,0:T(8,128)(2,1)S(1)} %bitcast.118), kind=kOutput, calls=%fused_computation.61 | convolution fusion | flops 3221225472 | bytes 12058624 | tf_op jit(solution)/shard_map/dot_general | solution.py:41
  102.1 12.7 %all-to-all-done.1 = bf16[128,16,512]{2,1,0:T(8,128)(2,1)} async-done(((bf16[128,16,512]{2,1,0:T(8,128)(2,1)}), bf16[128,16,512]{2,1,0:T(8,128)(2,1)}, u32[]{:S(2)}, u32[]{:S(2)}) %all-to-all-start.1) | async-done | bytes 2097184 | tf_op jit(solution)/shard_map/all_to_all | solution.py:1031
  114.9 5.6 %all-to-all-start.2 = ((bf16[128,16,512]{2,1,0:T(8,128)(2,1)}), bf16[128,16,512]{2,1,0:T(8,128)(2,1)}, u32[]{:S(2)}, u32[]{:S(2)}) async-start(bf16[128,16,512]{2,1,0:T(8,128)(2,1)} %bitcast.125), calls=%async_computation.2 | async-start | bytes 4194304 | tf_op jit(solution)/shard_map/all_to_all | solution.py:1031
  121.7 23.7 %expert.3 = (bf16[2048,512]{1,0:T(8,128)(2,1)}, bf16[256,4096]{1,0:T(8,128)(2,1)}, bf16[256,768]{1,0:T(8,128)(2,1)}, bf16[256,64]{1,0:T(8,128)(2,1)}, bf16[2,256...) custom-call(bf16[2048,512]{1,0:T(8,128)(2,1)} %bitcast.28.blocks_hbm, ...), custom_call_target="tpu_custom_call" | custom-call | flops 6442450944 | bytes 31457280 | tf_op jit(solution)/shard_map/expert/pallas_call | solution.py:893
  145.4 4.5 %all-to-all-done.2 = bf16[128,16,512]{2,1,0:T(8,128)(2,1)} async-done(((bf16[128,16,512]{2,1,0:T(8,128)(2,1)}), bf16[128,16,512]{2,1,0:T(8,128)(2,1)}, u32[]{:S(2)}, u32[]{:S(2)}) %all-to-all-start.2) | async-done | bytes 2097184 | tf_op jit(solution)/shard_map/all_to_all | solution.py:1031
  150.0 5.4 %all-to-all-start.4 = ((bf16[128,16,512]{2,1,0:T(8,128)(2,1)}), bf16[128,16,512]{2,1,0:T(8,128)(2,1)S(1)}, u32[]{:S(2)}, u32[]{:S(2)}) async-start(bf16[128,16,512]{2,1,0:T(8,128)(2,1)} %bitcast.126), calls=%async_computation.4 | async-start | bytes 4194304 | tf_op jit(solution)/shard_map/all_to_all | solution.py:1031
  155.4 23.7 %expert.2 = (bf16[2048,512]{1,0:T(8,128)(2,1)}, bf16[256,4096]{1,0:T(8,128)(2,1)}, bf16[256,768]{1,0:T(8,128)(2,1)}, bf16[256,64]{1,0:T(8,128)(2,1)}, bf16[2,256...) custom-call(bf16[2048,512]{1,0:T(8,128)(2,1)} %bitcast.30.blocks_hbm, ...), custom_call_target="tpu_custom_call" | custom-call | flops 6442450944 | bytes 31457280 | tf_op jit(solution)/shard_map/expert/pallas_call | solution.py:893
  179.0 6.0 %all-to-all-done.4 = bf16[128,16,512]{2,1,0:T(8,128)(2,1)S(1)} async-done(((bf16[128,16,512]{2,1,0:T(8,128)(2,1)}), bf16[128,16,512]{2,1,0:T(8,128)(2,1)S(1)}, u32[]{:S(2)}, u32[]{:S(2)}) %all-to-all-start.4) | async-done | bytes 2097184 | tf_op jit(solution)/shard_map/all_to_all | solution.py:1031
  185.1 5.8 %all-to-all-start.3 = ((bf16[128,16,512]{2,1,0:T(8,128)(2,1)}), bf16[128,16,512]{2,1,0:T(8,128)(2,1)}, u32[]{:S(2)}, u32[]{:S(2)}) async-start(bf16[128,16,512]{2,1,0:T(8,128)(2,1)} %bitcast.124), calls=%async_computation.3 | async-start | bytes 4194304 | tf_op jit(solution)/shard_map/all_to_all | solution.py:1031
  191.7 4.1 %combine_first.1.first_hbm = f32[8,128,512]{2,1,0:T(8,128)} custom-call(f32[128,128]{1,0:T(8,128)} %get-tuple-element.73.slots_ref, f32[128,128]{1,0:T(8,128)} %select_add_fusion.1.gates_ref, bf16[2048,512]{1,0:T(8,128)(2,1)} %bitcast.113), custom_call_target="tpu_custom_call" | custom-call | flops 1 | bytes 1 | tf_op jit(solution)/shard_map/combine_first/pallas_call | solution.py:714
  196.7 13.1 %expert_grads.1 = (f32[1,4096]{1,0:T(1,128)}, f32[32,4096]{1,0:T(8,128)}, f32[64,4096]{1,0:T(8,128)}, f32[32,768]{1,0:T(8,128)}, f32[2,32,768]{2,1,0:T(8,128)}) custom-call(bf16[512,4096]{1,0:T(8,128)(2,1)} %bitcast.112, f32[1,4096]{1,0:T(1,128)} %copy-done.16, bf16[768,4096]{1,0:T(8,128)(2,1)} %bitcast.114, bf16[32,4096]{1,0:T(8,128)(2,1)} %bitcast.131, ...), custom_call_target="tpu_custom_call" | custom-call | flops 1 | bytes 1 | tf_op jit(solution)/shard_map/expert_grads/pallas_call | solution.py:975
  212.7 7.7 %all-to-all-done.3 = bf16[128,16,512]{2,1,0:T(8,128)(2,1)} async-done(((bf16[128,16,512]{2,1,0:T(8,128)(2,1)}), bf16[128,16,512]{2,1,0:T(8,128)(2,1)}, u32[]{:S(2)}, u32[]{:S(2)}) %all-to-all-start.3) | async-done | bytes 2097184 | tf_op jit(solution)/shard_map/all_to_all | solution.py:1031
  221.6 4.0 %combine_last.1.grad_ref = bf16[128,4096]{1,0:T(8,128)(2,1)S(1)} custom-call(f32[128,128]{1,0:T(8,128)S(1)} %copy-done.1, f32[128,128]{1,0:T(8,128)S(1)} %copy-done.2, bf16[2048,512]{1,0:T(8,128)(2,1)} %bitcast.34.blocks_ref, f32[1,4096]{1,0:T(1,128)S(1)} %bitcast.111, f32[128,1]{1,0:T(8,128)S(1)} %copy-done.7, f32[8,128,512]{2,1,0:T(8,128)} %combine_first.1.first_hbm, ...), custom_call_target="tpu_custom_call" | custom-call | flops 2147483648 | bytes 8388608 | tf_op jit(solution)/shard_map/combine_last/pallas_call | solution.py:738
  225.6 16.9 %finish.1 = (bf16[128,4096]{1,0:T(8,128)(2,1)S(1)}, bf16[128,512]{1,0:T(8,128)(2,1)S(1)}, f32[8,128]{1,0:T(8,128)S(1)}) custom-call(bf16[128,4096]{1,0:T(8,128)(2,1)S(1)} %bitcast.109, bf16[128,4096]{1,0:T(8,128)(2,1)S(1)} %combine_last.1.grad_ref, bf16[4,640,1024]{2,1,0:T(8,128)(2,1)} %get-tuple-element.98.prob_ref, bf16[640,512]{1,0:T(8,128)(2,1)S(1)} %copy-done.4, ...), custom_call_target="tpu_custom_call" | custom-call | flops 2684354560 | bytes 10485760 | tf_op jit(solution)/shard_map/finish/pallas_call | solution.py:582
  (112 shorter events, 21.3 us)
Async XLA Ops:
  14.2 14.2 %copy-start.11 = (bf16[1,2,4096,32]{2,3,1,0:T(8,128)(2,1)S(1)}, bf16[1,2,4096,32]{2,3,1,0:T(8,128)(2,1)}, u32[]{:S(2)}) copy-start(bf16[1,2,4096,32]{2,3,1,0:T(8,128)(2,1)} %param.23) | copy-start | bytes 1572868
  14.3 14.2 %copy-start.24 = (bf16[1,2,32,768]{3,2,1,0:T(8,128)(2,1)S(1)}, bf16[1,2,32,768]{3,2,1,0:T(8,128)(2,1)}, u32[]{:S(2)}) copy-start(bf16[1,2,32,768]{3,2,1,0:T(8,128)(2,1)} %param.24) | copy-start | bytes 294916
  14.3 18.6 %slice-start = ((s8[6291456]{0:T(1024)(128)(4,1)}), s8[2097152]{0:T(1024)(128)(4,1)S(1)}, s32[]{:S(2)}) async-start(s8[6291456]{0:T(1024)(128)(4,1)} %bitcast.115), calls=%async_computation.5 | async-start | bytes 4194304
  14.3 65.7 %all-to-all-start = ((bf16[128,16,1024]{2,1,0:T(8,128)(2,1)}), bf16[128,16,1024]{2,1,0:T(8,128)(2,1)}, u32[]{:S(2)}, u32[]{:S(2)}) async-start(bf16[128,16,1024]{2,1,0:T(8,128)(2,1)} %bitcast.121), calls=%async_computation | async-start | bytes 8388608 | tf_op jit(solution)/shard_map/all_to_all | solution.py:1031
  38.9 15.1 %copy-start.19 = (f32[1,4096]{1,0:T(1,128)S(1)}, f32[1,4096]{1,0:T(1,128)}, u32[]{:S(2)}) copy-start(f32[1,4096]{1,0:T(1,128)} %param.29) | copy-start | bytes 49156
  38.9 15.2 %copy-start.9 = (s32[1,128,3]{2,1,0:T(8,128)S(1)}, s32[1,128,3]{2,1,0:T(8,128)}, u32[]{:S(2)}) copy-start(s32[1,128,3]{2,1,0:T(8,128)} %copy.36) | copy-start | bytes 4612
  38.9 15.3 %copy-start.20 = (f32[1,2,768]{2,1,0:T(2,128)S(1)}, f32[1,2,768]{2,1,0:T(2,128)}, u32[]{:S(2)}) copy-start(f32[1,2,768]{2,1,0:T(2,128)} %param.25) | copy-start | bytes 18436
  54.0 39.3 %copy-start.16 = (f32[1,4096]{1,0:T(1,128)}, f32[1,4096]{1,0:T(1,128)S(1)}, u32[]{:S(2)}) copy-start(f32[1,4096]{1,0:T(1,128)S(1)} %div.22.scale_ref) | copy-start | bytes 49156
  80.0 34.9 %all-to-all-start.1 = ((bf16[128,16,512]{2,1,0:T(8,128)(2,1)}), bf16[128,16,512]{2,1,0:T(8,128)(2,1)}, u32[]{:S(2)}, u32[]{:S(2)}) async-start(bf16[128,16,512]{2,1,0:T(8,128)(2,1)} %bitcast.127), calls=%async_computation.1 | async-start | bytes 4194304 | tf_op jit(solution)/shard_map/all_to_all | solution.py:1031
  85.5 12.6 %slice-start.2 = ((s8[6291456]{0:T(1024)(128)(4,1)}), s8[2097152]{0:T(1024)(128)(4,1)S(1)}, s32[]{:S(2)}) async-start(s8[6291456]{0:T(1024)(128)(4,1)} %bitcast.117), calls=%async_computation.7 | async-start | bytes 4194304
  114.9 35.1 %all-to-all-start.2 = ((bf16[128,16,512]{2,1,0:T(8,128)(2,1)}), bf16[128,16,512]{2,1,0:T(8,128)(2,1)}, u32[]{:S(2)}, u32[]{:S(2)}) async-start(bf16[128,16,512]{2,1,0:T(8,128)(2,1)} %bitcast.125), calls=%async_computation.2 | async-start | bytes 4194304 | tf_op jit(solution)/shard_map/all_to_all | solution.py:1031
  150.0 35.1 %all-to-all-start.4 = ((bf16[128,16,512]{2,1,0:T(8,128)(2,1)}), bf16[128,16,512]{2,1,0:T(8,128)(2,1)S(1)}, u32[]{:S(2)}, u32[]{:S(2)}) async-start(bf16[128,16,512]{2,1,0:T(8,128)(2,1)} %bitcast.126), calls=%async_computation.4 | async-start | bytes 4194304 | tf_op jit(solution)/shard_map/all_to_all | solution.py:1031
  185.1 35.3 %all-to-all-start.3 = ((bf16[128,16,512]{2,1,0:T(8,128)(2,1)}), bf16[128,16,512]{2,1,0:T(8,128)(2,1)}, u32[]{:S(2)}, u32[]{:S(2)}) async-start(bf16[128,16,512]{2,1,0:T(8,128)(2,1)} %bitcast.124), calls=%async_computation.3 | async-start | bytes 4194304 | tf_op jit(solution)/shard_map/all_to_all | solution.py:1031
  196.7 13.2 %copy-start.17 = (f32[256,1]{1,0:T(8,128)S(1)}, f32[256,1]{1,0:T(8,128)}, u32[]{:S(2)}) copy-start(f32[256,1]{1,0:T(8,128)} %get-tuple-element.99) | copy-start | bytes 3076
  196.7 13.2 %copy-start.18 = (f32[256,1]{1,0:T(8,128)S(1)}, f32[256,1]{1,0:T(8,128)}, u32[]{:S(2)}) copy-start(f32[256,1]{1,0:T(8,128)} %get-tuple-element.100) | copy-start | bytes 3076
  196.7 15.4 %copy-start.21 = (f32[2,768]{1,0:T(2,128)S(1)}, f32[2,768]{1,0:T(2,128)}, u32[]{:S(2)}) copy-start(f32[2,768]{1,0:T(2,128)} %get-tuple-element.116) | copy-start | bytes 18436
  196.7 15.4 %copy-start.22 = (f32[2,768]{1,0:T(2,128)S(1)}, f32[2,768]{1,0:T(2,128)}, u32[]{:S(2)}) copy-start(f32[2,768]{1,0:T(2,128)} %get-tuple-element.117) | copy-start | bytes 18436
  196.7 23.7 %copy-start = (bf16[1,128,4096]{2,1,0:T(8,128)(2,1)S(1)}, bf16[1,128,4096]{2,1,0:T(8,128)(2,1)}, u32[]{:S(2)}) copy-start(bf16[1,128,4096]{2,1,0:T(8,128)(2,1)} %param.21) | copy-start | bytes 3145732
  196.7 23.7 %copy-start.1 = (f32[128,128]{1,0:T(8,128)S(1)}, f32[128,128]{1,0:T(8,128)}, u32[]{:S(2)}) copy-start(f32[128,128]{1,0:T(8,128)} %get-tuple-element.73.slots_ref) | copy-start | bytes 196612
  196.7 23.6 %copy-start.2 = (f32[128,128]{1,0:T(8,128)S(1)}, f32[128,128]{1,0:T(8,128)}, u32[]{:S(2)}) copy-start(f32[128,128]{1,0:T(8,128)} %select_add_fusion.1.gates_ref) | copy-start | bytes 196612
  196.7 23.6 %copy-start.5 = (f32[4096]{0:T(1024)S(1)}, f32[4096]{0:T(1024)}, u32[]{:S(2)}) copy-start(f32[4096]{0:T(1024)} %param.18) | copy-start | bytes 49156
  196.7 23.6 %copy-start.7 = (f32[128,1]{1,0:T(8,128)S(1)}, f32[128,1]{1,0:T(8,128)}, u32[]{:S(2)}) copy-start(f32[128,1]{1,0:T(8,128)} %get-tuple-element.80.rinv_ref) | copy-start | bytes 1540
  210.1 15.6 %copy-start.3 = (bf16[1,128,4096]{2,1,0:T(8,128)(2,1)S(1)}, bf16[1,128,4096]{2,1,0:T(8,128)(2,1)}, u32[]{:S(2)}) copy-start(bf16[1,128,4096]{2,1,0:T(8,128)(2,1)} %param.15) | copy-start | bytes 3145732
  210.1 15.6 %copy-start.4 = (bf16[640,512]{1,0:T(8,128)(2,1)S(1)}, bf16[640,512]{1,0:T(8,128)(2,1)}, u32[]{:S(2)}) copy-start(bf16[640,512]{1,0:T(8,128)(2,1)} %get-tuple-element.66.keyval_ref.keys_ref.values_ref) | copy-start | bytes 1966084
  (14 other events, 74.0 us)

commit v6 on v4

--- a/solution.py
+++ b/solution.py
@@ -745,8 +745,8 @@
             pltpu.VMEM(hidden.shape, BF16),
             pltpu.SemaphoreType.DMA((3,)),
         ],
-        compiler_params=params(50),
-        cost_estimate=cost(2 * total * tokens * width, 8 * MB),
+        compiler_params=params(51),
+        cost_estimate=cost(2 * total * tokens * width, 1),
         name="combine_last",
     )(slots, gates, blocks, gain, rinv, first, grad_out, hidden)
 

time: 247 us -> 246 us (level)
    unnamed x67 -> x65, local copies, waits for them, and re-layouts: 5.04 us -> 3.86 us
  transfers between devices with their start and end apart: 5 -> 5, of which waited for: 5 -> 5; matrix products, arithmetic and copies ran while one was open for 12% -> 13% of each run, Pallas kernels for 39% -> 39%
where the time goes in v6:
time: 246 us; the launch traced here: 244 us
  Pallas kernels  128 us (52%)
  waiting for transfers between devices  43.5 us (18%)
  starting transfers between devices  36.4 us (15%)
  matrix products  16.8 us (7%)
  other arithmetic  12.6 us (5%)
  local copies, waits for them, and re-layouts  5.88 us (2%)
    pallas_call x2, Pallas kernels, expert(): pl.pallas_call(functools.partial(expert_kernel, slots), in_specs=[hbm, hb...  47.4 us
    all_to_all x5, waiting for transfers between devices, exchange(): moved = lax.all_to_all(split, axes, split_axis=0, concat_axis=0, tiled=True)  43.5 us
    all_to_all x5, starting transfers between devices, exchange(): moved = lax.all_to_all(split, axes, split_axis=0, concat_axis=0, tiled=True)  36.4 us
    pallas_call x1, Pallas kernels, finish(): pl.pallas_call(functools.partial(finish_kernel, heads, steps_per_kv, coun...  16.9 us
    pallas_call x1, Pallas kernels, attend(): pl.pallas_call(functools.partial(attend_kernel, heads, per_kv), grid=(ste...  13.2 us
    pallas_call x1, Pallas kernels, expert_grads(): pl.pallas_call(functools.partial(expert_grads_kernel, halves), grid=(widt...  13.1 us
    pallas_call x1, Pallas kernels, open_exchange(): pl.pallas_call(functools.partial(open_kernel, count), in_specs=[vmem] * 3...  12.2 us
    dot_general x4, matrix products, dot(): return jnp.dot(left, right, preferred_element_type=F32)  11.6 us
  transfers between devices with their start and end apart: 5, of which 5 were waited for; matrix products, arithmetic and copies ran while one was open for 13% of the time, Pallas kernels for 39%

profile of v6, /device:TPU:1, one launch (start us, length us, event | category | flops | bytes accessed | tf_op | source)
XLA Modules:
  0.0 244.5 jit_solution(11570278365185797331)
XLA Ops:
  2.3 12.2 %open_exchange.1 = (bf16[640,512]{1,0:T(8,128)(2,1)}, bf16[2048,1024]{1,0:T(8,128)(2,1)}) custom-call(bf16[128,512]{1,0:T(8,128)(2,1)} %bitcast.141, f32[128,128]{1,0:T(8,128)} %get-tuple-element.162.slots_ref, bf16[128,4096]{1,0:T(8,128)(2,1)} %bitcast.114), custom_call_target="tpu_custom_call" | custom-call | tf_op jit(solution)/shard_map/open_exchange/pallas_call | solution.py:314
  14.5 14.2 %all-to-all-start = ((bf16[128,16,1024]{2,1,0:T(8,128)(2,1)}), bf16[128,16,1024]{2,1,0:T(8,128)(2,1)}, u32[]{:S(2)}, u32[]{:S(2)}) async-start(bf16[128,16,1024]{2,1,0:T(8,128)(2,1)} %bitcast.129), calls=%async_computation | async-start | bytes 8388608 | tf_op jit(solution)/shard_map/all_to_all | solution.py:1019
  28.8 4.8 %multiply_reduce_fusion = f32[4096]{0:T(1024)S(1)} fusion(bf16[1,768,32]{1,2,0:T(8,128)(2,1)S(1)} %copy-done.13, bf16[1,32,4096]{2,1,0:T(8,128)(2,1)S(1)} %copy-done.12, bf16[1,768,4096]{2,1,0:T(8,128)(2,1)} %param.26), kind=kOutput, calls=%fused_computation.6 | convolution fusion | flops 213905408 | bytes 6619136 | tf_op jit(solution)/shard_map/dot_general | solution.py:37
  33.7 4.3 %fusion.1 = f32[768]{0:T(1024)S(1)} fusion(bf16[1,2,4096,768]{3,2,1,0:T(8,128)(2,1)} %param.22, bf16[1,2,32,768]{3,2,1,0:T(8,128)(2,1)S(1)} %copy-done.22, bf16[1,2,4096,32]{2,3,1,0:T(8,128)(2,1)S(1)} %copy-done.9), kind=kOutput, calls=%fused_computation.2 | convolution fusion | flops 213908736 | bytes 6605824 | tf_op jit(solution)/shard_map/dot_general | solution.py:37
  42.3 13.2 %attend.1 = (bf16[4,640,1024]{2,1,0:T(8,128)(2,1)}, bf16[128,4096]{1,0:T(8,128)(2,1)}) custom-call(s32[6]{0:T(128)} %pad_add_fusion.place_ref, bf16[128,4096]{1,0:T(8,128)(2,1)} %bitcast.118, bf16[640,512]{1,0:T(8,128)(2,1)} %get-tuple-element.63.keyval_ref.keys_ref.values_ref), custom_call_target="tpu_custom_call" | custom-call | flops 1342177280 | bytes 9437184 | tf_op jit(solution)/shard_map/attend/pallas_call | solution.py:399
  57.0 9.2 %dispatch.1 = (bf16[2048,512]{1,0:T(8,128)(2,1)}, bf16[2048,512]{1,0:T(8,128)(2,1)}, f32[128,1]{1,0:T(8,128)}) custom-call(f32[128,128]{1,0:T(8,128)} %get-tuple-element.162.slots_ref, bf16[128,4096]{1,0:T(8,128)(2,1)} %get-tuple-element.93.rows_ref.hidden_hbm, f32[1,4096]{1,0:T(1,128)} %bitcast.120), custom_call_target="tpu_custom_call" | custom-call | flops 4294967296 | bytes 10485760 | tf_op jit(solution)/shard_map/dispatch/pallas_call | solution.py:111
  67.7 12.5 %all-to-all-done = bf16[128,16,1024]{2,1,0:T(8,128)(2,1)} async-done(((bf16[128,16,1024]{2,1,0:T(8,128)(2,1)}), bf16[128,16,1024]{2,1,0:T(8,128)(2,1)}, u32[]{:S(2)}, u32[]{:S(2)}) %all-to-all-start) | async-done | bytes 4194336 | tf_op jit(solution)/shard_map/all_to_all | solution.py:1019
  80.3 5.5 %all-to-all-start.1 = ((bf16[128,16,512]{2,1,0:T(8,128)(2,1)}), bf16[128,16,512]{2,1,0:T(8,128)(2,1)}, u32[]{:S(2)}, u32[]{:S(2)}) async-start(bf16[128,16,512]{2,1,0:T(8,128)(2,1)} %bitcast.135), calls=%async_computation.1 | async-start | bytes 4194304 | tf_op jit(solution)/shard_map/all_to_all | solution.py:1019
  85.8 7.8 %unpack.1 = bf16[2,256,4096]{2,1,0:T(8,128)(2,1)} custom-call(bf16[2048,1024]{1,0:T(8,128)(2,1)} %bitcast.12.blocks_ref), custom_call_target="tpu_custom_call" | custom-call | flops 1073741824 | bytes 8388608 | tf_op jit(solution)/shard_map/unpack/pallas_call | solution.py:145
  93.6 3.5 %multiply_convert_fusion = bf16[2,256,4096]{2,1,0:T(8,128)(2,1)S(1)} fusion(bf16[2,256,4096]{2,1,0:T(8,128)(2,1)} %unpack.1, f32[4096]{0:T(1024)S(1)} %bitcast.138), kind=kLoop, calls=%fused_computation.7 | loop fusion | flops 6291456 | bytes 8404992 | tf_op jit(solution)/shard_map/convert_element_type | solution.py:1058
  98.4 3.6 %fusion.28 = f32[512,768]{1,0:T(8,128)S(1)} fusion(bf16[512,4096]{1,0:T(8,128)(2,1)S(1)} %bitcast.131, bf16[1,768,4096]{2,1,0:T(8,128)(2,1)S(1)} %bitcast.126), kind=kOutput, calls=%fused_computation.73 | convolution fusion | flops 3221225472 | bytes 12058624 | tf_op jit(solution)/shard_map/dot_general | solution.py:41
  102.4 12.7 %all-to-all-done.1 = bf16[128,16,512]{2,1,0:T(8,128)(2,1)} async-done(((bf16[128,16,512]{2,1,0:T(8,128)(2,1)}), bf16[128,16,512]{2,1,0:T(8,128)(2,1)}, u32[]{:S(2)}, u32[]{:S(2)}) %all-to-all-start.1) | async-done | bytes 2097184 | tf_op jit(solution)/shard_map/all_to_all | solution.py:1019
  115.1 5.6 %all-to-all-start.2 = ((bf16[128,16,512]{2,1,0:T(8,128)(2,1)}), bf16[128,16,512]{2,1,0:T(8,128)(2,1)}, u32[]{:S(2)}, u32[]{:S(2)}) async-start(bf16[128,16,512]{2,1,0:T(8,128)(2,1)} %bitcast.133), calls=%async_computation.2 | async-start | bytes 4194304 | tf_op jit(solution)/shard_map/all_to_all | solution.py:1019
  122.0 23.7 %expert.3 = (bf16[2048,512]{1,0:T(8,128)(2,1)}, bf16[256,4096]{1,0:T(8,128)(2,1)}, bf16[256,768]{1,0:T(8,128)(2,1)}, bf16[256,64]{1,0:T(8,128)(2,1)}, bf16[2,256...) custom-call(bf16[2048,512]{1,0:T(8,128)(2,1)} %bitcast.31.blocks_hbm, ...), custom_call_target="tpu_custom_call" | custom-call | flops 6442450944 | bytes 31457280 | tf_op jit(solution)/shard_map/expert/pallas_call | solution.py:881
  145.7 4.5 %all-to-all-done.2 = bf16[128,16,512]{2,1,0:T(8,128)(2,1)} async-done(((bf16[128,16,512]{2,1,0:T(8,128)(2,1)}), bf16[128,16,512]{2,1,0:T(8,128)(2,1)}, u32[]{:S(2)}, u32[]{:S(2)}) %all-to-all-start.2) | async-done | bytes 2097184 | tf_op jit(solution)/shard_map/all_to_all | solution.py:1019
  150.2 5.4 %all-to-all-start.4 = ((bf16[128,16,512]{2,1,0:T(8,128)(2,1)}), bf16[128,16,512]{2,1,0:T(8,128)(2,1)S(1)}, u32[]{:S(2)}, u32[]{:S(2)}) async-start(bf16[128,16,512]{2,1,0:T(8,128)(2,1)} %bitcast.134), calls=%async_computation.4 | async-start | bytes 4194304 | tf_op jit(solution)/shard_map/all_to_all | solution.py:1019
  155.6 23.7 %expert.2 = (bf16[2048,512]{1,0:T(8,128)(2,1)}, bf16[256,4096]{1,0:T(8,128)(2,1)}, bf16[256,768]{1,0:T(8,128)(2,1)}, bf16[256,64]{1,0:T(8,128)(2,1)}, bf16[2,256...) custom-call(bf16[2048,512]{1,0:T(8,128)(2,1)} %bitcast.33.blocks_hbm, ...), custom_call_target="tpu_custom_call" | custom-call | flops 6442450944 | bytes 31457280 | tf_op jit(solution)/shard_map/expert/pallas_call | solution.py:881
  179.3 6.0 %all-to-all-done.4 = bf16[128,16,512]{2,1,0:T(8,128)(2,1)S(1)} async-done(((bf16[128,16,512]{2,1,0:T(8,128)(2,1)}), bf16[128,16,512]{2,1,0:T(8,128)(2,1)S(1)}, u32[]{:S(2)}, u32[]{:S(2)}) %all-to-all-start.4) | async-done | bytes 2097184 | tf_op jit(solution)/shard_map/all_to_all | solution.py:1019
  185.3 5.8 %all-to-all-start.3 = ((bf16[128,16,512]{2,1,0:T(8,128)(2,1)}), bf16[128,16,512]{2,1,0:T(8,128)(2,1)}, u32[]{:S(2)}, u32[]{:S(2)}) async-start(bf16[128,16,512]{2,1,0:T(8,128)(2,1)} %bitcast.132), calls=%async_computation.3 | async-start | bytes 4194304 | tf_op jit(solution)/shard_map/all_to_all | solution.py:1019
  191.9 4.0 %combine_first.1.first_hbm = f32[8,128,512]{2,1,0:T(8,128)} custom-call(f32[128,128]{1,0:T(8,128)} %get-tuple-element.69.slots_ref, f32[128,128]{1,0:T(8,128)} %select_add_fusion.1.gates_ref, bf16[2048,512]{1,0:T(8,128)(2,1)} %bitcast.123), custom_call_target="tpu_custom_call" | custom-call | flops 1 | bytes 1 | tf_op jit(solution)/shard_map/combine_first/pallas_call | solution.py:702
  197.0 13.1 %expert_grads.1 = (f32[1,4096]{1,0:T(1,128)}, f32[32,4096]{1,0:T(8,128)}, f32[64,4096]{1,0:T(8,128)}, f32[32,768]{1,0:T(8,128)}, f32[2,32,768]{2,1,0:T(8,128)}) custom-call(bf16[512,4096]{1,0:T(8,128)(2,1)} %bitcast.122, f32[1,4096]{1,0:T(1,128)} %copy-done.14, bf16[768,4096]{1,0:T(8,128)(2,1)} %bitcast.124, bf16[32,4096]{1,0:T(8,128)(2,1)} %bitcast.137, ...), custom_call_target="tpu_custom_call" | custom-call | flops 1 | bytes 1 | tf_op jit(solution)/shard_map/expert_grads/pallas_call | solution.py:963
  212.9 7.7 %all-to-all-done.3 = bf16[128,16,512]{2,1,0:T(8,128)(2,1)} async-done(((bf16[128,16,512]{2,1,0:T(8,128)(2,1)}), bf16[128,16,512]{2,1,0:T(8,128)(2,1)}, u32[]{:S(2)}, u32[]{:S(2)}) %all-to-all-start.3) | async-done | bytes 2097184 | tf_op jit(solution)/shard_map/all_to_all | solution.py:1019
  220.6 4.3 %combine_last.1.grad_ref = bf16[128,4096]{1,0:T(8,128)(2,1)S(1)} custom-call(f32[128,128]{1,0:T(8,128)S(1)} %copy-done.1, f32[128,128]{1,0:T(8,128)S(1)} %copy-done.2, bf16[2048,512]{1,0:T(8,128)(2,1)} %bitcast.37.blocks_ref, f32[1,4096]{1,0:T(1,128)S(1)} %bitcast.121, f32[128,1]{1,0:T(8,128)S(1)} %copy-done.6, f32[8,128,512]{2,1,0:T(8,128)} %combine_first.1.first_hbm, ...), custom_call_target="tpu_custom_call" | custom-call | flops 2147483648 | bytes 1 | tf_op jit(solution)/shard_map/combine_last/pallas_call | solution.py:726
  224.9 16.9 %finish.1 = (bf16[128,4096]{1,0:T(8,128)(2,1)S(1)}, bf16[128,512]{1,0:T(8,128)(2,1)S(1)}, f32[8,128]{1,0:T(8,128)S(1)}) custom-call(bf16[128,4096]{1,0:T(8,128)(2,1)S(1)} %bitcast.119, bf16[128,4096]{1,0:T(8,128)(2,1)S(1)} %combine_last.1.grad_ref, bf16[4,640,1024]{2,1,0:T(8,128)(2,1)} %get-tuple-element.94.prob_ref, bf16[640,512]{1,0:T(8,128)(2,1)S(1)} %copy-done.4, ...), custom_call_target="tpu_custom_call" | custom-call | flops 2684354560 | bytes 10485760 | tf_op jit(solution)/shard_map/finish/pallas_call | solution.py:570
  (106 shorter events, 18.9 us)
Async XLA Ops:
  14.5 14.2 %copy-start.12 = (bf16[1,32,4096]{2,1,0:T(8,128)(2,1)S(1)}, bf16[1,32,4096]{2,1,0:T(8,128)(2,1)}, u32[]{:S(2)}) copy-start(bf16[1,32,4096]{2,1,0:T(8,128)(2,1)} %param.28) | copy-start | bytes 786436
  14.5 14.2 %copy-start.13 = (bf16[1,768,32]{1,2,0:T(8,128)(2,1)S(1)}, bf16[1,768,32]{1,2,0:T(8,128)(2,1)}, u32[]{:S(2)}) copy-start(bf16[1,768,32]{1,2,0:T(8,128)(2,1)} %param.27) | copy-start | bytes 147460
  14.5 65.7 %all-to-all-start = ((bf16[128,16,1024]{2,1,0:T(8,128)(2,1)}), bf16[128,16,1024]{2,1,0:T(8,128)(2,1)}, u32[]{:S(2)}, u32[]{:S(2)}) async-start(bf16[128,16,1024]{2,1,0:T(8,128)(2,1)} %bitcast.129), calls=%async_computation | async-start | bytes 8388608 | tf_op jit(solution)/shard_map/all_to_all | solution.py:1019
  40.4 15.1 %copy-start.17 = (f32[1,4096]{1,0:T(1,128)S(1)}, f32[1,4096]{1,0:T(1,128)}, u32[]{:S(2)}) copy-start(f32[1,4096]{1,0:T(1,128)} %param.29) | copy-start | bytes 49156
  40.4 15.2 %copy-start.18 = (f32[1,2,768]{2,1,0:T(2,128)S(1)}, f32[1,2,768]{2,1,0:T(2,128)}, u32[]{:S(2)}) copy-start(f32[1,2,768]{2,1,0:T(2,128)} %param.25) | copy-start | bytes 18436
  55.5 38.1 %copy-start.14 = (f32[1,4096]{1,0:T(1,128)}, f32[1,4096]{1,0:T(1,128)S(1)}, u32[]{:S(2)}) copy-start(f32[1,4096]{1,0:T(1,128)S(1)} %div.22.scale_ref) | copy-start | bytes 49156
  80.3 34.9 %all-to-all-start.1 = ((bf16[128,16,512]{2,1,0:T(8,128)(2,1)}), bf16[128,16,512]{2,1,0:T(8,128)(2,1)}, u32[]{:S(2)}, u32[]{:S(2)}) async-start(bf16[128,16,512]{2,1,0:T(8,128)(2,1)} %bitcast.135), calls=%async_computation.1 | async-start | bytes 4194304 | tf_op jit(solution)/shard_map/all_to_all | solution.py:1019
  85.8 12.6 %slice-start = ((s8[6291456]{0:T(1024)(128)(4,1)}), s8[2097152]{0:T(1024)(128)(4,1)S(1)}, s32[]{:S(2)}) async-start(s8[6291456]{0:T(1024)(128)(4,1)} %bitcast.125), calls=%async_computation.5 | async-start | bytes 4194304
  115.1 35.1 %all-to-all-start.2 = ((bf16[128,16,512]{2,1,0:T(8,128)(2,1)}), bf16[128,16,512]{2,1,0:T(8,128)(2,1)}, u32[]{:S(2)}, u32[]{:S(2)}) async-start(bf16[128,16,512]{2,1,0:T(8,128)(2,1)} %bitcast.133), calls=%async_computation.2 | async-start | bytes 4194304 | tf_op jit(solution)/shard_map/all_to_all | solution.py:1019
  150.2 35.1 %all-to-all-start.4 = ((bf16[128,16,512]{2,1,0:T(8,128)(2,1)}), bf16[128,16,512]{2,1,0:T(8,128)(2,1)S(1)}, u32[]{:S(2)}, u32[]{:S(2)}) async-start(bf16[128,16,512]{2,1,0:T(8,128)(2,1)} %bitcast.134), calls=%async_computation.4 | async-start | bytes 4194304 | tf_op jit(solution)/shard_map/all_to_all | solution.py:1019
  185.3 10.7 %copy-start.10 = (bf16[256,768]{1,0:T(8,128)(2,1)S(1)}, bf16[256,768]{1,0:T(8,128)(2,1)}, u32[]{:S(2)}) copy-start(bf16[256,768]{1,0:T(8,128)(2,1)} %get-tuple-element.100) | copy-start | bytes 1179652
  185.3 10.7 %copy-start.11 = (bf16[256,768]{1,0:T(8,128)(2,1)S(1)}, bf16[256,768]{1,0:T(8,128)(2,1)}, u32[]{:S(2)}) copy-start(bf16[256,768]{1,0:T(8,128)(2,1)} %get-tuple-element.101) | copy-start | bytes 1179652
  185.3 35.3 %all-to-all-start.3 = ((bf16[128,16,512]{2,1,0:T(8,128)(2,1)}), bf16[128,16,512]{2,1,0:T(8,128)(2,1)}, u32[]{:S(2)}, u32[]{:S(2)}) async-start(bf16[128,16,512]{2,1,0:T(8,128)(2,1)} %bitcast.132), calls=%async_computation.3 | async-start | bytes 4194304 | tf_op jit(solution)/shard_map/all_to_all | solution.py:1019
  196.9 13.2 %copy-start.15 = (f32[256,1]{1,0:T(8,128)S(1)}, f32[256,1]{1,0:T(8,128)}, u32[]{:S(2)}) copy-start(f32[256,1]{1,0:T(8,128)} %get-tuple-element.95) | copy-start | bytes 3076
  196.9 13.2 %copy-start.16 = (f32[256,1]{1,0:T(8,128)S(1)}, f32[256,1]{1,0:T(8,128)}, u32[]{:S(2)}) copy-start(f32[256,1]{1,0:T(8,128)} %get-tuple-element.96) | copy-start | bytes 3076
  196.9 15.4 %copy-start.19 = (f32[2,768]{1,0:T(2,128)S(1)}, f32[2,768]{1,0:T(2,128)}, u32[]{:S(2)}) copy-start(f32[2,768]{1,0:T(2,128)} %get-tuple-element.112) | copy-start | bytes 18436
  196.9 15.4 %copy-start.20 = (f32[2,768]{1,0:T(2,128)S(1)}, f32[2,768]{1,0:T(2,128)}, u32[]{:S(2)}) copy-start(f32[2,768]{1,0:T(2,128)} %get-tuple-element.113) | copy-start | bytes 18436
  196.9 23.7 %copy-start = (bf16[1,128,4096]{2,1,0:T(8,128)(2,1)S(1)}, bf16[1,128,4096]{2,1,0:T(8,128)(2,1)}, u32[]{:S(2)}) copy-start(bf16[1,128,4096]{2,1,0:T(8,128)(2,1)} %param.21) | copy-start | bytes 3145732
  196.9 23.7 %copy-start.1 = (f32[128,128]{1,0:T(8,128)S(1)}, f32[128,128]{1,0:T(8,128)}, u32[]{:S(2)}) copy-start(f32[128,128]{1,0:T(8,128)} %get-tuple-element.69.slots_ref) | copy-start | bytes 196612
  196.9 23.7 %copy-start.2 = (f32[128,128]{1,0:T(8,128)S(1)}, f32[128,128]{1,0:T(8,128)}, u32[]{:S(2)}) copy-start(f32[128,128]{1,0:T(8,128)} %select_add_fusion.1.gates_ref) | copy-start | bytes 196612
  197.0 23.6 %copy-start.5 = (f32[4096]{0:T(1024)S(1)}, f32[4096]{0:T(1024)}, u32[]{:S(2)}) copy-start(f32[4096]{0:T(1024)} %param.18) | copy-start | bytes 49156
  197.0 23.6 %copy-start.6 = (f32[128,1]{1,0:T(8,128)S(1)}, f32[128,1]{1,0:T(8,128)}, u32[]{:S(2)}) copy-start(f32[128,1]{1,0:T(8,128)} %get-tuple-element.76.rinv_ref) | copy-start | bytes 1540
  210.3 14.6 %copy-start.3 = (bf16[1,128,4096]{2,1,0:T(8,128)(2,1)S(1)}, bf16[1,128,4096]{2,1,0:T(8,128)(2,1)}, u32[]{:S(2)}) copy-start(bf16[1,128,4096]{2,1,0:T(8,128)(2,1)} %param.15) | copy-start | bytes 3145732
  210.3 14.6 %copy-start.4 = (bf16[640,512]{1,0:T(8,128)(2,1)S(1)}, bf16[640,512]{1,0:T(8,128)(2,1)}, u32[]{:S(2)}) copy-start(bf16[640,512]{1,0:T(8,128)(2,1)} %get-tuple-element.63.keyval_ref.keys_ref.values_ref) | copy-start | bytes 1966084
  (10 other events, 54.5 us)
